TPU v7x, 256 devices: a whole 4x4x8 slice. The times are simulated.
256 devices in a mesh: section: 4 (over y), dp: 16 (over z_hi, x, core), tensor: 4 (over z_lo).
Axes of the slice: x: 4, y: 4, z: 8 (z_hi: 2, z_lo: 4; z = z_hi * 4 + z_lo), core: 2. Of those that a mesh axis runs over, the one named last changes fastest.
Arguments:
- query_grads: bfloat16 [4, 16, 128, 15872], P('section', 'dp', None, 'tensor'), may hold values from -450 to 450
- query_master: float32 [4, 128, 15872], P('section', 'dp', 'tensor'), may hold values from -5 to 5
- query_first: float32 [4, 128, 15872], P('section', 'dp', 'tensor'), may hold values from -3 to 3
- query_second: float32 [4, 128, 15872], P('section', 'dp', 'tensor'), may hold values from 0.01 to 1
- output_grads: bfloat16 [4, 16, 256, 14848], P('section', 'dp', 'tensor'), may hold values from -450 to 450
- output_master: float32 [4, 256, 14848], P('section', 'tensor', 'dp'), may hold values from -5 to 5
- output_first: float32 [4, 256, 14848], P('section', 'tensor', 'dp'), may hold values from -3 to 3
- output_second: float32 [4, 256, 14848], P('section', 'tensor', 'dp'), may hold values from 0.01 to 1
- table_grads: bfloat16 [4, 16, 256, 14848], P('section', 'dp', 'tensor'), may hold values from -450 to 450
- table_master: float32 [256, 14848], P('tensor', ('section', 'dp')), may hold values from -5 to 5
- table_first: float32 [256, 14848], P('tensor', ('section', 'dp')), may hold values from -3 to 3
- table_second: float32 [256, 14848], P('tensor', ('section', 'dp')), may hold values from 0.01 to 1
Outputs:
- query_weights: bfloat16 [4, 128, 15872], P('section', None, 'tensor')
- query_updated: float32 [4, 128, 15872], P('section', 'dp', 'tensor')
- query_moment: float32 [4, 128, 15872], P('section', 'dp', 'tensor')
- query_variance: float32 [4, 128, 15872], P('section', 'dp', 'tensor')
- output_weights: bfloat16 [4, 256, 14848], P('section', 'tensor')
- output_updated: float32 [4, 256, 14848], P('section', 'tensor', 'dp')
- output_moment: float32 [4, 256, 14848], P('section', 'tensor', 'dp')
- output_variance: float32 [4, 256, 14848], P('section', 'tensor', 'dp')
- table_weights: bfloat16 [256, 14848], P('tensor')
- table_updated: float32 [256, 14848], P('tensor', ('section', 'dp'))
- table_moment: float32 [256, 14848], P('tensor', ('section', 'dp'))
- table_variance: float32 [256, 14848], P('tensor', ('section', 'dp'))
All inputs are finite; a program needn't handle non-finite values.
Results may differ from a plain program's by a relative error of at most 0.001.
Values may be sent and summed in bfloat16 or wider, within the bound.
No kernel may reach another device: no remote copies, remote signals or barrier semaphores. Data moves between devices by JAX's collectives and lax.ppermute only.
A program may use at most 128 MiB of HBM per device.

v0:
```python
import math

import jax
import jax.numpy as jnp
from jax import lax
from jax.sharding import PartitionSpec as P

STEP = 10


beta_first = 0.9
beta_second = 0.95
learn_rate = 0.02
weight_decay = 0.1
tiny_value = 1e-08


def adamw(gradient, master, first, second, factor):
    clipped = gradient * factor
    first_new = beta_first * first + (1.0 - beta_first) * clipped
    second_new = beta_second * second + (1.0 - beta_second) * clipped * clipped
    first_hat = first_new / (1.0 - beta_first**STEP)
    second_hat = second_new / (1.0 - beta_second**STEP)
    master_new = master - learn_rate * (
        first_hat / (jnp.sqrt(second_hat) + tiny_value) + weight_decay * master
    )
    return (master_new, first_new, second_new, master_new.astype(jnp.bfloat16))


def per_device(
    query_grads,
    query_master,
    query_first,
    query_second,
    output_grads,
    output_master,
    output_first,
    output_second,
    table_grads,
    table_master,
    table_first,
    table_second,
):
    sections = lax.axis_size("section")
    members = lax.axis_size("dp")
    tensors = lax.axis_size("tensor")
    section_index = lax.axis_index("section")
    query_sum = lax.psum_scatter(
        query_grads[0, 0].astype(jnp.float32), "dp", scatter_dimension=0, tiled=True
    )
    output_sum = lax.psum_scatter(
        output_grads[0, 0].astype(jnp.float32), "dp", scatter_dimension=1, tiled=True
    )
    attn_square = jnp.sum(query_sum * query_sum) + jnp.sum(output_sum * output_sum)
    at_ends = jnp.logical_or(section_index == 0, section_index == sections - 1)
    table_local = jnp.where(at_ends, table_grads[0, 0].astype(jnp.float32), jnp.float32(0.0))
    table_rows, width = table_local.shape
    piece = width // (sections * members)
    ordered = (
        table_local.reshape(table_rows, sections, members, piece)
        .transpose(0, 2, 1, 3)
        .reshape(table_rows, members * sections * piece)
    )
    member_share = lax.psum_scatter(ordered, "dp", scatter_dimension=1, tiled=True)
    table_sum = lax.psum_scatter(member_share, "section", scatter_dimension=1, tiled=True)
    table_square = jnp.sum(table_sum * table_sum)
    attn_total, table_total = lax.psum((attn_square, table_square), ("section", "dp", "tensor"))
    query_rows, query_cols = (query_grads.shape[2], query_grads.shape[3])
    output_rows = output_grads.shape[2]
    params_count = (
        sections * (query_rows * query_cols * tensors + output_rows * tensors * width)
        + table_rows * tensors * width
    )
    grad_norm = jnp.sqrt(attn_total + table_total)
    factor = jnp.minimum(jnp.float32(1.0), 0.5 * math.sqrt(params_count) / (grad_norm + 1e-06))
    query_new, query_mom, query_var, query_half = adamw(
        query_sum, query_master[0], query_first[0], query_second[0], factor
    )
    query_full = lax.all_gather(query_half, "dp", axis=0, tiled=True)
    output_new, output_mom, output_var, output_half = adamw(
        output_sum, output_master[0], output_first[0], output_second[0], factor
    )
    output_full = lax.all_gather(output_half, "dp", axis=1, tiled=True)
    table_new, table_mom, table_var, table_half = adamw(
        table_sum, table_master, table_first, table_second, factor
    )
    table_full = lax.all_gather(table_half, ("section", "dp"), axis=1, tiled=True)
    return (
        query_full[None],
        query_new[None],
        query_mom[None],
        query_var[None],
        output_full[None],
        output_new[None],
        output_mom[None],
        output_var[None],
        table_full,
        table_new,
        table_mom,
        table_var,
    )


def solution(mesh):
    return jax.shard_map(
        per_device,
        mesh=mesh,
        in_specs=(
            P("section", "dp", None, "tensor"),
            P("section", "dp", "tensor"),
            P("section", "dp", "tensor"),
            P("section", "dp", "tensor"),
            P("section", "dp", "tensor", None),
            P("section", "tensor", "dp"),
            P("section", "tensor", "dp"),
            P("section", "tensor", "dp"),
            P("section", "dp", "tensor", None),
            P("tensor", ("section", "dp")),
            P("tensor", ("section", "dp")),
            P("tensor", ("section", "dp")),
        ),
        out_specs=(
            P("section", None, "tensor"),
            P("section", "dp", "tensor"),
            P("section", "dp", "tensor"),
            P("section", "dp", "tensor"),
            P("section", "tensor", None),
            P("section", "tensor", "dp"),
            P("section", "tensor", "dp"),
            P("section", "tensor", "dp"),
            P("tensor", None),
            P("tensor", ("section", "dp")),
            P("tensor", ("section", "dp")),
            P("tensor", ("section", "dp")),
        ),
        check_vma=False,
    )
```

profile of v0, /device:TPU:1, one launch (start us, length us, event | category | flops | bytes accessed | tf_op | source)
XLA Modules:
  0.0 774.6 jit_solution(16311261391677278455)
XLA Ops:
  7.2 0.0 reduce-scatter.10.cloned.1.call-start
  7.2 3.6 convert_select_fusion
  10.8 8.6 %select_n.14 = f32[64,4,16,232]{3,2,1,0:T(8,128)} reshape(f32[1,1,64,14848]{3,2,1,0:T(8,128)} %convert_select_fusion) | data formatting | bytes 7602176 | tf_op jit(solution)/shard_map/jit(_where)/select_n | solution.py:56
  19.4 8.2 %copy.39 = f32[64,4,16,232]{3,1,2,0:T(4,128)} copy(f32[64,4,16,232]{3,2,1,0:T(8,128)} %select_n.14) | data formatting | bytes 7602176 | tf_op jit(solution)/shard_map/jit(_where)/select_n | solution.py:56
  27.6 7.3 copy.37
  34.9 0.0 reduce-scatter.10.cloned.1.call-update
  34.9 0.0 copy-start
  34.9 0.0 all-reduce.5.cloned.1.call-start
  35.0 1.1 copy-done.1
  36.1 1.4 bitcast_convert_fusion.1
  37.6 0.0 all-reduce.5.cloned.1.call-update
  37.6 0.0 reduce-scatter.8.cloned.1.call-start
  37.6 2.1 bitcast_convert_fusion
  39.7 6.5 copy.31
  46.2 0.0 reduce-scatter.8.cloned.1.call-update
  46.2 0.0 copy-start.2
  46.3 0.0 copy-start.3
  46.3 0.0 copy-start.4
  46.3 0.0 all-reduce.7.cloned.1.call-start
  46.3 122.2 %reduce-scatter.10.cloned.1.call-done = f32[928,64]{1,0:T(8,128)} async-done(((f32[14848,64]{1,0:T(8,128)}), f32[928,64]{1,0:T(8,128)}) %reduce-scatter.10.cloned.1.call-update) | async-done | bytes 237584
  168.5 1.9 copy.34
  170.5 0.0 all-reduce.7.cloned.1.call-update
  170.5 0.0 all-gather.5.cloned.1.call-start
  170.5 0.6 dynamic-slice.2
  171.1 0.6 dynamic-slice
  173.0 179.2 %all-reduce.5.cloned.1.call-done = f32[128,3968]{1,0:T(8,128)} async-done(((f32[128,3968]{1,0:T(8,128)}), f32[128,3968]{1,0:T(8,128)}) %all-reduce.5.cloned.1.call-update) | async-done | bytes 2031632
  352.2 1.5 multiply_reduce_fusion.1
  353.8 134.3 %reduce-scatter.8.cloned.1.call-done = f32[928,64]{1,0:T(8,128)} async-done(((f32[14848,64]{1,0:T(8,128)}), f32[928,64]{1,0:T(8,128)}) %reduce-scatter.8.cloned.1.call-update) | async-done | bytes 237584
  488.1 1.2 copy.32
  489.3 0.7 multiply_reduce_fusion
  491.2 41.2 %all-reduce.7.cloned.1.call-done = f32[64,928]{1,0:T(8,128)} async-done(((f32[64,928]{1,0:T(8,128)}), f32[64,928]{1,0:T(8,128)}) %all-reduce.7.cloned.1.call-update) | async-done | bytes 237584
  532.4 1.6 multiply_reduce_fusion.2
  534.7 78.0 %psum.16 = f32[]{:T(128)} all-reduce(f32[]{:T(128)S(6)} %add.67), channel_id=1, replica_groups=mesh['section'=4,'dp'=16,'tensor'=4] {'section','dp','tensor'}, use_global_device_ids=true, to_apply=%region_4.5 | all-reduce | flops 1 | bytes 8 | tf_op jit(solution)/shard_map/psum | solution.py:67
  613.4 1.1 convert_bitcast_fusion
  614.5 0.0 all-gather.5.cloned.1.call-update
  614.6 0.0 all-gather.7.cloned.1.call-start
  614.6 0.0 copy-done.8
  614.6 1.7 convert_bitcast_fusion.1
  616.3 0.0 all-gather.7.cloned.1.call-update
  616.4 1.7 fusion.12
  618.1 33.9 %all_gather.9 = bf16[128,3968]{1,0:T(8,128)(2,1)S(1)} all-gather(bf16[8,3968]{1,0:T(8,128)(2,1)S(1)} %get-tuple-element.18), channel_id=1, replica_groups=mesh['section'=4,'dp'=16,'tensor'=4] {'dp'}, dimensions={0}, use_global_device_ids=true | all-gather | bytes 1079296 | tf_op jit(solution)/shard_map/all_gather | solution.py:79
  652.0 23.8 %all-gather.5.cloned.1.call-done = bf16[16,928,64]{1,2,0:T(8,128)(2,1)} async-done(((bf16[1,928,64]{1,2,0:T(8,128)(2,1)}), bf16[16,928,64]{1,2,0:T(8,128)(2,1)}) %all-gather.5.cloned.1.call-update) | async-done | bytes 1900560 | tf_op jit(solution)/shard_map/all_gather | solution.py:83
  675.8 2.7 copy.29
  678.6 3.6 reshape.49
  682.2 76.8 %all-gather.7.cloned.1.call-done = bf16[64,232,64]{1,2,0:T(8,128)(2,1)} async-done(((bf16[1,232,64]{1,2,0:T(8,128)(2,1)}), bf16[64,232,64]{1,2,0:T(8,128)(2,1)}) %all-gather.7.cloned.1.call-update) | async-done | bytes 1900560 | tf_op jit(solution)/shard_map/all_gather | solution.py:87
  759.0 2.8 copy.30
  761.8 5.0 reshape.51
  766.8 1.0 copy.43
  (20 shorter events, 0.0 us)
Async XLA Ops:
  7.2 161.3 %reduce-scatter.10.cloned.1.call-start = ((), (), s32[]{:S(2)}) async-start(), calls=%async_computation.5 | async-start | bytes 8077312
  34.9 1.2 copy-start.1
  34.9 2.7 copy-start
  34.9 317.3 %all-reduce.5.cloned.1.call-start = ((), (), s32[]{:S(2)}) async-start(), calls=%async_computation.6 | async-start | bytes 4063232
  37.6 450.5 %reduce-scatter.8.cloned.1.call-start = ((), (), s32[]{:S(2)}) async-start(), calls=%async_computation.4 | async-start | bytes 8077312
  46.2 124.3 %copy-start.12 = (u32[256]{0:T(256)S(1)}, u32[256]{0:T(256)}, u32[]{:S(2)}) copy-start(u32[256]{0:T(256)} %constant.74) | copy-start | bytes 3076
  46.2 124.9 %copy-start.11 = (u32[256]{0:T(256)S(1)}, u32[256]{0:T(256)}, u32[]{:S(2)}) copy-start(u32[256]{0:T(256)} %constant.70) | copy-start | bytes 3076
  46.2 567.1 %copy-start.2 = (f32[1,64,928]{2,1,0:T(8,128)S(1)}, f32[1,64,928]{2,1,0:T(8,128)}, u32[]{:S(2)}) copy-start(f32[1,64,928]{2,1,0:T(8,128)} %param.19) | copy-start | bytes 712708
  46.3 567.1 %copy-start.3 = (f32[1,64,928]{2,1,0:T(8,128)S(1)}, f32[1,64,928]{2,1,0:T(8,128)}, u32[]{:S(2)}) copy-start(f32[1,64,928]{2,1,0:T(8,128)} %param.18) | copy-start | bytes 712708
  46.3 567.1 %copy-start.4 = (f32[1,64,928]{2,1,0:T(8,128)S(1)}, f32[1,64,928]{2,1,0:T(8,128)}, u32[]{:S(2)}) copy-start(f32[1,64,928]{2,1,0:T(8,128)} %param.17) | copy-start | bytes 712708
  46.3 486.1 %all-reduce.7.cloned.1.call-start = ((), (), s32[]{:S(2)}) async-start(), calls=%async_computation.7 | async-start | bytes 524288
  168.5 446.1 %copy-start.8 = (f32[64,232]{1,0:T(8,128)S(1)}, f32[64,232]{1,0:T(8,128)}, u32[]{:S(2)}) copy-start(f32[64,232]{1,0:T(8,128)} %param.21) | copy-start | bytes 178180
  168.5 446.1 %copy-start.9 = (f32[64,232]{1,0:T(8,128)S(1)}, f32[64,232]{1,0:T(8,128)}, u32[]{:S(2)}) copy-start(f32[64,232]{1,0:T(8,128)} %param.22) | copy-start | bytes 178180
  168.5 446.1 %copy-start.10 = (f32[64,232]{1,0:T(8,128)S(1)}, f32[64,232]{1,0:T(8,128)}, u32[]{:S(2)}) copy-start(f32[64,232]{1,0:T(8,128)} %param.23) | copy-start | bytes 178180
  170.5 445.9 %copy-start.5 = (f32[1,8,3968]{2,1,0:T(8,128)S(1)}, f32[1,8,3968]{2,1,0:T(8,128)}, u32[]{:S(2)}) copy-start(f32[1,8,3968]{2,1,0:T(8,128)} %param.15) | copy-start | bytes 380932
  170.5 445.9 %copy-start.6 = (f32[1,8,3968]{2,1,0:T(8,128)S(1)}, f32[1,8,3968]{2,1,0:T(8,128)}, u32[]{:S(2)}) copy-start(f32[1,8,3968]{2,1,0:T(8,128)} %param.14) | copy-start | bytes 380932
  170.5 445.9 %copy-start.7 = (f32[1,8,3968]{2,1,0:T(8,128)S(1)}, f32[1,8,3968]{2,1,0:T(8,128)}, u32[]{:S(2)}) copy-start(f32[1,8,3968]{2,1,0:T(8,128)} %param.13) | copy-start | bytes 380932
  170.5 505.4 %all-gather.5.cloned.1.call-start = ((), (), s32[]{:S(2)}) async-start(), calls=%async_computation.2 | async-start | bytes 2228224 | tf_op jit(solution)/shard_map/all_gather | solution.py:83
  614.6 144.5 %all-gather.7.cloned.1.call-start = ((), (), s32[]{:S(2)}) async-start(), calls=%async_computation.3 | async-start | bytes 2129920 | tf_op jit(solution)/shard_map/all_gather | solution.py:87
Sparse Core Ops, SparseCore 0:
  35.1 133.3 reduce-scatter.9
  171.4 180.8 all-reduce.4
  357.4 130.5 reduce-scatter.7
  490.8 41.5 all-reduce.6
  614.7 61.1 all-gather.4
  680.6 78.4 all-gather.6
where the time goes:
time: 775 us
  waiting for transfers between devices  578 us (75%)
  blocking collectives  112 us (14%)
  local copies, waits for them, and re-layouts  51.1 us (7%)
  between operations  18.3 us (2%)
  other arithmetic  15.4 us (2%)
    unnamed x10, waiting for transfers between devices  477 us
    psum x1, blocking collectives, per_device(): lax.psum((attn_square, table_square), ('section', 'dp', 'tensor'))  78 us
    all_gather x1, waiting for transfers between devices, per_device(): lax.all_gather(table_half, ('section', 'dp'), axis=1, tiled=True)  76.8 us
    all_gather x1, blocking collectives, per_device(): query_full = lax.all_gather(query_half, 'dp', axis=0, tiled=True)  33.9 us
    unnamed x35, local copies, waits for them, and re-layouts  28.8 us
    all_gather x1, waiting for transfers between devices, per_device(): output_full = lax.all_gather(output_half, 'dp', axis=1, tiled=True)  23.8 us
    select_n x2, local copies, waits for them, and re-layouts, per_device(): jnp.where(at_ends, table_grads[0, 0].astype(jnp.float32), jnp.float32(0.0))  16.8 us
  transfers between devices with their start and end apart: 6, of which 6 were waited for; matrix products, arithmetic and copies ran while one was open for 3% of the time, Pallas kernels for 0%

commit v1 on v0

v1 whole, which is shorter than its diff:
```python
import math

import jax
import jax.numpy as jnp
from jax import lax
from jax.experimental import pallas as pl
from jax.experimental.pallas import tpu as pltpu
from jax.sharding import PartitionSpec as P

STEP = 10

beta_first = 0.9
beta_second = 0.95
learn_rate = 0.02
weight_decay = 0.1
tiny_value = 1e-08

F32, BF16, F16 = jnp.float32, jnp.bfloat16, jnp.float16

QT = 31
QROWS, OROWS, TROWS = 248, 464, 128
SUMS = QROWS + OROWS
WQ = 256
WEIGHTS = WQ + OROWS
PARAMS_KERNEL = pltpu.CompilerParams(vmem_limit_bytes=40 * 1024 * 1024)


def pair_perm(move):
    return [(d, move(d)) for d in range(16)]


CORE = pair_perm(lambda d: d ^ 1)
ZHALF = pair_perm(lambda d: d ^ 8)


def x_perm(k):
    return pair_perm(lambda d: (d & 9) | ((((d >> 1) + k) & 3) << 1))


def ring_perm(k):
    return [(i, (i + k) % 4) for i in range(4)]


def lanes(rows):
    return lax.broadcasted_iota(jnp.int32, (rows, 128), 1)


def call(kernel, outs, *args):
    return pl.pallas_call(kernel, out_shape=outs, compiler_params=PARAMS_KERNEL)(*args)


def out(shape, dtype):
    return jax.ShapeDtypeStruct(shape, dtype)


def position():
    d = lax.axis_index("dp")
    return d // 8, (d // 2) % 4, d % 2


def split_kernel(q_ref, o_ref, qs_ref, os_ref):
    _, _, core = position()
    other = 1 - core

    def rows(j, carry):
        r = pl.multiple_of(j * 32, 32)
        v = q_ref[pl.ds(r, 32), :].astype(F32)
        first = jnp.where(other == 0, v[0:8], v[8:16])
        second = jnp.where(other == 0, v[16:24], v[24:32])
        qs_ref[pl.ds(pl.multiple_of(j * 16, 16), 16), :] = jnp.concatenate(
            [first, second], axis=0
        ).astype(BF16)
        return carry

    lax.fori_loop(0, 4, rows, 0)

    def cols(j, carry):
        start = pl.multiple_of(((29 * (2 * j + other)) // 4) * 128, 128)
        os_ref[j] = o_ref[:, pl.ds(start, 1024)]
        return carry

    lax.fori_loop(0, 8, cols, 0)


def pack_kernel(q_ref, o_ref, qr_ref, or_ref, out_ref):
    _, x, core = position()
    lane = lanes(64)
    lane16 = lanes(16)

    def block(j, carry):
        half, xb = j // 4, j % 4
        slot = (xb - x + 4) % 4
        v = q_ref[pl.ds(pl.multiple_of(j * 16, 16), 16), :].astype(F32)
        w = qr_ref[pl.ds(pl.multiple_of((j // 2) * 16, 16), 16), :].astype(F32)
        total = jnp.where(core == 0, v[0:8], v[8:16]) + jnp.where(j % 2 == 0, w[0:8], w[8:16])
        for t in range(QT):
            out_ref[slot, half, 8 * t : 8 * t + 8, :] = total[:, 128 * t : 128 * t + 128]
        d = 2 * j + core
        start = pl.multiple_of(((29 * d) // 4) * 128, 128)
        shift = 32 * (d % 4)
        turn = (128 - shift) % 128
        tiles = []
        for t in range(8):
            a = o_ref[:, pl.ds(start + 128 * t, 128)].astype(F32)
            b = or_ref[j, :, 128 * t : 128 * t + 128].astype(F32)
            tiles.append(pltpu.roll(a + b, turn, 1))
        for t in range(7):
            out_ref[slot, half, QROWS + 64 * t : QROWS + 64 * t + 64, :] = jnp.where(
                lane < 128 - shift, tiles[t], tiles[t + 1]
            )
        last = tiles[7]
        rest = last[0:16]
        for g in range(1, 4):
            rest = jnp.where(lane16 < 32 * g, rest, pltpu.roll(last[16 * g : 16 * g + 16], 32 * g, 1))
        out_ref[slot, half, QROWS + 448 : QROWS + 464, :] = rest
        return carry

    lax.fori_loop(0, 8, block, 0)


def table_pack_kernel(t_ref, out_ref):
    lane = lanes(64)
    for d in range(16):
        half, xb, core = d // 8, (d // 2) % 4, d % 2
        for i in range(2):
            first = 232 * d + 128 * i
            tile, shift = first // 128, first % 128
            v = t_ref[:, 128 * tile : 128 * tile + 128]
            if shift:
                v = pltpu.roll(v, 128 - shift, 1)
                if tile + 1 < 29:
                    w = pltpu.roll(t_ref[:, 128 * tile + 128 : 128 * tile + 256], 128 - shift, 1)
                    v = jnp.where(lane < 128 - shift, v, w)
            if i == 1:
                v = jnp.where(lane < 104, v, 0.0)
            out_ref[core, xb, half, 64 * i : 64 * i + 64, :] = v


def adamw(gradient, master, first, second, factor):
    clipped = gradient * factor
    first_new = beta_first * first + (1.0 - beta_first) * clipped
    second_new = beta_second * second + (1.0 - beta_second) * clipped * clipped
    first_hat = first_new / (1.0 - beta_first**STEP)
    second_hat = second_new / (1.0 - beta_second**STEP)
    master_new = master - learn_rate * (
        first_hat / (jnp.sqrt(second_hat) + tiny_value) + weight_decay * master
    )
    return master_new, first_new, second_new


def update_kernel(limit):
    def kernel(
        n_ref, g_ref, gt_ref,
        qw_ref, qm_ref, qv_ref, ow_ref, om_ref, ov_ref, tw_ref, tm_ref, tv_ref,
        pack_ref, tpack_ref,
        qw2_ref, qm2_ref, qv2_ref, ow2_ref, om2_ref, ov2_ref, tw2_ref, tm2_ref, tv2_ref,
    ):
        grad_norm = jnp.sqrt(jnp.sum(n_ref[...], keepdims=True))
        factor = jnp.minimum(1.0, limit / (grad_norm + 1e-06))

        def step(g, rows, cols, refs, outs):
            new = adamw(g, *(r[rows, cols] for r in refs), factor)
            for ref, value in zip(outs, new):
                ref[rows, cols] = value
            return new[0]

        refs, outs = (qw_ref, qm_ref, qv_ref), (qw2_ref, qm2_ref, qv2_ref)
        every = slice(None)
        new = [
            step(g_ref[8 * t : 8 * t + 8, :], every, slice(128 * t, 128 * t + 128), refs, outs)
            for t in range(QT)
        ]
        new.append(jnp.zeros_like(new[0]))
        for t in range(16):
            pack_ref[16 * t : 16 * t + 16, :] = jnp.concatenate(
                [new[t], new[t + 16]], axis=0
            ).astype(BF16)

        refs, outs = (ow_ref, om_ref, ov_ref), (ow2_ref, om2_ref, ov2_ref)
        for t in range(7):
            g = g_ref[QROWS + 64 * t : QROWS + 64 * t + 64, :]
            w = step(g, every, slice(128 * t, 128 * t + 128), refs, outs)
            pack_ref[WQ + 64 * t : WQ + 64 * t + 64, :] = w.astype(BF16)
        rest = g_ref[QROWS + 448 : QROWS + 464, :]
        lane = lanes(16)
        packed = jnp.zeros((16, 128), F32)
        for g in range(4):
            piece = rest if g == 0 else pltpu.roll(rest, 128 - 32 * g, 1)
            w = step(piece[:, 0:32], slice(16 * g, 16 * g + 16), slice(896, 928), refs, outs)
            w = jnp.concatenate([w, jnp.zeros((16, 96), F32)], axis=1)
            w = w if g == 0 else pltpu.roll(w, 32 * g, 1)
            packed = jnp.where((lane >= 32 * g) & (lane < 32 * g + 32), w, packed)
        pack_ref[WQ + 448 : WQ + 464, :] = packed.astype(BF16)

        refs, outs = (tw_ref, tm_ref, tv_ref), (tw2_ref, tm2_ref, tv2_ref)
        w = step(gt_ref[0:64, :], every, slice(0, 128), refs, outs)
        tpack_ref[0:64, :] = w.astype(BF16)
        w = step(gt_ref[64:128, 0:104], every, slice(128, 232), refs, outs)
        tpack_ref[64:128, :] = jnp.concatenate([w, jnp.zeros((64, 24), F32)], axis=1).astype(BF16)

    return kernel


def take(own_ref, got_ref, index, rows, mine):
    a = own_ref[(*index, rows, slice(None))].astype(F32)
    b = got_ref[(*index, rows, slice(None))].astype(F32)
    return jnp.where(mine, a, b)


def cover(t, width, count):
    found = []
    for b in range(count):
        begin = 128 * t - width * b
        for i in range(-(-width // 128)):
            lo = max(0, 128 * i - begin)
            hi = min(128, 128 * i - begin + 128, width - begin)
            if lo < hi:
                found.append((b, i, (-begin) % 128, lo, hi))
    return found


def join_kernel(own_ref, got_ref, q_ref, o_ref):
    zh, x, core = position()

    def rows(j, carry):
        index = ((x - j % 4 + 4) % 4, jnp.where(zh == j // 4, 0, 1))
        for p in range(16):
            a = own_ref[(*index, slice(16 * p, 16 * p + 16), slice(None))].astype(F32)
            b = got_ref[(*index, slice(16 * p, 16 * p + 16), slice(None))].astype(F32)
            c0, c1 = jnp.where(core == 0, a, b), jnp.where(core == 0, b, a)
            for t, part in ((p, slice(0, 8)), (p + 16, slice(8, 16))):
                if t < QT:
                    q_ref[pl.ds(pl.multiple_of(j * 16, 16), 16), 128 * t : 128 * t + 128] = (
                        jnp.concatenate([c0[part], c1[part]], axis=0).astype(BF16)
                    )
        return carry

    lax.fori_loop(0, 8, rows, 0)
    lane = lanes(64)

    def cols(g, carry):
        index = [
            ((x - (2 * (g % 2) + b // 2) + 4) % 4, jnp.where(zh == g // 2, 0, 1)) for b in range(4)
        ]

        def tile(b, i, turn):
            mine = core == b % 2
            if i < 7:
                v = take(own_ref, got_ref, index[b], slice(WQ + 64 * i, WQ + 64 * i + 64), mine)
                return pltpu.roll(v, turn, 1) if turn else v
            v = take(own_ref, got_ref, index[b], slice(WQ + 448, WQ + 464), mine)
            parts = []
            for k in range(4):
                move = (turn - 32 * k) % 128
                parts.append(pltpu.roll(v, move, 1) if move else v)
            return jnp.concatenate(parts, axis=0)

        base = pl.multiple_of(g * 3712, 128)
        for t in range(29):
            value = None
            for b, i, turn, lo, hi in cover(t, 928, 4):
                v = tile(b, i, turn)
                value = v if value is None else jnp.where(lane >= lo, v, value)
            o_ref[:, pl.ds(base + 128 * t, 128)] = value.astype(BF16)
        return carry

    lax.fori_loop(0, 4, cols, 0)


def table_join_kernel(own_ref, got_ref, t_ref):
    zh, x, core = position()
    section = lax.axis_index("section")
    lane = lanes(64)

    def quarter(s, carry):
        m = (section - s + 4) % 4
        base = pl.multiple_of(s * 3712, 128)
        for t in range(29):
            value = None
            for d, i, turn, lo, hi in cover(t, 232, 16):
                index = (m, (x - (d // 2) % 4 + 4) % 4, jnp.where(zh == d // 8, 0, 1))
                v = take(own_ref, got_ref, index, slice(64 * i, 64 * i + 64), core == d % 2)
                v = pltpu.roll(v, turn, 1) if turn else v
                value = v if value is None else jnp.where(lane >= lo, v, value)
            t_ref[:, pl.ds(base + 128 * t, 128)] = value.astype(BF16)
        return carry

    lax.fori_loop(0, 4, quarter, 0)


def per_device(
    query_grads,
    query_master,
    query_first,
    query_second,
    output_grads,
    output_master,
    output_first,
    output_second,
    table_grads,
    table_master,
    table_first,
    table_second,
):
    section = lax.axis_index("section")
    member = lax.axis_index("dp")
    zh, x, core = member // 8, (member // 2) % 4, member % 2
    query, output, table = query_grads[0, 0], output_grads[0, 0], table_grads[0, 0]

    def dp_send(value, perm):
        return lax.ppermute(value, "dp", perm)

    def quarter(i):
        return lax.dynamic_slice(table, (0, i * 3712), (64, 3712))

    first_section = section == 0
    at_ends = jnp.logical_or(first_section, section == 3)
    t_far = lax.ppermute(quarter(jnp.where(first_section, 2, 1)), "section", [(0, 2), (3, 1)])
    t_near = lax.ppermute(quarter(jnp.where(first_section, 1, 2)), "section", [(0, 1), (3, 2)])
    t_end = lax.ppermute(quarter(jnp.where(first_section, 3, 0)), "section", [(0, 3), (3, 0)])

    q_send, o_send = call(
        split_kernel, (out((64, 3968), BF16), out((8, 64, 1024), BF16)), query, output
    )
    q_got, o_got = dp_send(q_send, CORE), dp_send(o_send, CORE)
    sums = call(pack_kernel, out((4, 2, SUMS, 128), F32), query, output, q_got, o_got)

    got = [dp_send(sums[k].astype(F16), x_perm(k)) for k in (1, 2, 3)]
    total = sums[0] + got[0].astype(F32) + got[1].astype(F32) + got[2].astype(F32)
    z_got = dp_send(lax.dynamic_index_in_dim(total, 1 - zh, 0, False).astype(F16), ZHALF)
    gradient = lax.dynamic_index_in_dim(total, zh, 0, False) + z_got.astype(F32)

    t_sum = jnp.where(at_ends, quarter(section), t_near).astype(F32) + jnp.where(
        at_ends, t_end, t_far
    ).astype(F32)
    t_blocks = call(table_pack_kernel, out((2, 4, 2, TROWS, 128), F32), t_sum)
    t_got = dp_send(lax.dynamic_index_in_dim(t_blocks, 1 - core, 0, False).astype(F16), CORE)
    t_chip = lax.dynamic_index_in_dim(t_blocks, core, 0, False) + t_got.astype(F32)

    def t_slot(k):
        return lax.dynamic_index_in_dim(t_chip, (x + k) % 4, 0, False)

    t_gots = [dp_send(t_slot(k).astype(F16), x_perm(k)) for k in (1, 2, 3)]
    t_total = (
        t_slot(0) + t_gots[0].astype(F32) + t_gots[1].astype(F32) + t_gots[2].astype(F32)
    )
    tz_got = dp_send(lax.dynamic_index_in_dim(t_total, 1 - zh, 0, False).astype(F16), ZHALF)
    t_gradient = lax.dynamic_index_in_dim(t_total, zh, 0, False) + tz_got.astype(F32)

    squares = jnp.sum((gradient * gradient).reshape(-1, 8, 128), axis=0) + jnp.sum(
        (t_gradient * t_gradient).reshape(-1, 8, 128), axis=0
    )
    squares = squares + dp_send(squares, CORE)
    squares = squares + sum(dp_send(squares, x_perm(k)) for k in (1, 2, 3))
    squares = squares + sum(lax.ppermute(squares, "section", ring_perm(k)) for k in (1, 2, 3))
    squares = squares + dp_send(squares, ZHALF)
    squares = squares + sum(lax.ppermute(squares, "tensor", ring_perm(k)) for k in (1, 2, 3))

    params_count = 4 * (128 * 15872 + 256 * 14848) + 256 * 14848
    limit = 0.5 * math.sqrt(params_count)
    small = [out((8, 3968), F32)] * 3 + [out((64, 928), F32)] * 3 + [out((64, 232), F32)] * 3
    packed, t_packed, *new = call(
        update_kernel(limit),
        (out((WEIGHTS, 128), BF16), out((TROWS, 128), BF16), *small),
        squares, gradient, t_gradient,
        query_master[0], query_first[0], query_second[0],
        output_master[0], output_first[0], output_second[0],
        table_master, table_first, table_second,
    )

    def spread(value):
        both = jnp.stack([value, dp_send(value, ZHALF)])
        return jnp.stack([both] + [dp_send(both, x_perm(k)) for k in (1, 2, 3)])

    t_all = spread(t_packed)
    t_all = jnp.stack([t_all] + [lax.ppermute(t_all, "section", ring_perm(k)) for k in (1, 2, 3)])
    w_all = spread(packed)
    w_other = dp_send(w_all, CORE)
    t_other = dp_send(t_all, CORE)
    query_full, output_full = call(
        join_kernel, (out((128, 3968), BF16), out((64, 14848), BF16)), w_all, w_other
    )
    table_full = call(table_join_kernel, out((64, 14848), BF16), t_all, t_other)
    return (
        query_full[None],
        *(a[None] for a in new[0:3]),
        output_full[None],
        *(a[None] for a in new[3:6]),
        table_full,
        *new[6:9],
    )


def solution(mesh):
    return jax.shard_map(
        per_device,
        mesh=mesh,
        in_specs=(
            P("section", "dp", None, "tensor"),
            P("section", "dp", "tensor"),
            P("section", "dp", "tensor"),
            P("section", "dp", "tensor"),
            P("section", "dp", "tensor", None),
            P("section", "tensor", "dp"),
            P("section", "tensor", "dp"),
            P("section", "tensor", "dp"),
            P("section", "dp", "tensor", None),
            P("tensor", ("section", "dp")),
            P("tensor", ("section", "dp")),
            P("tensor", ("section", "dp")),
        ),
        out_specs=(
            P("section", None, "tensor"),
            P("section", "dp", "tensor"),
            P("section", "dp", "tensor"),
            P("section", "dp", "tensor"),
            P("section", "tensor", None),
            P("section", "tensor", "dp"),
            P("section", "tensor", "dp"),
            P("section", "tensor", "dp"),
            P("tensor", None),
            P("tensor", ("section", "dp")),
            P("tensor", ("section", "dp")),
            P("tensor", ("section", "dp")),
        ),
        check_vma=False,
    )
```

time: 775 us -> 179 us (0.23)
  waiting for transfers between devices: 578 us -> 70.1 us
  blocking collectives: 112 us -> 0 us
  starting transfers between devices: 0.25 us -> 80.1 us
  local copies, waits for them, and re-layouts: 51.1 us -> 10.7 us
  between operations: 18.3 us -> 0.98 us
  Pallas kernels: 0 us -> 10.3 us
  other arithmetic: 15.4 us -> 6.26 us
    unnamed x10 -> x0, waiting for transfers between devices: 477 us -> none
    all_gather x2 -> x0, waiting for transfers between devices: 101 us -> none  [the longest x1 76.8 us: per_device(): lax.all_gather(table_half, ('section', 'dp'), axis=1, tiled=True)]
    ppermute x0 -> x38, starting transfers between devices: none -> 80.1 us  [the longest x26 56.6 us: dp_send(): return lax.ppermute(value, 'dp', perm)]
    psum x1 -> x0, blocking collectives: 78 us -> none  [per_device(): lax.psum((attn_square, table_square), ('section', 'dp', 'tensor'))]
    ppermute x0 -> x38, waiting for transfers between devices: none -> 70.1 us  [the longest x26 46.6 us: dp_send(): return lax.ppermute(value, 'dp', perm)]
    all_gather x1 -> x0, blocking collectives: 33.9 us -> none  [per_device(): query_full = lax.all_gather(query_half, 'dp', axis=0, tiled=True)]
    unnamed x35 -> x34, local copies, waits for them, and re-layouts: 28.8 us -> 7.09 us
    select_n x2 -> x0, local copies, waits for them, and re-layouts: 16.8 us -> none  [per_device(): jnp.where(at_ends, table_grads[0, 0].astype(jnp.float32), jnp.float32(0.0))]
  transfers between devices with their start and end apart: 6 -> 38, of which waited for: 6 -> 22; matrix products, arithmetic and copies ran while one was open for 3% -> 2% of each run, Pallas kernels for 0% -> 2%
where the time goes in v1:
time: 179 us; the launch traced here: 178 us
  starting transfers between devices  80.1 us (45%)
  waiting for transfers between devices  70.1 us (39%)
  local copies, waits for them, and re-layouts  10.7 us (6%)
  Pallas kernels  10.3 us (6%)
  other arithmetic  6.26 us (3%)
    ppermute x26, starting transfers between devices, dp_send(): return lax.ppermute(value, 'dp', perm)  56.6 us
    ppermute x26, waiting for transfers between devices, dp_send(): return lax.ppermute(value, 'dp', perm)  46.6 us
    pallas_call x6, Pallas kernels, call(): pl.pallas_call(kernel, out_shape=outs, compiler_params=PARAMS_KERNEL)(*args)  10.3 us
    ppermute x3, waiting for transfers between devices, per_device(): lax.ppermute(t_all, 'section', ring_perm(k))  7.92 us
    unnamed x34, local copies, waits for them, and re-layouts  7.09 us
    ppermute x3, starting transfers between devices, per_device(): lax.ppermute(squares, 'section', ring_perm(k))  5.42 us
    ppermute x1, waiting for transfers between devices, per_device(): lax.ppermute(quarter(jnp.where(first_section, 3, 0)), 'section', [(0, 3),...  5.19 us
    ppermute x1, starting transfers between devices, per_device(): lax.ppermute(quarter(jnp.where(first_section, 1, 2)), 'section', [(0, 1),...  4.81 us
  transfers between devices with their start and end apart: 38, of which 22 were waited for; matrix products, arithmetic and copies ran while one was open for 2% of the time, Pallas kernels for 2%

profile of v1, /device:TPU:1, one launch (start us, length us, event | category | flops | bytes accessed | tf_op | source)
XLA Modules:
  0.0 178.3 jit_solution(6166293766142559200)
XLA Ops:
  0.7 2.5 %dynamic-slice_bitcast_fusion = (bf16[64,3712]{1,0:T(8,128)(2,1)S(1)}, bf16[64,3712]{1,0:T(8,128)(2,1)}, bf16[64,3712]{1,0:T(8,128)(2,1)}) fusion(bf16[1,1,64,14848]{3,2,1,0:T(8,128)(2,1)} %param.20, s32[]{:T(128)S(6)} %select_n.109, s32[]{:T(128)S(6)} %select_n.104, s32[]{:T(128)S(6)} %select_n.107), kind=kLoop, calls=%fused_computation.10 | loop fusion | bytes 2850828 | tf_op jit(solution)/shard_map/dynamic_slice | solution.py:314
  3.1 4.8 %collective-permute-start.6 = (bf16[64,3712]{1,0:T(8,128)(2,1)}, bf16[64,3712]{1,0:T(8,128)(2,1)}, u32[]{:S(2)}, u32[]{:S(2)}) collective-permute-start(bf16[64,3712]{1,0:T(8,128)(2,1)} %get-tuple-element.47), channel_id=1, source_target_pairs={{0,64},{192,128},{1,65},{193,129},{2,66},{194,130},{3,67},{195,131... | collective-permute-start | bytes 1425416 | tf_op jit(solution)/shard_map/ppermute | solution.py:319
  8.0 3.8 %collective-permute-start.7 = (bf16[64,3712]{1,0:T(8,128)(2,1)}, bf16[64,3712]{1,0:T(8,128)(2,1)}, u32[]{:S(2)}, u32[]{:S(2)}) collective-permute-start(bf16[64,3712]{1,0:T(8,128)(2,1)} %get-tuple-element.48), channel_id=1, source_target_pairs={{0,192},{192,0},{1,193},{193,1},{2,194},{194,2},{3,195},{195,3},{4... | collective-permute-start | bytes 1425416 | tf_op jit(solution)/shard_map/ppermute | solution.py:320
  11.8 2.1 %collective-permute-start.8 = (bf16[64,3712]{1,0:T(8,128)(2,1)S(1)}, bf16[64,3712]{1,0:T(8,128)(2,1)}, u32[]{:S(2)}, u32[]{:S(2)}) collective-permute-start(bf16[64,3712]{1,0:T(8,128)(2,1)S(1)} %get-tuple-element.46), channel_id=1, source_target_pairs={{0,128},{192,64},{1,129},{193,65},{2,130},{194,66},{3,131},{195,67... | collective-permute-start | bytes 1425416 | tf_op jit(solution)/shard_map/ppermute | solution.py:318
  15.1 1.3 shard_map.211
  17.6 5.2 %collective-permute-done.7 = bf16[64,3712]{1,0:T(8,128)(2,1)} collective-permute-done((bf16[64,3712]{1,0:T(8,128)(2,1)}, bf16[64,3712]{1,0:T(8,128)(2,1)}, u32[]{:S(2)}, u32[]{:S(2)}) %collective-permute-start.7) | collective-permute-done | bytes 475168 | tf_op jit(solution)/shard_map/ppermute | solution.py:320
  22.8 4.3 %collective-permute-done.8 = bf16[64,3712]{1,0:T(8,128)(2,1)} collective-permute-done((bf16[64,3712]{1,0:T(8,128)(2,1)S(1)}, bf16[64,3712]{1,0:T(8,128)(2,1)}, u32[]{:S(2)}, u32[]{:S(2)}) %collective-permute-start.8) | collective-permute-done | bytes 475168 | tf_op jit(solution)/shard_map/ppermute | solution.py:318
  27.1 1.4 convert_add_fusion.t_ref
  29.8 1.5 collective-permute-start.9
  31.3 1.4 collective-permute-done.9
  33.8 1.5 copy-done.1
  37.8 1.4 shard_map.212
  40.5 2.5 %collective-permute-start.4 = (f16[2,712,128]{2,1,0:T(8,128)(2,1)}, f16[2,712,128]{2,1,0:T(8,128)(2,1)S(1)}, u32[]{:S(2)}, u32[]{:S(2)}) collective-permute-start(f16[2,712,128]{2,1,0:T(8,128)(2,1)} %get-tuple-element.50), channel_id=1, source_target_pairs={{0,24},{4,28},{8,0},{12,4},{16,8},{20,12},{24,16},{28,20},{32,56},... | collective-permute-start | bytes 1093640 | tf_op jit(solution)/shard_map/ppermute | solution.py:311
  44.1 2.1 %collective-permute-start.12 = (f16[2,128,128]{2,1,0:T(8,128)(2,1)S(1)}, f16[2,128,128]{2,1,0:T(8,128)(2,1)S(1)}, u32[]{:S(2)}, u32[]{:S(2)}) collective-permute-start(f16[2,128,128]{2,1,0:T(8,128)(2,1)S(1)} %get-tuple-element.53), channel_id=1, source_target_pairs={{0,24},{4,28},{8,0},{12,4},{16,8},{20,12},{24,16},{28,20},{32,56},... | collective-permute-start | bytes 196616 | tf_op jit(solution)/shard_map/ppermute | solution.py:311
  47.5 13.7 %collective-permute-done.12 = f16[2,128,128]{2,1,0:T(8,128)(2,1)S(1)} collective-permute-done((f16[2,128,128]{2,1,0:T(8,128)(2,1)S(1)}, f16[2,128,128]{2,1,0:T(8,128)(2,1)S(1)}, u32[]{:S(2)}, u32[]{:S(2)}) %collective-permute-start.12) | collective-permute-done | bytes 65568 | tf_op jit(solution)/shard_map/ppermute | solution.py:311
  61.2 1.9 %collective-permute-done.11 = f16[2,128,128]{2,1,0:T(8,128)(2,1)S(1)} collective-permute-done((f16[2,128,128]{2,1,0:T(8,128)(2,1)S(1)}, f16[2,128,128]{2,1,0:T(8,128)(2,1)S(1)}, u32[]{:S(2)}, u32[]{:S(2)}) %collective-permute-start.11) | collective-permute-done | bytes 65568 | tf_op jit(solution)/shard_map/ppermute | solution.py:311
  63.0 3.4 %collective-permute-done.10 = f16[2,128,128]{2,1,0:T(8,128)(2,1)} collective-permute-done((f16[2,128,128]{2,1,0:T(8,128)(2,1)S(1)}, f16[2,128,128]{2,1,0:T(8,128)(2,1)}, u32[]{:S(2)}, u32[]{:S(2)}) %collective-permute-start.10) | collective-permute-done | bytes 65568 | tf_op jit(solution)/shard_map/ppermute | solution.py:311
  69.7 7.0 %collective-permute-start.5 = (f16[712,128]{1,0:T(8,128)(2,1)S(1)}, f16[712,128]{1,0:T(8,128)(2,1)S(1)}, u32[]{:S(2)}, u32[]{:S(2)}) collective-permute-start(f16[712,128]{1,0:T(8,128)(2,1)S(1)} %fusion.4), channel_id=1, source_target_pairs={{0,32},{4,36},{8,40},{12,44},{16,48},{20,52},{24,56},{28,60},{32,0... | collective-permute-start | bytes 546824 | tf_op jit(solution)/shard_map/ppermute | solution.py:311
  76.8 6.7 %collective-permute-done.13 = f16[128,128]{1,0:T(8,128)(2,1)S(1)} collective-permute-done((f16[128,128]{1,0:T(8,128)(2,1)S(1)}, f16[128,128]{1,0:T(8,128)(2,1)S(1)}, u32[]{:S(2)}, u32[]{:S(2)}) %collective-permute-start.13) | collective-permute-done | bytes 32800 | tf_op jit(solution)/shard_map/ppermute | solution.py:311
  84.7 3.5 %collective-permute-start.14 = (f32[8,128]{1,0:T(8,128)S(1)}, f32[8,128]{1,0:T(8,128)S(1)}, u32[]{:S(2)}, u32[]{:S(2)}) collective-permute-start(f32[8,128]{1,0:T(8,128)S(1)} %add.171), channel_id=1, source_target_pairs={{0,4},{4,0},{8,12},{12,8},{16,20},{20,16},{24,28},{28,24},{32,36},... | collective-permute-start | bytes 12296 | tf_op jit(solution)/shard_map/ppermute | solution.py:311
  89.0 1.7 collective-permute-start.17
  92.0 2.5 %collective-permute-done.15 = f32[8,128]{1,0:T(8,128)S(1)} collective-permute-done((f32[8,128]{1,0:T(8,128)S(1)}, f32[8,128]{1,0:T(8,128)S(1)}, u32[]{:S(2)}, u32[]{:S(2)}) %collective-permute-start.15) | collective-permute-done | bytes 4128 | tf_op jit(solution)/shard_map/ppermute | solution.py:311
  94.7 1.9 %collective-permute-start.20 = (f32[8,128]{1,0:T(8,128)S(1)}, f32[8,128]{1,0:T(8,128)S(1)}, u32[]{:S(2)}, u32[]{:S(2)}) collective-permute-start(f32[8,128]{1,0:T(8,128)S(1)} %add_add_fusion.2), channel_id=1, source_target_pairs={{0,192},{64,0},{128,64},{192,128},{1,193},{65,1},{129,65},{193,129... | collective-permute-start | bytes 12296 | tf_op jit(solution)/shard_map/ppermute | solution.py:355
  96.6 1.6 collective-permute-start.18
  98.3 1.9 %collective-permute-start.19 = (f32[8,128]{1,0:T(8,128)S(1)}, f32[8,128]{1,0:T(8,128)S(1)}, u32[]{:S(2)}, u32[]{:S(2)}) collective-permute-start(f32[8,128]{1,0:T(8,128)S(1)} %add_add_fusion.2), channel_id=1, source_target_pairs={{0,128},{64,192},{128,0},{192,64},{1,129},{65,193},{129,1},{193,65... | collective-permute-start | bytes 12296 | tf_op jit(solution)/shard_map/ppermute | solution.py:355
  100.3 1.9 %collective-permute-done.19 = f32[8,128]{1,0:T(8,128)S(1)} collective-permute-done((f32[8,128]{1,0:T(8,128)S(1)}, f32[8,128]{1,0:T(8,128)S(1)}, u32[]{:S(2)}, u32[]{:S(2)}) %collective-permute-start.19) | collective-permute-done | bytes 4128 | tf_op jit(solution)/shard_map/ppermute | solution.py:355
  102.3 5.0 %collective-permute-start.21 = (f32[8,128]{1,0:T(8,128)S(1)}, f32[8,128]{1,0:T(8,128)S(1)}, u32[]{:S(2)}, u32[]{:S(2)}) collective-permute-start(f32[8,128]{1,0:T(8,128)S(1)} %add_add_fusion.1), channel_id=1, source_target_pairs={{0,32},{4,36},{8,40},{12,44},{16,48},{20,52},{24,56},{28,60},{32,0... | collective-permute-start | bytes 12296 | tf_op jit(solution)/shard_map/ppermute | solution.py:311
  107.3 1.3 collective-permute-done.21
  108.6 3.5 %collective-permute-start.24 = (f32[8,128]{1,0:T(8,128)S(1)}, f32[8,128]{1,0:T(8,128)S(1)}, u32[]{:S(2)}, u32[]{:S(2)}) collective-permute-start(f32[8,128]{1,0:T(8,128)S(1)} %add.179), channel_id=1, source_target_pairs={{0,3},{1,0},{2,1},{3,2},{4,7},{5,4},{6,5},{7,6},{8,11},{9,8},{10,9... | collective-permute-start | bytes 12296 | tf_op jit(solution)/shard_map/ppermute | solution.py:357
  112.9 3.5 %collective-permute-done.22 = f32[8,128]{1,0:T(8,128)S(1)} collective-permute-done((f32[8,128]{1,0:T(8,128)S(1)}, f32[8,128]{1,0:T(8,128)S(1)}, u32[]{:S(2)}, u32[]{:S(2)}) %collective-permute-start.22) | collective-permute-done | bytes 4128 | tf_op jit(solution)/shard_map/ppermute | solution.py:357
  116.5 1.4 shard_map.214
  117.9 2.7 %collective-permute-start.25 = (bf16[720,128]{1,0:T(8,128)(2,1)S(1)}, bf16[720,128]{1,0:T(8,128)(2,1)S(1)}, u32[]{:S(2)}, u32[]{:S(2)}) collective-permute-start(bf16[720,128]{1,0:T(8,128)(2,1)S(1)} %get-tuple-element.29), channel_id=1, source_target_pairs={{0,32},{4,36},{8,40},{12,44},{16,48},{20,52},{24,56},{28,60},{32,0... | collective-permute-start | bytes 552968 | tf_op jit(solution)/shard_map/ppermute | solution.py:311
  120.6 7.6 %collective-permute-done.25 = bf16[720,128]{1,0:T(8,128)(2,1)S(1)} collective-permute-done((bf16[720,128]{1,0:T(8,128)(2,1)S(1)}, bf16[720,128]{1,0:T(8,128)(2,1)S(1)}, u32[]{:S(2)}, u32[]{:S(2)}) %collective-permute-start.25) | collective-permute-done | bytes 184352 | tf_op jit(solution)/shard_map/ppermute | solution.py:311
  128.3 2.7 %collective-permute-start.28 = (bf16[2,720,128]{2,1,0:T(8,128)(2,1)S(1)}, bf16[2,720,128]{2,1,0:T(8,128)(2,1)S(1)}, u32[]{:S(2)}, u32[]{:S(2)}) collective-permute-start(bf16[2,720,128]{2,1,0:T(8,128)(2,1)S(1)} %get-tuple-element.56), channel_id=1, source_target_pairs={{0,24},{4,28},{8,0},{12,4},{16,8},{20,12},{24,16},{28,20},{32,56},... | collective-permute-start | bytes 1105928 | tf_op jit(solution)/shard_map/ppermute | solution.py:311
  131.7 2.4 %collective-permute-start.30 = (bf16[128,128]{1,0:T(8,128)(2,1)S(1)}, bf16[128,128]{1,0:T(8,128)(2,1)S(1)}, u32[]{:S(2)}, u32[]{:S(2)}) collective-permute-start(bf16[128,128]{1,0:T(8,128)(2,1)S(1)} %get-tuple-element.38), channel_id=1, source_target_pairs={{0,32},{4,36},{8,40},{12,44},{16,48},{20,52},{24,56},{28,60},{32,0... | collective-permute-start | bytes 98312 | tf_op jit(solution)/shard_map/ppermute | solution.py:311
  134.1 4.3 %collective-permute-done.30 = bf16[128,128]{1,0:T(8,128)(2,1)S(1)} collective-permute-done((bf16[128,128]{1,0:T(8,128)(2,1)S(1)}, bf16[128,128]{1,0:T(8,128)(2,1)S(1)}, u32[]{:S(2)}, u32[]{:S(2)}) %collective-permute-start.30) | collective-permute-done | bytes 32800 | tf_op jit(solution)/shard_map/ppermute | solution.py:311
  138.4 2.1 %collective-permute-start.33 = (bf16[2,128,128]{2,1,0:T(8,128)(2,1)S(1)}, bf16[2,128,128]{2,1,0:T(8,128)(2,1)S(1)}, u32[]{:S(2)}, u32[]{:S(2)}) collective-permute-start(bf16[2,128,128]{2,1,0:T(8,128)(2,1)S(1)} %get-tuple-element.60), channel_id=1, source_target_pairs={{0,24},{4,28},{8,0},{12,4},{16,8},{20,12},{24,16},{28,20},{32,56},... | collective-permute-start | bytes 196616 | tf_op jit(solution)/shard_map/ppermute | solution.py:311
  140.5 1.8 collective-permute-start.32
  142.7 10.1 %collective-permute-start.29 = (bf16[4,2,720,128]{3,2,1,0:T(8,128)(2,1)S(1)}, bf16[4,2,720,128]{3,2,1,0:T(8,128)(2,1)S(1)}, u32[]{:S(2)}, u32[]{:S(2)}) collective-permute-start(bf16[4,2,720,128]{3,2,1,0:T(8,128)(2,1)S(1)} %pad_maximum_fusion.own_ref), channel_id=1, source_target_pairs={{0,4},{4,0},{8,12},{12,8},{16,20},{20,16},{24,28},{28,24},{32,36},... | collective-permute-start | bytes 4423688 | tf_op jit(solution)/shard_map/ppermute | solution.py:311
  152.9 1.4 collective-permute-start.36
  154.3 2.1 %collective-permute-start.35 = (bf16[4,2,128,128]{3,2,1,0:T(8,128)(2,1)S(1)}, bf16[4,2,128,128]{3,2,1,0:T(8,128)(2,1)S(1)}, u32[]{:S(2)}, u32[]{:S(2)}) collective-permute-start(bf16[4,2,128,128]{3,2,1,0:T(8,128)(2,1)S(1)} %get-tuple-element.58), channel_id=1, source_target_pairs={{0,128},{64,192},{128,0},{192,64},{1,129},{65,193},{129,1},{193,65... | collective-permute-start | bytes 786440 | tf_op jit(solution)/shard_map/ppermute | solution.py:376
  156.4 2.0 %collective-permute-done.36 = bf16[4,2,128,128]{3,2,1,0:T(8,128)(2,1)S(1)} collective-permute-done((bf16[4,2,128,128]{3,2,1,0:T(8,128)(2,1)S(1)}, bf16[4,2,128,128]{3,2,1,0:T(8,128)(2,1)S(1)}, u32[]{:S(2)}, u32[]{:S(2)}) %collective-permute-start.36) | collective-permute-done | bytes 262176 | tf_op jit(solution)/shard_map/ppermute | solution.py:376
  158.4 2.7 %collective-permute-done.35 = bf16[4,2,128,128]{3,2,1,0:T(8,128)(2,1)S(1)} collective-permute-done((bf16[4,2,128,128]{3,2,1,0:T(8,128)(2,1)S(1)}, bf16[4,2,128,128]{3,2,1,0:T(8,128)(2,1)S(1)}, u32[]{:S(2)}, u32[]{:S(2)}) %collective-permute-start.35) | collective-permute-done | bytes 262176 | tf_op jit(solution)/shard_map/ppermute | solution.py:376
  161.1 3.2 %collective-permute-done.34 = bf16[4,2,128,128]{3,2,1,0:T(8,128)(2,1)S(1)} collective-permute-done((bf16[4,2,128,128]{3,2,1,0:T(8,128)(2,1)S(1)}, bf16[4,2,128,128]{3,2,1,0:T(8,128)(2,1)S(1)}, u32[]{:S(2)}, u32[]{:S(2)}) %collective-permute-start.34) | collective-permute-done | bytes 262176 | tf_op jit(solution)/shard_map/ppermute | solution.py:376
  164.5 5.9 %collective-permute-start.37 = (bf16[4,4,2,128,128]{4,3,2,1,0:T(8,128)(2,1)S(1)}, bf16[4,4,2,128,128]{4,3,2,1,0:T(8,128)(2,1)S(1)}, u32[]{:S(2)}, u32[]{:S(2)}) collective-permute-start(bf16[4,4,2,128,128]{4,3,2,1,0:T(8,128)(2,1)S(1)} %pad_maximum_fusion.1.own_ref), channel_id=1, source_target_pairs={{0,4},{4,0},{8,12},{12,8},{16,20},{20,16},{24,28},{28,24},{32,36},... | collective-permute-start | bytes 3145736 | tf_op jit(solution)/shard_map/ppermute | solution.py:311
  170.4 2.3 %collective-permute-done.37.got_ref = bf16[4,4,2,128,128]{4,3,2,1,0:T(8,128)(2,1)S(1)} collective-permute-done((bf16[4,4,2,128,128]{4,3,2,1,0:T(8,128)(2,1)S(1)}, bf16[4,4,2,128,128]{4,3,2,1,0:T(8,128)(2,1)S(1)}, u32[]{:S(2)}, u32[]{:S(2)}) %collective-permute-start.37) | collective-permute-done | bytes 1048608 | tf_op jit(solution)/shard_map/ppermute | solution.py:311
  172.7 2.6 %shard_map.216 = bf16[64,14848]{1,0:T(8,128)(2,1)} custom-call(bf16[4,4,2,128,128]{4,3,2,1,0:T(8,128)(2,1)S(1)} %pad_maximum_fusion.1.own_ref, bf16[4,4,2,128,128]{4,3,2,1,0:T(8,128)(2,1)S(1)} %collective-permute-done.37.got_ref), custom_call_target="tpu_custom_call" | custom-call | tf_op jit(solution)/shard_map/pallas_call | solution.py:49
  175.3 3.1 %shard_map.215 = (bf16[128,3968]{1,0:T(8,128)(2,1)}, bf16[64,14848]{1,0:T(8,128)(2,1)}) custom-call(bf16[4,2,720,128]{3,2,1,0:T(8,128)(2,1)S(1)} %pad_maximum_fusion.own_ref, bf16[4,2,720,128]{3,2,1,0:T(8,128)(2,1)S(1)} %collective-permute-done.29.got_ref), custom_call_target="tpu_custom_call" | custom-call | tf_op jit(solution)/shard_map/pallas_call | solution.py:49
  (92 shorter events, 20.0 us)
Async XLA Ops:
  0.6 13.2 %copy-start = (bf16[1,1,64,14848]{3,2,1,0:T(8,128)(2,1)S(1)}, bf16[1,1,64,14848]{3,2,1,0:T(8,128)(2,1)}, u32[]{:S(2)}) copy-start(bf16[1,1,64,14848]{3,2,1,0:T(8,128)(2,1)} %param.16) | copy-start | bytes 5701636
  3.1 14.4 %collective-permute-start.6 = (bf16[64,3712]{1,0:T(8,128)(2,1)}, bf16[64,3712]{1,0:T(8,128)(2,1)}, u32[]{:S(2)}, u32[]{:S(2)}) collective-permute-start(bf16[64,3712]{1,0:T(8,128)(2,1)} %get-tuple-element.47), channel_id=1, source_target_pairs={{0,64},{192,128},{1,65},{193,129},{2,66},{194,130},{3,67},{195,131... | collective-permute-start | bytes 1425416 | tf_op jit(solution)/shard_map/ppermute | solution.py:319
  8.0 14.8 %collective-permute-start.7 = (bf16[64,3712]{1,0:T(8,128)(2,1)}, bf16[64,3712]{1,0:T(8,128)(2,1)}, u32[]{:S(2)}, u32[]{:S(2)}) collective-permute-start(bf16[64,3712]{1,0:T(8,128)(2,1)} %get-tuple-element.48), channel_id=1, source_target_pairs={{0,192},{192,0},{1,193},{193,1},{2,194},{194,2},{3,195},{195,3},{4... | collective-permute-start | bytes 1425416 | tf_op jit(solution)/shard_map/ppermute | solution.py:320
  11.8 15.3 %collective-permute-start.8 = (bf16[64,3712]{1,0:T(8,128)(2,1)S(1)}, bf16[64,3712]{1,0:T(8,128)(2,1)}, u32[]{:S(2)}, u32[]{:S(2)}) collective-permute-start(bf16[64,3712]{1,0:T(8,128)(2,1)S(1)} %get-tuple-element.46), channel_id=1, source_target_pairs={{0,128},{192,64},{1,129},{193,65},{2,130},{194,66},{3,131},{195,67... | collective-permute-start | bytes 1425416 | tf_op jit(solution)/shard_map/ppermute | solution.py:318
  16.4 16.4 %collective-permute-start = (bf16[64,3968]{1,0:T(8,128)(2,1)S(1)}, bf16[64,3968]{1,0:T(8,128)(2,1)S(1)}, u32[]{:S(2)}, u32[]{:S(2)}) collective-permute-start(bf16[64,3968]{1,0:T(8,128)(2,1)S(1)} %get-tuple-element.27), channel_id=1, source_target_pairs={{0,4},{4,0},{8,12},{12,8},{16,20},{20,16},{24,28},{28,24},{32,36},... | collective-permute-start | bytes 1523720 | tf_op jit(solution)/shard_map/ppermute | solution.py:311
  17.6 15.2 %collective-permute-start.1 = (bf16[8,64,1024]{2,1,0:T(8,128)(2,1)}, bf16[8,64,1024]{2,1,0:T(8,128)(2,1)S(1)}, u32[]{:S(2)}, u32[]{:S(2)}) collective-permute-start(bf16[8,64,1024]{2,1,0:T(8,128)(2,1)} %get-tuple-element.28), channel_id=1, source_target_pairs={{0,4},{4,0},{8,12},{12,8},{16,20},{20,16},{24,28},{28,24},{32,36},... | collective-permute-start | bytes 3145736 | tf_op jit(solution)/shard_map/ppermute | solution.py:311
  29.8 2.9 %collective-permute-start.9 = (f16[4,2,128,128]{3,2,1,0:T(8,128)(2,1)}, f16[4,2,128,128]{3,2,1,0:T(8,128)(2,1)S(1)}, u32[]{:S(2)}, u32[]{:S(2)}) collective-permute-start(f16[4,2,128,128]{3,2,1,0:T(8,128)(2,1)} %fusion.3), channel_id=1, source_target_pairs={{0,4},{4,0},{8,12},{12,8},{16,20},{20,16},{24,28},{28,24},{32,36},... | collective-permute-start | bytes 786440 | tf_op jit(solution)/shard_map/ppermute | solution.py:311
  40.5 27.0 %collective-permute-start.4 = (f16[2,712,128]{2,1,0:T(8,128)(2,1)}, f16[2,712,128]{2,1,0:T(8,128)(2,1)S(1)}, u32[]{:S(2)}, u32[]{:S(2)}) collective-permute-start(f16[2,712,128]{2,1,0:T(8,128)(2,1)} %get-tuple-element.50), channel_id=1, source_target_pairs={{0,24},{4,28},{8,0},{12,4},{16,8},{20,12},{24,16},{28,20},{32,56},... | collective-permute-start | bytes 1093640 | tf_op jit(solution)/shard_map/ppermute | solution.py:311
  42.9 24.5 %collective-permute-start.3 = (f16[2,712,128]{2,1,0:T(8,128)(2,1)}, f16[2,712,128]{2,1,0:T(8,128)(2,1)}, u32[]{:S(2)}, u32[]{:S(2)}) collective-permute-start(f16[2,712,128]{2,1,0:T(8,128)(2,1)} %get-tuple-element.51), channel_id=1, source_target_pairs={{0,16},{4,20},{8,24},{12,28},{16,0},{20,4},{24,8},{28,12},{32,48},... | collective-permute-start | bytes 1093640 | tf_op jit(solution)/shard_map/ppermute | solution.py:311
  43.5 24.0 %collective-permute-start.2 = (f16[2,712,128]{2,1,0:T(8,128)(2,1)}, f16[2,712,128]{2,1,0:T(8,128)(2,1)}, u32[]{:S(2)}, u32[]{:S(2)}) collective-permute-start(f16[2,712,128]{2,1,0:T(8,128)(2,1)} %get-tuple-element.49), channel_id=1, source_target_pairs={{0,8},{4,12},{8,16},{12,20},{16,24},{20,28},{24,0},{28,4},{32,40},... | collective-permute-start | bytes 1093640 | tf_op jit(solution)/shard_map/ppermute | solution.py:311
  44.1 17.0 %collective-permute-start.12 = (f16[2,128,128]{2,1,0:T(8,128)(2,1)S(1)}, f16[2,128,128]{2,1,0:T(8,128)(2,1)S(1)}, u32[]{:S(2)}, u32[]{:S(2)}) collective-permute-start(f16[2,128,128]{2,1,0:T(8,128)(2,1)S(1)} %get-tuple-element.53), channel_id=1, source_target_pairs={{0,24},{4,28},{8,0},{12,4},{16,8},{20,12},{24,16},{28,20},{32,56},... | collective-permute-start | bytes 196616 | tf_op jit(solution)/shard_map/ppermute | solution.py:311
  46.3 16.8 %collective-permute-start.11 = (f16[2,128,128]{2,1,0:T(8,128)(2,1)S(1)}, f16[2,128,128]{2,1,0:T(8,128)(2,1)S(1)}, u32[]{:S(2)}, u32[]{:S(2)}) collective-permute-start(f16[2,128,128]{2,1,0:T(8,128)(2,1)S(1)} %get-tuple-element.54), channel_id=1, source_target_pairs={{0,16},{4,20},{8,24},{12,28},{16,0},{20,4},{24,8},{28,12},{32,48},... | collective-permute-start | bytes 196616 | tf_op jit(solution)/shard_map/ppermute | solution.py:311
  61.1 5.3 %collective-permute-start.10 = (f16[2,128,128]{2,1,0:T(8,128)(2,1)S(1)}, f16[2,128,128]{2,1,0:T(8,128)(2,1)}, u32[]{:S(2)}, u32[]{:S(2)}) collective-permute-start(f16[2,128,128]{2,1,0:T(8,128)(2,1)S(1)} %get-tuple-element.52), channel_id=1, source_target_pairs={{0,8},{4,12},{8,16},{12,20},{16,24},{20,28},{24,0},{28,4},{32,40},... | collective-permute-start | bytes 196616 | tf_op jit(solution)/shard_map/ppermute | solution.py:311
  69.6 46.8 %copy-start.6 = (f32[1,64,928]{2,1,0:T(8,128)S(1)}, f32[1,64,928]{2,1,0:T(8,128)}, u32[]{:S(2)}) copy-start(f32[1,64,928]{2,1,0:T(8,128)} %param.17) | copy-start | bytes 712708
  69.6 46.8 %copy-start.7 = (f32[1,64,928]{2,1,0:T(8,128)S(1)}, f32[1,64,928]{2,1,0:T(8,128)}, u32[]{:S(2)}) copy-start(f32[1,64,928]{2,1,0:T(8,128)} %param.18) | copy-start | bytes 712708
  69.6 46.8 %copy-start.8 = (f32[1,64,928]{2,1,0:T(8,128)S(1)}, f32[1,64,928]{2,1,0:T(8,128)}, u32[]{:S(2)}) copy-start(f32[1,64,928]{2,1,0:T(8,128)} %param.19) | copy-start | bytes 712708
  69.6 46.8 %copy-start.9 = (f32[1,8,3968]{2,1,0:T(8,128)S(1)}, f32[1,8,3968]{2,1,0:T(8,128)}, u32[]{:S(2)}) copy-start(f32[1,8,3968]{2,1,0:T(8,128)} %param.13) | copy-start | bytes 380932
  69.6 46.9 %copy-start.10 = (f32[1,8,3968]{2,1,0:T(8,128)S(1)}, f32[1,8,3968]{2,1,0:T(8,128)}, u32[]{:S(2)}) copy-start(f32[1,8,3968]{2,1,0:T(8,128)} %param.14) | copy-start | bytes 380932
  69.6 46.8 %copy-start.11 = (f32[1,8,3968]{2,1,0:T(8,128)S(1)}, f32[1,8,3968]{2,1,0:T(8,128)}, u32[]{:S(2)}) copy-start(f32[1,8,3968]{2,1,0:T(8,128)} %param.15) | copy-start | bytes 380932
  69.6 46.8 %copy-start.12 = (f32[64,232]{1,0:T(8,128)S(1)}, f32[64,232]{1,0:T(8,128)}, u32[]{:S(2)}) copy-start(f32[64,232]{1,0:T(8,128)} %tw_ref.1) | copy-start | bytes 178180
  69.6 46.8 %copy-start.13 = (f32[64,232]{1,0:T(8,128)S(1)}, f32[64,232]{1,0:T(8,128)}, u32[]{:S(2)}) copy-start(f32[64,232]{1,0:T(8,128)} %tm_ref.1) | copy-start | bytes 178180
  69.6 46.8 %copy-start.14 = (f32[64,232]{1,0:T(8,128)S(1)}, f32[64,232]{1,0:T(8,128)}, u32[]{:S(2)}) copy-start(f32[64,232]{1,0:T(8,128)} %tv_ref.1) | copy-start | bytes 178180
  69.7 13.9 %collective-permute-start.5 = (f16[712,128]{1,0:T(8,128)(2,1)S(1)}, f16[712,128]{1,0:T(8,128)(2,1)S(1)}, u32[]{:S(2)}, u32[]{:S(2)}) collective-permute-start(f16[712,128]{1,0:T(8,128)(2,1)S(1)} %fusion.4), channel_id=1, source_target_pairs={{0,32},{4,36},{8,40},{12,44},{16,48},{20,52},{24,56},{28,60},{32,0... | collective-permute-start | bytes 546824 | tf_op jit(solution)/shard_map/ppermute | solution.py:311
  76.7 6.9 %collective-permute-start.13 = (f16[128,128]{1,0:T(8,128)(2,1)S(1)}, f16[128,128]{1,0:T(8,128)(2,1)S(1)}, u32[]{:S(2)}, u32[]{:S(2)}) collective-permute-start(f16[128,128]{1,0:T(8,128)(2,1)S(1)} %fusion.10), channel_id=1, source_target_pairs={{0,32},{4,36},{8,40},{12,44},{16,48},{20,52},{24,56},{28,60},{32,0... | collective-permute-start | bytes 98312 | tf_op jit(solution)/shard_map/ppermute | solution.py:311
  84.7 4.3 %collective-permute-start.14 = (f32[8,128]{1,0:T(8,128)S(1)}, f32[8,128]{1,0:T(8,128)S(1)}, u32[]{:S(2)}, u32[]{:S(2)}) collective-permute-start(f32[8,128]{1,0:T(8,128)S(1)} %add.171), channel_id=1, source_target_pairs={{0,4},{4,0},{8,12},{12,8},{16,20},{20,16},{24,28},{28,24},{32,36},... | collective-permute-start | bytes 12296 | tf_op jit(solution)/shard_map/ppermute | solution.py:311
  89.0 2.9 %collective-permute-start.17 = (f32[8,128]{1,0:T(8,128)S(1)}, f32[8,128]{1,0:T(8,128)S(1)}, u32[]{:S(2)}, u32[]{:S(2)}) collective-permute-start(f32[8,128]{1,0:T(8,128)S(1)} %add.172), channel_id=1, source_target_pairs={{0,24},{4,28},{8,0},{12,4},{16,8},{20,12},{24,16},{28,20},{32,56},... | collective-permute-start | bytes 12296 | tf_op jit(solution)/shard_map/ppermute | solution.py:311
  90.8 3.7 %collective-permute-start.15 = (f32[8,128]{1,0:T(8,128)S(1)}, f32[8,128]{1,0:T(8,128)S(1)}, u32[]{:S(2)}, u32[]{:S(2)}) collective-permute-start(f32[8,128]{1,0:T(8,128)S(1)} %add.172), channel_id=1, source_target_pairs={{0,8},{4,12},{8,16},{12,20},{16,24},{20,28},{24,0},{28,4},{32,40},... | collective-permute-start | bytes 12296 | tf_op jit(solution)/shard_map/ppermute | solution.py:311
  90.8 4.0 %collective-permute-start.16 = (f32[8,128]{1,0:T(8,128)S(1)}, f32[8,128]{1,0:T(8,128)S(1)}, u32[]{:S(2)}, u32[]{:S(2)}) collective-permute-start(f32[8,128]{1,0:T(8,128)S(1)} %add.172), channel_id=1, source_target_pairs={{0,16},{4,20},{8,24},{12,28},{16,0},{20,4},{24,8},{28,12},{32,48},... | collective-permute-start | bytes 12296 | tf_op jit(solution)/shard_map/ppermute | solution.py:311
  94.7 5.4 %collective-permute-start.20 = (f32[8,128]{1,0:T(8,128)S(1)}, f32[8,128]{1,0:T(8,128)S(1)}, u32[]{:S(2)}, u32[]{:S(2)}) collective-permute-start(f32[8,128]{1,0:T(8,128)S(1)} %add_add_fusion.2), channel_id=1, source_target_pairs={{0,192},{64,0},{128,64},{192,128},{1,193},{65,1},{129,65},{193,129... | collective-permute-start | bytes 12296 | tf_op jit(solution)/shard_map/ppermute | solution.py:355
  96.6 3.7 %collective-permute-start.18 = (f32[8,128]{1,0:T(8,128)S(1)}, f32[8,128]{1,0:T(8,128)S(1)}, u32[]{:S(2)}, u32[]{:S(2)}) collective-permute-start(f32[8,128]{1,0:T(8,128)S(1)} %add_add_fusion.2), channel_id=1, source_target_pairs={{0,64},{64,128},{128,192},{192,0},{1,65},{65,129},{129,193},{193,1... | collective-permute-start | bytes 12296 | tf_op jit(solution)/shard_map/ppermute | solution.py:355
  98.3 4.0 %collective-permute-start.19 = (f32[8,128]{1,0:T(8,128)S(1)}, f32[8,128]{1,0:T(8,128)S(1)}, u32[]{:S(2)}, u32[]{:S(2)}) collective-permute-start(f32[8,128]{1,0:T(8,128)S(1)} %add_add_fusion.2), channel_id=1, source_target_pairs={{0,128},{64,192},{128,0},{192,64},{1,129},{65,193},{129,1},{193,65... | collective-permute-start | bytes 12296 | tf_op jit(solution)/shard_map/ppermute | solution.py:355
  102.3 6.4 %collective-permute-start.21 = (f32[8,128]{1,0:T(8,128)S(1)}, f32[8,128]{1,0:T(8,128)S(1)}, u32[]{:S(2)}, u32[]{:S(2)}) collective-permute-start(f32[8,128]{1,0:T(8,128)S(1)} %add_add_fusion.1), channel_id=1, source_target_pairs={{0,32},{4,36},{8,40},{12,44},{16,48},{20,52},{24,56},{28,60},{32,0... | collective-permute-start | bytes 12296 | tf_op jit(solution)/shard_map/ppermute | solution.py:311
  108.6 4.3 %collective-permute-start.24 = (f32[8,128]{1,0:T(8,128)S(1)}, f32[8,128]{1,0:T(8,128)S(1)}, u32[]{:S(2)}, u32[]{:S(2)}) collective-permute-start(f32[8,128]{1,0:T(8,128)S(1)} %add.179), channel_id=1, source_target_pairs={{0,3},{1,0},{2,1},{3,2},{4,7},{5,4},{6,5},{7,6},{8,11},{9,8},{10,9... | collective-permute-start | bytes 12296 | tf_op jit(solution)/shard_map/ppermute | solution.py:357
  112.1 4.3 %collective-permute-start.22 = (f32[8,128]{1,0:T(8,128)S(1)}, f32[8,128]{1,0:T(8,128)S(1)}, u32[]{:S(2)}, u32[]{:S(2)}) collective-permute-start(f32[8,128]{1,0:T(8,128)S(1)} %add.179), channel_id=1, source_target_pairs={{0,1},{1,2},{2,3},{3,0},{4,5},{5,6},{6,7},{7,4},{8,9},{9,10},{10,1... | collective-permute-start | bytes 12296 | tf_op jit(solution)/shard_map/ppermute | solution.py:357
  112.1 4.3 %collective-permute-start.23 = (f32[8,128]{1,0:T(8,128)S(1)}, f32[8,128]{1,0:T(8,128)S(1)}, u32[]{:S(2)}, u32[]{:S(2)}) collective-permute-start(f32[8,128]{1,0:T(8,128)S(1)} %add.179), channel_id=1, source_target_pairs={{0,2},{1,3},{2,0},{3,1},{4,6},{5,7},{6,4},{7,5},{8,10},{9,11},{10,... | collective-permute-start | bytes 12296 | tf_op jit(solution)/shard_map/ppermute | solution.py:357
  117.9 10.3 %collective-permute-start.25 = (bf16[720,128]{1,0:T(8,128)(2,1)S(1)}, bf16[720,128]{1,0:T(8,128)(2,1)S(1)}, u32[]{:S(2)}, u32[]{:S(2)}) collective-permute-start(bf16[720,128]{1,0:T(8,128)(2,1)S(1)} %get-tuple-element.29), channel_id=1, source_target_pairs={{0,32},{4,36},{8,40},{12,44},{16,48},{20,52},{24,56},{28,60},{32,0... | collective-permute-start | bytes 552968 | tf_op jit(solution)/shard_map/ppermute | solution.py:311
  128.3 13.9 %collective-permute-start.28 = (bf16[2,720,128]{2,1,0:T(8,128)(2,1)S(1)}, bf16[2,720,128]{2,1,0:T(8,128)(2,1)S(1)}, u32[]{:S(2)}, u32[]{:S(2)}) collective-permute-start(bf16[2,720,128]{2,1,0:T(8,128)(2,1)S(1)} %get-tuple-element.56), channel_id=1, source_target_pairs={{0,24},{4,28},{8,0},{12,4},{16,8},{20,12},{24,16},{28,20},{32,56},... | collective-permute-start | bytes 1105928 | tf_op jit(solution)/shard_map/ppermute | solution.py:311
  131.0 11.2 %collective-permute-start.27 = (bf16[2,720,128]{2,1,0:T(8,128)(2,1)S(1)}, bf16[2,720,128]{2,1,0:T(8,128)(2,1)S(1)}, u32[]{:S(2)}, u32[]{:S(2)}) collective-permute-start(bf16[2,720,128]{2,1,0:T(8,128)(2,1)S(1)} %get-tuple-element.56), channel_id=1, source_target_pairs={{0,16},{4,20},{8,24},{12,28},{16,0},{20,4},{24,8},{28,12},{32,48},... | collective-permute-start | bytes 1105928 | tf_op jit(solution)/shard_map/ppermute | solution.py:311
  131.0 11.5 %collective-permute-start.26 = (bf16[2,720,128]{2,1,0:T(8,128)(2,1)S(1)}, bf16[2,720,128]{2,1,0:T(8,128)(2,1)S(1)}, u32[]{:S(2)}, u32[]{:S(2)}) collective-permute-start(bf16[2,720,128]{2,1,0:T(8,128)(2,1)S(1)} %get-tuple-element.56), channel_id=1, source_target_pairs={{0,8},{4,12},{8,16},{12,20},{16,24},{20,28},{24,0},{28,4},{32,40},... | collective-permute-start | bytes 1105928 | tf_op jit(solution)/shard_map/ppermute | solution.py:311
  131.7 6.7 %collective-permute-start.30 = (bf16[128,128]{1,0:T(8,128)(2,1)S(1)}, bf16[128,128]{1,0:T(8,128)(2,1)S(1)}, u32[]{:S(2)}, u32[]{:S(2)}) collective-permute-start(bf16[128,128]{1,0:T(8,128)(2,1)S(1)} %get-tuple-element.38), channel_id=1, source_target_pairs={{0,32},{4,36},{8,40},{12,44},{16,48},{20,52},{24,56},{28,60},{32,0... | collective-permute-start | bytes 98312 | tf_op jit(solution)/shard_map/ppermute | solution.py:311
  138.4 14.5 %collective-permute-start.33 = (bf16[2,128,128]{2,1,0:T(8,128)(2,1)S(1)}, bf16[2,128,128]{2,1,0:T(8,128)(2,1)S(1)}, u32[]{:S(2)}, u32[]{:S(2)}) collective-permute-start(bf16[2,128,128]{2,1,0:T(8,128)(2,1)S(1)} %get-tuple-element.60), channel_id=1, source_target_pairs={{0,24},{4,28},{8,0},{12,4},{16,8},{20,12},{24,16},{28,20},{32,56},... | collective-permute-start | bytes 196616 | tf_op jit(solution)/shard_map/ppermute | solution.py:311
  140.5 12.4 %collective-permute-start.32 = (bf16[2,128,128]{2,1,0:T(8,128)(2,1)S(1)}, bf16[2,128,128]{2,1,0:T(8,128)(2,1)S(1)}, u32[]{:S(2)}, u32[]{:S(2)}) collective-permute-start(bf16[2,128,128]{2,1,0:T(8,128)(2,1)S(1)} %get-tuple-element.60), channel_id=1, source_target_pairs={{0,16},{4,20},{8,24},{12,28},{16,0},{20,4},{24,8},{28,12},{32,48},... | collective-permute-start | bytes 196616 | tf_op jit(solution)/shard_map/ppermute | solution.py:311
  142.2 10.6 %collective-permute-start.31 = (bf16[2,128,128]{2,1,0:T(8,128)(2,1)S(1)}, bf16[2,128,128]{2,1,0:T(8,128)(2,1)S(1)}, u32[]{:S(2)}, u32[]{:S(2)}) collective-permute-start(bf16[2,128,128]{2,1,0:T(8,128)(2,1)S(1)} %get-tuple-element.60), channel_id=1, source_target_pairs={{0,8},{4,12},{8,16},{12,20},{16,24},{20,28},{24,0},{28,4},{32,40},... | collective-permute-start | bytes 196616 | tf_op jit(solution)/shard_map/ppermute | solution.py:311
  142.7 32.5 %collective-permute-start.29 = (bf16[4,2,720,128]{3,2,1,0:T(8,128)(2,1)S(1)}, bf16[4,2,720,128]{3,2,1,0:T(8,128)(2,1)S(1)}, u32[]{:S(2)}, u32[]{:S(2)}) collective-permute-start(bf16[4,2,720,128]{3,2,1,0:T(8,128)(2,1)S(1)} %pad_maximum_fusion.own_ref), channel_id=1, source_target_pairs={{0,4},{4,0},{8,12},{12,8},{16,20},{20,16},{24,28},{28,24},{32,36},... | collective-permute-start | bytes 4423688 | tf_op jit(solution)/shard_map/ppermute | solution.py:311
  152.9 5.5 %collective-permute-start.36 = (bf16[4,2,128,128]{3,2,1,0:T(8,128)(2,1)S(1)}, bf16[4,2,128,128]{3,2,1,0:T(8,128)(2,1)S(1)}, u32[]{:S(2)}, u32[]{:S(2)}) collective-permute-start(bf16[4,2,128,128]{3,2,1,0:T(8,128)(2,1)S(1)} %get-tuple-element.58), channel_id=1, source_target_pairs={{0,192},{64,0},{128,64},{192,128},{1,193},{65,1},{129,65},{193,129... | collective-permute-start | bytes 786440 | tf_op jit(solution)/shard_map/ppermute | solution.py:376
  154.3 6.8 %collective-permute-start.35 = (bf16[4,2,128,128]{3,2,1,0:T(8,128)(2,1)S(1)}, bf16[4,2,128,128]{3,2,1,0:T(8,128)(2,1)S(1)}, u32[]{:S(2)}, u32[]{:S(2)}) collective-permute-start(bf16[4,2,128,128]{3,2,1,0:T(8,128)(2,1)S(1)} %get-tuple-element.58), channel_id=1, source_target_pairs={{0,128},{64,192},{128,0},{192,64},{1,129},{65,193},{129,1},{193,65... | collective-permute-start | bytes 786440 | tf_op jit(solution)/shard_map/ppermute | solution.py:376
  156.4 7.9 %collective-permute-start.34 = (bf16[4,2,128,128]{3,2,1,0:T(8,128)(2,1)S(1)}, bf16[4,2,128,128]{3,2,1,0:T(8,128)(2,1)S(1)}, u32[]{:S(2)}, u32[]{:S(2)}) collective-permute-start(bf16[4,2,128,128]{3,2,1,0:T(8,128)(2,1)S(1)} %get-tuple-element.58), channel_id=1, source_target_pairs={{0,64},{64,128},{128,192},{192,0},{1,65},{65,129},{129,193},{193,1... | collective-permute-start | bytes 786440 | tf_op jit(solution)/shard_map/ppermute | solution.py:376
  164.5 8.2 %collective-permute-start.37 = (bf16[4,4,2,128,128]{4,3,2,1,0:T(8,128)(2,1)S(1)}, bf16[4,4,2,128,128]{4,3,2,1,0:T(8,128)(2,1)S(1)}, u32[]{:S(2)}, u32[]{:S(2)}) collective-permute-start(bf16[4,4,2,128,128]{4,3,2,1,0:T(8,128)(2,1)S(1)} %pad_maximum_fusion.1.own_ref), channel_id=1, source_target_pairs={{0,4},{4,0},{8,12},{12,8},{16,20},{20,16},{24,28},{28,24},{32,36},... | collective-permute-start | bytes 3145736 | tf_op jit(solution)/shard_map/ppermute | solution.py:311
  (7 other events, 18.3 us)

commit v2 on v0

v2 whole, which is shorter than its diff:
```python
import math

import jax
import jax.numpy as jnp
from jax import lax
from jax.experimental import pallas as pl
from jax.experimental.pallas import tpu as pltpu
from jax.sharding import PartitionSpec as P

STEP = 10

beta_first = 0.9
beta_second = 0.95
learn_rate = 0.02
weight_decay = 0.1
tiny_value = 1e-08

F32, BF16, F16 = jnp.float32, jnp.bfloat16, jnp.float16

QT = 31
QROWS, OROWS, TROWS = 256, 464, 128
PACK = QROWS + OROWS
UPPER = 352


def pair_perm(move):
    return [(d, move(d)) for d in range(16)]


CORE = pair_perm(lambda d: d ^ 1)
ZHALF = pair_perm(lambda d: d ^ 8)


def x_perm(e):
    return pair_perm(lambda d: d ^ (2 * e))


def ring_perm(k):
    return [(i, (i + k) % 4) for i in range(4)]


def lanes(rows):
    return lax.broadcasted_iota(jnp.int32, (rows, 128), 1)


def call(kernel, outs, *args, micros=2, hbm=(), out_hbm=(), scratch=(), vmem=16):
    return pl.pallas_call(
        kernel,
        out_shape=list(outs) if isinstance(outs, (list, tuple)) else outs,
        cost_estimate=pl.CostEstimate(flops=0, bytes_accessed=3000000 * micros, transcendentals=0),
        in_specs=[
            pl.BlockSpec(memory_space=pltpu.HBM if i in hbm else pltpu.VMEM)
            for i in range(len(args))
        ],
        out_specs=jax.tree.map(
            lambda i: pl.BlockSpec(memory_space=pltpu.HBM if i in out_hbm else pltpu.VMEM),
            list(range(len(outs))) if isinstance(outs, (list, tuple)) else 0,
        ),
        scratch_shapes=scratch,
        compiler_params=pltpu.CompilerParams(vmem_limit_bytes=vmem * 1024 * 1024),
    )(*args)


def out(shape, dtype):
    return jax.ShapeDtypeStruct(shape, dtype)


def position():
    d = lax.axis_index("dp")
    return d // 8, (d // 2) % 4, d % 2


def chunk_copy(src_ref, dst_ref, sems, index, chunk):
    return pltpu.make_async_copy(src_ref.at[chunk], dst_ref.at[chunk], sems.at[index])


def columns(s):
    return slice(None), pl.ds(pl.multiple_of(s * 3712, 128), 3712)


def rolled(value, turn):
    return pltpu.roll(value, turn, 1) if turn else value


def table_split_kernel(t_hbm, _, own_ref, send_ref, t_ref, sems):
    _, _, core = position()
    lane = lanes(64)
    for s in range(4):
        chunk_copy(t_hbm, t_ref, sems, s, columns(s)).start()

    def split(outs):
        def quarter(s, carry):
            chunk_copy(t_hbm, t_ref, sems, s, columns(s)).wait()
            base = pl.multiple_of(s * 3712, 128)
            for d in range(16):
                start, shift = 232 * d // 128, 232 * d % 128
                count = -(-(shift + 232) // 128)
                tiles = [
                    rolled(t_ref[:, pl.ds(base + 128 * (start + i), 128)], -shift % 128)
                    for i in range(count)
                ]
                for i in range(2):
                    v = tiles[i]
                    if shift and i + 1 < count:
                        v = jnp.where(lane < 128 - shift, v, tiles[i + 1])
                    if i == 1:
                        v = jnp.where(lane < 104, v, jnp.zeros_like(v))
                    outs[d % 2][s, d // 2, 64 * i : 64 * i + 64, :] = v
            return carry

        lax.fori_loop(0, 4, quarter, 0)

    pl.when(core == 0)(lambda: split((own_ref, send_ref)))
    pl.when(core == 1)(lambda: split((send_ref, own_ref)))


def split_kernel(q_hbm, o_hbm, own_ref, send_ref, tick_ref, q_ref, o_ref, q_sems, o_sems):
    _, x, core = position()
    lane = lanes(64)
    lane16 = lanes(16)

    def rows(s):
        return pl.ds(pl.multiple_of(s * 32, 32), 32), slice(None)

    tick_ref[...] = jnp.zeros_like(tick_ref)
    for s in range(4):
        chunk_copy(q_hbm, q_ref, q_sems, s, rows(s)).start()
        chunk_copy(o_hbm, o_ref, o_sems, s, columns(s)).start()

    def split(outs):
        def group(s, carry):
            chunk_copy(q_hbm, q_ref, q_sems, s, rows(s)).wait()
            chunk_copy(o_hbm, o_ref, o_sems, s, columns(s)).wait()
            half = s // 2
            for p in range(2):
                slot = (2 * (s % 2) + p) ^ x
                v = q_ref[pl.ds(pl.multiple_of(s * 32 + 16 * p, 16), 16), :]
                for c in range(2):
                    out_ref = outs[c]
                    part = v[8 * c : 8 * c + 8]
                    for t in range(16):
                        low = part[:, 128 * t : 128 * t + 128]
                        t2 = t + 16
                        high = part[:, 128 * t2 : 128 * t2 + 128] if t2 < QT else jnp.zeros_like(low)
                        out_ref[half, slot, 16 * t : 16 * t + 16, :] = jnp.concatenate(
                            [low, high], axis=0
                        )
                    b = 2 * p + c
                    shift = 32 * b
                    base = s * 3712 + 128 * (29 * b // 4)
                    tiles = [
                        rolled(
                            o_ref[:, pl.ds(pl.multiple_of(base + 128 * t, 128), 128)],
                            -shift % 128,
                        )
                        for t in range(8)
                    ]
                    for t in range(7):
                        w = jnp.where(lane < 128 - shift, tiles[t], tiles[t + 1]) if b else tiles[t]
                        first = QROWS + 64 * t
                        out_ref[half, slot, first : first + 64, :] = w
                    last = tiles[7]
                    rest = last[0:16]
                    for g in range(1, 4):
                        piece = pltpu.roll(last[16 * g : 16 * g + 16], 32 * g, 1)
                        rest = jnp.where(lane16 < 32 * g, rest, piece)
                    out_ref[half, slot, QROWS + 448 : QROWS + 464, :] = rest
            return carry

        lax.fori_loop(0, 4, group, 0)

    pl.when(core == 0)(lambda: split((own_ref, send_ref)))
    pl.when(core == 1)(lambda: split((send_ref, own_ref)))


def adamw(gradient, master, first, second, factor):
    clipped = gradient * factor
    first_new = beta_first * first + (1.0 - beta_first) * clipped
    second_new = beta_second * second + (1.0 - beta_second) * clipped * clipped
    first_hat = first_new / (1.0 - beta_first**STEP)
    second_hat = second_new / (1.0 - beta_second**STEP)
    master_new = master - learn_rate * (
        first_hat / (jnp.sqrt(second_hat) + tiny_value) + weight_decay * master
    )
    return master_new, first_new, second_new


def update_kernel(limit):
    def kernel(
        n_ref, g_ref,
        qw_ref, qm_ref, qv_ref, ow_ref, om_ref, ov_ref, tw_ref, tm_ref, tv_ref,
        pack_ref,
        qw2_ref, qm2_ref, qv2_ref, ow2_ref, om2_ref, ov2_ref, tw2_ref, tm2_ref, tv2_ref,
    ):
        grad_norm = jnp.sqrt(jnp.sum(n_ref[...], keepdims=True))
        factor = jnp.minimum(1.0, limit / (grad_norm + 1e-06))

        def step(g, rows, cols, refs, outs):
            new = adamw(g, *(r[rows, cols] for r in refs), factor)
            for ref, value in zip(outs, new):
                ref[rows, cols] = value
            return new[0]

        refs, outs = (qw_ref, qm_ref, qv_ref), (qw2_ref, qm2_ref, qv2_ref)
        every = slice(None)
        new = [
            step(
                g_ref[16 * (t % 16) + 8 * (t // 16) : 16 * (t % 16) + 8 * (t // 16) + 8, :],
                every, slice(128 * t, 128 * t + 128), refs, outs,
            )
            for t in range(QT)
        ]
        new.append(jnp.zeros_like(new[0]))
        for t in range(16):
            pack_ref[16 * t : 16 * t + 16, :] = jnp.concatenate(
                [new[t], new[t + 16]], axis=0
            ).astype(BF16)

        refs, outs = (ow_ref, om_ref, ov_ref), (ow2_ref, om2_ref, ov2_ref)
        for t in range(7):
            g = g_ref[QROWS + 64 * t : QROWS + 64 * t + 64, :]
            w = step(g, every, slice(128 * t, 128 * t + 128), refs, outs)
            pack_ref[QROWS + 64 * t : QROWS + 64 * t + 64, :] = w.astype(BF16)
        rest = g_ref[QROWS + 448 : QROWS + 464, :]
        lane = lanes(16)
        packed = jnp.zeros((16, 128), F32)
        for g in range(4):
            piece = rest if g == 0 else pltpu.roll(rest, 128 - 32 * g, 1)
            w = step(piece[:, 0:32], slice(16 * g, 16 * g + 16), slice(896, 928), refs, outs)
            w = jnp.concatenate([w, jnp.zeros((16, 96), F32)], axis=1)
            w = w if g == 0 else pltpu.roll(w, 32 * g, 1)
            packed = jnp.where((lane >= 32 * g) & (lane < 32 * g + 32), w, packed)
        pack_ref[QROWS + 448 : QROWS + 464, :] = packed.astype(BF16)

        refs, outs = (tw_ref, tm_ref, tv_ref), (tw2_ref, tm2_ref, tv2_ref)
        w = step(g_ref[PACK : PACK + 64, :], every, slice(0, 128), refs, outs)
        pack_ref[PACK : PACK + 64, :] = w.astype(BF16)
        w = step(g_ref[PACK + 64 : PACK + 128, 0:104], every, slice(128, 232), refs, outs)
        pack_ref[PACK + 64 : PACK + 128, :] = jnp.concatenate([w, jnp.zeros((64, 24), F32)], axis=1).astype(BF16)

    return kernel


def cover(t, width, count):
    found = []
    for b in range(count):
        begin = 128 * t - width * b
        for i in range(-(-width // 128)):
            lo = max(0, 128 * i - begin)
            hi = min(128, 128 * i - begin + 128, width - begin)
            if lo < hi:
                found.append((b, i, (-begin) % 128, lo, hi))
    return found


def join_kernel(own_ref, got_ref, _, q_hbm, o_hbm, q_ref, o_ref, q_sems, o_sems):
    zh, x, core = position()
    lane = lanes(64)

    def row_copy(j):
        chunk = pl.ds(pl.multiple_of(j * 16, 16), 16), slice(None)
        return chunk_copy(q_ref, q_hbm, q_sems, j, chunk)

    def join(refs):
        def rows(j, carry):
            index = (zh ^ (j // 4), x ^ (j % 4))
            for p in range(16):
                a, b = (ref[(*index, slice(16 * p, 16 * p + 16), slice(None))] for ref in refs)
                for t, part in ((p, slice(0, 8)), (p + 16, slice(8, 16))):
                    if t < QT:
                        q_ref[pl.ds(pl.multiple_of(j * 16, 16), 16), 128 * t : 128 * t + 128] = (
                            jnp.concatenate([a[part], b[part]], axis=0)
                        )
            row_copy(j).start()
            return carry

        lax.fori_loop(0, 8, rows, 0)

        def cols(g, carry):
            index = [
                (zh ^ (g // 2), x ^ (2 * (g % 2) + b // 2))
                for b in range(4)
            ]

            def tile(b, i, turn):
                if i < 7:
                    rows = slice(QROWS + 64 * i, QROWS + 64 * i + 64)
                    v = refs[b % 2][(*index[b], rows, slice(None))]
                    return pltpu.roll(v, turn, 1) if turn else v
                v = refs[b % 2][(*index[b], slice(QROWS + 448, QROWS + 464), slice(None))]
                parts = []
                for k in range(4):
                    move = (turn - 32 * k) % 128
                    parts.append(pltpu.roll(v, move, 1) if move else v)
                return jnp.concatenate(parts, axis=0)

            base = pl.multiple_of(g * 3712, 128)
            for t in range(29):
                value = None
                for b, i, turn, lo, hi in cover(t, 928, 4):
                    v = tile(b, i, turn)
                    value = v if value is None else jnp.where(lane >= lo, v, value)
                o_ref[:, pl.ds(base + 128 * t, 128)] = value
            chunk_copy(o_ref, o_hbm, o_sems, g, columns(g)).start()
            return carry

        lax.fori_loop(0, 4, cols, 0)

    pl.when(core == 0)(lambda: join((own_ref, got_ref)))
    pl.when(core == 1)(lambda: join((got_ref, own_ref)))
    for j in range(8):
        row_copy(j).wait()
    for g in range(4):
        chunk_copy(o_ref, o_hbm, o_sems, g, columns(g)).wait()


def table_join_kernel(own_ref, got_ref, t_hbm, tick_ref, t_ref, sems):
    tick_ref[...] = jnp.zeros_like(tick_ref)
    zh, x, core = position()
    section = lax.axis_index("section")
    lane = lanes(64)

    def join(refs):
        def quarter(s, carry):
            m = (section - s + 4) % 4
            base = pl.multiple_of(s * 3712, 128)
            for t in range(29):
                value = None
                for d, i, turn, lo, hi in cover(t, 232, 16):
                    index = (m, x ^ ((d // 2) % 4), zh ^ (d // 8))
                    rows = slice(64 * i, 64 * i + 64)
                    v = refs[d % 2][(*index, rows, slice(None))]
                    v = pltpu.roll(v, turn, 1) if turn else v
                    value = v if value is None else jnp.where(lane >= lo, v, value)
                t_ref[:, pl.ds(base + 128 * t, 128)] = value
            chunk_copy(t_ref, t_hbm, sems, s, columns(s)).start()
            return carry

        lax.fori_loop(0, 4, quarter, 0)

    pl.when(core == 0)(lambda: join((own_ref, got_ref)))
    pl.when(core == 1)(lambda: join((got_ref, own_ref)))
    for s in range(4):
        chunk_copy(t_ref, t_hbm, sems, s, columns(s)).wait()


def per_device(
    query_grads,
    query_master,
    query_first,
    query_second,
    output_grads,
    output_master,
    output_first,
    output_second,
    table_grads,
    table_master,
    table_first,
    table_second,
):
    section = lax.axis_index("section")
    member = lax.axis_index("dp")
    zh, x = member // 8, (member // 2) % 4
    query, output, table = query_grads[0, 0], output_grads[0, 0], table_grads[0, 0]

    def dp_send(value, perm):
        return lax.ppermute(value, "dp", perm)

    def pick(value, i):
        return lax.dynamic_index_in_dim(value, i, 0, False)

    own, send, tick = call(
        split_kernel, [out((2, 4, PACK, 128), BF16)] * 2 + [out((8, 128), F32)], query, output,
        hbm=(0, 1), micros=3, vmem=60,
        scratch=[
            pltpu.VMEM((128, 3968), BF16), pltpu.VMEM((64, 14848), BF16),
            pltpu.SemaphoreType.DMA((4,)), pltpu.SemaphoreType.DMA((4,)),
        ],
    )
    got = dp_send(send, CORE)
    t_own, t_send = call(
        table_split_kernel, [out((4, 8, TROWS, 128), BF16)] * 2, table, tick, hbm=(0,),
        scratch=[pltpu.VMEM((64, 14848), BF16), pltpu.SemaphoreType.DMA((4,))],
    )

    def slots(h, e):
        return own[h, e].astype(F32) + got[h, e].astype(F32)

    near, wrap = slots(0, slice(1, 3)).astype(F16), slots(1, slice(2, 4)).astype(F16)
    near, wrap, t_send = lax.optimization_barrier((near, wrap, t_send))
    t_got = dp_send(t_send, CORE)
    near = dp_send(near, x_perm(1)).astype(F32)
    wrap = dp_send(wrap, x_perm(3)).astype(F32)
    near_last = dp_send((slots(0, 3) + near[1]).astype(F16), x_perm(3)).astype(F32)
    wrap_last = dp_send((slots(1, 1) + wrap[0]).astype(F16), x_perm(1)).astype(F32)
    halves = (slots(0, 0) + near[0] + near_last, slots(1, 0) + wrap[1] + wrap_last)

    first_section = section == 0
    at_ends = jnp.logical_or(first_section, section == 3)

    def quarter(i):
        return pick(t_own, i).astype(F32) + pick(t_got, i).astype(F32)

    def section_send(i, perm):
        return lax.ppermute(quarter(i).astype(F16), "section", perm)

    t_far = section_send(jnp.where(first_section, 2, 1), [(0, 2), (3, 1)])
    t_near = section_send(jnp.where(first_section, 1, 2), [(0, 1), (3, 2)])
    t_end = section_send(jnp.where(first_section, 3, 0), [(0, 3), (3, 0)])
    t_sum = jnp.where(at_ends, quarter(section), t_near.astype(F32)) + jnp.where(
        at_ends, t_end, t_far
    ).astype(F32)
    t_sum = t_sum.reshape(2, 4, TROWS, 128)

    def t_slot(k):
        return lax.dynamic_index_in_dim(t_sum, x ^ k, 1, False)

    t_parts = [t_slot(0)] + [dp_send(t_slot(k).astype(F16), x_perm(k)) for k in (1, 2, 3)]

    first_half = zh == 0

    def t_half(i):
        return sum(pick(v, i).astype(F32) for v in t_parts)

    leave = jnp.concatenate([jnp.where(first_half, halves[1], halves[0]), t_half(1 - zh)])
    keep = jnp.concatenate([jnp.where(first_half, halves[0], halves[1]), t_half(zh)])
    gradient = keep + dp_send(leave.astype(F16), ZHALF).astype(F32)

    squares = jnp.sum((gradient * gradient).reshape(-1, 8, 128), axis=0)
    squares = squares + dp_send(squares, CORE)
    squares = squares + sum(dp_send(squares, x_perm(k)) for k in (1, 2, 3))
    squares = squares + sum(lax.ppermute(squares, "section", ring_perm(k)) for k in (1, 2, 3))
    squares = squares + dp_send(squares, ZHALF)
    squares = squares + sum(lax.ppermute(squares, "tensor", ring_perm(k)) for k in (1, 2, 3))

    params_count = 4 * (128 * 15872 + 256 * 14848) + 256 * 14848
    limit = 0.5 * math.sqrt(params_count)
    small = [out((8, 3968), F32)] * 3 + [out((64, 928), F32)] * 3 + [out((64, 232), F32)] * 3
    packed, *new = call(
        update_kernel(limit),
        (out((PACK + TROWS, 128), BF16), *small),
        squares, gradient,
        query_master[0], query_first[0], query_second[0],
        output_master[0], output_first[0], output_second[0],
        table_master, table_first, table_second,
    )

    def along_x(value):
        return jnp.stack([value] + [dp_send(value, x_perm(k)) for k in (1, 2, 3)])

    packed = jnp.stack([packed, dp_send(packed, ZHALF)])
    t_all = along_x(packed[:, PACK:])
    upper, lower = packed[:, :UPPER], packed[:, UPPER:PACK]
    upper_wrap = dp_send(upper, x_perm(3))
    lower_near = dp_send(lower, x_perm(1))
    _, upper_wrap, lower_near = lax.optimization_barrier((t_all, upper_wrap, lower_near))
    t_all = jnp.stack([t_all] + [lax.ppermute(t_all, "section", ring_perm(k)) for k in (1, 2, 3)])
    upper_rest = dp_send(jnp.stack([upper, upper_wrap]), x_perm(1))
    lower_rest = dp_send(jnp.stack([lower, lower_near]), x_perm(3))
    _, upper_rest, lower_rest = lax.optimization_barrier((t_all, upper_rest, lower_rest))
    w_all = jnp.concatenate(
        [
            jnp.stack([upper, upper_rest[0], upper_rest[1], upper_wrap], axis=1),
            jnp.stack([lower, lower_near, lower_rest[1], lower_rest[0]], axis=1),
        ],
        axis=2,
    )
    t_other = dp_send(t_all, CORE)
    t_other, w_all = lax.optimization_barrier((t_other, w_all))
    w_other = dp_send(w_all, CORE)
    table_full, tick = call(
        table_join_kernel, (out((64, 14848), BF16), out((8, 128), F32)), t_all, t_other,
        out_hbm=(0,), scratch=[pltpu.VMEM((64, 14848), BF16), pltpu.SemaphoreType.DMA((4,))],
    )
    query_full, output_full = call(
        join_kernel, (out((128, 3968), BF16), out((64, 14848), BF16)),
        w_all, w_other, tick, micros=3, out_hbm=(0, 1),
        scratch=[
            pltpu.VMEM((128, 3968), BF16), pltpu.VMEM((64, 14848), BF16),
            pltpu.SemaphoreType.DMA((8,)), pltpu.SemaphoreType.DMA((4,)),
        ],
    )
    return (
        query_full[None],
        *(a[None] for a in new[0:3]),
        output_full[None],
        *(a[None] for a in new[3:6]),
        table_full,
        *new[6:9],
    )


def solution(mesh):
    return jax.shard_map(
        per_device,
        mesh=mesh,
        in_specs=(
            P("section", "dp", None, "tensor"),
            P("section", "dp", "tensor"),
            P("section", "dp", "tensor"),
            P("section", "dp", "tensor"),
            P("section", "dp", "tensor", None),
            P("section", "tensor", "dp"),
            P("section", "tensor", "dp"),
            P("section", "tensor", "dp"),
            P("section", "dp", "tensor", None),
            P("tensor", ("section", "dp")),
            P("tensor", ("section", "dp")),
            P("tensor", ("section", "dp")),
        ),
        out_specs=(
            P("section", None, "tensor"),
            P("section", "dp", "tensor"),
            P("section", "dp", "tensor"),
            P("section", "dp", "tensor"),
            P("section", "tensor", None),
            P("section", "tensor", "dp"),
            P("section", "tensor", "dp"),
            P("section", "tensor", "dp"),
            P("tensor", None),
            P("tensor", ("section", "dp")),
            P("tensor", ("section", "dp")),
            P("tensor", ("section", "dp")),
        ),
        check_vma=False,
    )
```

time: 775 us -> 132 us (0.17)
  waiting for transfers between devices: 578 us -> 36 us
  blocking collectives: 112 us -> 0 us
  starting transfers between devices: 0.25 us -> 74.4 us
  local copies, waits for them, and re-layouts: 51.1 us -> 0.81 us
  between operations: 18.3 us -> 1.19 us
  Pallas kernels: 0 us -> 10.9 us
    unnamed x10 -> x0, waiting for transfers between devices: 477 us -> none
    all_gather x2 -> x0, waiting for transfers between devices: 101 us -> none  [the longest x1 76.8 us: per_device(): lax.all_gather(table_half, ('section', 'dp'), axis=1, tiled=True)]
    psum x1 -> x0, blocking collectives: 78 us -> none  [per_device(): lax.psum((attn_square, table_square), ('section', 'dp', 'tensor'))]
    ppermute x0 -> x37, starting transfers between devices: none -> 74.4 us  [the longest x25 56.9 us: dp_send(): return lax.ppermute(value, 'dp', perm)]
    ppermute x0 -> x37, waiting for transfers between devices: none -> 36 us  [the longest x25 23.1 us: dp_send(): return lax.ppermute(value, 'dp', perm)]
    all_gather x1 -> x0, blocking collectives: 33.9 us -> none  [per_device(): query_full = lax.all_gather(query_half, 'dp', axis=0, tiled=True)]
    unnamed x35 -> x26, local copies, waits for them, and re-layouts: 28.8 us -> 0.76 us
    select_n x2 -> x0, local copies, waits for them, and re-layouts: 16.8 us -> none  [per_device(): jnp.where(at_ends, table_grads[0, 0].astype(jnp.float32), jnp.float32(0.0))]
  transfers between devices with their start and end apart: 6 -> 37, of which waited for: 6 -> 23; matrix products, arithmetic and copies ran while one was open for 3% -> 5% of each run, Pallas kernels for 0% -> 3%
where the time goes in v2:
time: 132 us
  starting transfers between devices  74.4 us (56%)
  waiting for transfers between devices  36 us (27%)
  Pallas kernels  10.9 us (8%)
  other arithmetic  8.29 us (6%)
    ppermute x25, starting transfers between devices, dp_send(): return lax.ppermute(value, 'dp', perm)  56.9 us
    ppermute x25, waiting for transfers between devices, dp_send(): return lax.ppermute(value, 'dp', perm)  23.1 us
    pallas_call x5, Pallas kernels, call(): pl.pallas_call(kernel, out_shape=list(outs) if isinstance(outs, (list, tu...  10.9 us
    ppermute x3, starting transfers between devices, section_send(): return lax.ppermute(quarter(i).astype(F16), 'section', perm)  8.55 us
    ppermute x3, waiting for transfers between devices, per_device(): lax.ppermute(t_all, 'section', ring_perm(k))  5.73 us
    ppermute x3, starting transfers between devices, per_device(): lax.ppermute(squares, 'section', ring_perm(k))  4.1 us
    ppermute x3, waiting for transfers between devices, per_device(): lax.ppermute(squares, 'section', ring_perm(k))  3.66 us
    ppermute x3, waiting for transfers between devices, per_device(): lax.ppermute(squares, 'tensor', ring_perm(k))  3.5 us
  transfers between devices with their start and end apart: 37, of which 23 were waited for; matrix products, arithmetic and copies ran while one was open for 5% of the time, Pallas kernels for 3%

profile of v2, /device:TPU:1, one launch (start us, length us, event | category | flops | bytes accessed | tf_op | source)
XLA Modules:
  0.0 131.6 jit_solution(11993132514131164393)
XLA Ops:
  0.7 3.9 %shard_map.211 = (bf16[2,4,720,128]{3,2,1,0:T(8,128)(2,1)}, bf16[2,4,720,128]{3,2,1,0:T(8,128)(2,1)}, f32[8,128]{1,0:T(8,128)}) custom-call(bf16[128,3968]{1,0:T(8,128)(2,1)} %bitcast.186, bf16[64,14848]{1,0:T(8,128)(2,1)} %bitcast.185), custom_call_target="tpu_custom_call" | custom-call | bytes 9000000 | tf_op jit(solution)/shard_map/pallas_call | solution.py:47
  4.5 3.3 %collective-permute-start = (bf16[2,4,720,128]{3,2,1,0:T(8,128)(2,1)}, bf16[2,4,720,128]{3,2,1,0:T(8,128)(2,1)S(1)}, u32[]{:S(2)}, u32[]{:S(2)}) collective-permute-start(bf16[2,4,720,128]{3,2,1,0:T(8,128)(2,1)} %get-tuple-element.41), channel_id=1, source_target_pairs={{0,4},{4,0},{8,12},{12,8},{16,20},{20,16},{24,28},{28,24},{32,36},... | collective-permute-start | bytes 4423688 | tf_op jit(solution)/shard_map/ppermute | solution.py:367
  8.6 1.3 shard_map.212
  9.8 1.1 collective-permute-done
  11.0 1.3 fusion.2
  12.7 1.3 collective-permute-start.3
  14.0 1.0 collective-permute-done.5
  15.2 3.8 %collective-permute-start.8 = (f16[8,128,128]{2,1,0:T(8,128)(2,1)S(1)}, f16[8,128,128]{2,1,0:T(8,128)(2,1)S(1)}, u32[]{:S(2)}, u32[]{:S(2)}) collective-permute-start(f16[8,128,128]{2,1,0:T(8,128)(2,1)S(1)} %get-tuple-element.76), channel_id=1, source_target_pairs={{0,128},{192,64},{1,129},{193,65},{2,130},{194,66},{3,131},{195,67... | collective-permute-start | bytes 786440 | tf_op jit(solution)/shard_map/ppermute | solution.py:405
  19.1 2.7 %collective-permute-start.7 = (f16[8,128,128]{2,1,0:T(8,128)(2,1)S(1)}, f16[8,128,128]{2,1,0:T(8,128)(2,1)S(1)}, u32[]{:S(2)}, u32[]{:S(2)}) collective-permute-start(f16[8,128,128]{2,1,0:T(8,128)(2,1)S(1)} %get-tuple-element.77), channel_id=1, source_target_pairs={{0,192},{192,0},{1,193},{193,1},{2,194},{194,2},{3,195},{195,3},{4... | collective-permute-start | bytes 786440 | tf_op jit(solution)/shard_map/ppermute | solution.py:405
  21.8 2.0 %collective-permute-start.6 = (f16[8,128,128]{2,1,0:T(8,128)(2,1)S(1)}, f16[8,128,128]{2,1,0:T(8,128)(2,1)}, u32[]{:S(2)}, u32[]{:S(2)}) collective-permute-start(f16[8,128,128]{2,1,0:T(8,128)(2,1)S(1)} %get-tuple-element.78), channel_id=1, source_target_pairs={{0,64},{192,128},{1,65},{193,129},{2,66},{194,130},{3,67},{195,131... | collective-permute-start | bytes 786440 | tf_op jit(solution)/shard_map/ppermute | solution.py:405
  23.8 1.0 convert_element_type.202
  24.9 1.0 convert_element_type.209
  25.9 1.3 %fusion.4 = (f16[720,128]{1,0:T(8,128)(2,1)S(1)}, f16[720,128]{1,0:T(8,128)(2,1)S(1)}) fusion(f32[2,720,128]{2,1,0:T(8,128)S(1)} %convert_element_type.209, bf16[2,4,720,128]{3,2,1,0:T(8,128)(2,1)} %copy-done.12, bf16[2,4,720,128]{3,2,1,0:T(8,128)(2,1)} %get-tuple-element.40, f32[2,720,128]{2,1,0:T(8,128)S(1)} %convert_element_type.202), kind=kLoop, calls=%fused_computation.17 | loop fusion | flops 921600 | bytes 1843200 | tf_op jit(solution)/shard_map/convert_element_type | solution.py:395
  27.8 1.8 %collective-permute-start.2 = (f16[720,128]{1,0:T(8,128)(2,1)S(1)}, f16[720,128]{1,0:T(8,128)(2,1)S(1)}, u32[]{:S(2)}, u32[]{:S(2)}) collective-permute-start(f16[720,128]{1,0:T(8,128)(2,1)S(1)} %get-tuple-element.73), channel_id=1, source_target_pairs={{0,24},{4,28},{8,16},{12,20},{16,8},{20,12},{24,0},{28,4},{32,56},... | collective-permute-start | bytes 552968 | tf_op jit(solution)/shard_map/ppermute | solution.py:367
  29.6 1.1 fusion
  31.5 2.7 %collective-permute-start.10 = (f16[2,128,128]{2,1,0:T(8,128)(2,1)S(1)}, f16[2,128,128]{2,1,0:T(8,128)(2,1)S(1)}, u32[]{:S(2)}, u32[]{:S(2)}) collective-permute-start(f16[2,128,128]{2,1,0:T(8,128)(2,1)S(1)} %get-tuple-element.82), channel_id=1, source_target_pairs={{0,16},{4,20},{8,24},{12,28},{16,0},{20,4},{24,8},{28,12},{32,48},... | collective-permute-start | bytes 196616 | tf_op jit(solution)/shard_map/ppermute | solution.py:367
  34.8 1.4 %broadcast_select_fusion = (f32[720,128]{1,0:T(8,128)S(1)}, f16[720,128]{1,0:T(8,128)(2,1)S(1)}) fusion(pred[]{:T(512)S(6)} %eq.11, f16[720,128]{1,0:T(8,128)(2,1)S(1)} %collective-permute-done.2, f32[2,720,128]{2,1,0:T(8,128)S(1)} %convert_element_type.202, bf16[2,4,720,128]{3,2,1,0:T(8,128)(2,1)} %copy-done.12, ...), kind=kLoop, calls=%fused_computation.37 | loop fusion | flops 1382400 | bytes 2396161 | tf_op jit(solution)/shard_map/jit(_where)/select_n | solution.py:426
  36.6 2.4 %collective-permute-done.11 = f16[2,128,128]{2,1,0:T(8,128)(2,1)S(1)} collective-permute-done((f16[2,128,128]{2,1,0:T(8,128)(2,1)S(1)}, f16[2,128,128]{2,1,0:T(8,128)(2,1)S(1)}, u32[]{:S(2)}, u32[]{:S(2)}) %collective-permute-start.11) | collective-permute-done | bytes 65568 | tf_op jit(solution)/shard_map/ppermute | solution.py:367
  39.1 7.0 %collective-permute-start.12 = (f16[848,128]{1,0:T(8,128)(2,1)S(1)}, f16[848,128]{1,0:T(8,128)(2,1)S(1)}, u32[]{:S(2)}, u32[]{:S(2)}) collective-permute-start(f16[848,128]{1,0:T(8,128)(2,1)S(1)} %pad_maximum_fusion.5), channel_id=1, source_target_pairs={{0,32},{4,36},{8,40},{12,44},{16,48},{20,52},{24,56},{28,60},{32,0... | collective-permute-start | bytes 651272 | tf_op jit(solution)/shard_map/ppermute | solution.py:367
  46.1 3.4 %collective-permute-done.12 = f16[848,128]{1,0:T(8,128)(2,1)S(1)} collective-permute-done((f16[848,128]{1,0:T(8,128)(2,1)S(1)}, f16[848,128]{1,0:T(8,128)(2,1)S(1)}, u32[]{:S(2)}, u32[]{:S(2)}) %collective-permute-start.12) | collective-permute-done | bytes 217120 | tf_op jit(solution)/shard_map/ppermute | solution.py:367
  49.6 6.6 %collective-permute-start.13 = (f32[8,128]{1,0:T(8,128)S(1)}, f32[8,128]{1,0:T(8,128)S(1)}, u32[]{:S(2)}, u32[]{:S(2)}) collective-permute-start(f32[8,128]{1,0:T(8,128)S(1)} %get-tuple-element.68), channel_id=1, source_target_pairs={{0,4},{4,0},{8,12},{12,8},{16,20},{20,16},{24,28},{28,24},{32,36},... | collective-permute-start | bytes 12296 | tf_op jit(solution)/shard_map/ppermute | solution.py:367
  57.4 2.9 %collective-permute-start.14 = (f32[8,128]{1,0:T(8,128)S(1)}, f32[8,128]{1,0:T(8,128)S(1)}, u32[]{:S(2)}, u32[]{:S(2)}) collective-permute-start(f32[8,128]{1,0:T(8,128)S(1)} %add.216), channel_id=1, source_target_pairs={{0,8},{4,12},{8,0},{12,4},{16,24},{20,28},{24,16},{28,20},{32,40},... | collective-permute-start | bytes 12296 | tf_op jit(solution)/shard_map/ppermute | solution.py:367
  61.6 2.2 %collective-permute-start.19 = (f32[8,128]{1,0:T(8,128)S(1)}, f32[8,128]{1,0:T(8,128)S(1)}, u32[]{:S(2)}, u32[]{:S(2)}) collective-permute-start(f32[8,128]{1,0:T(8,128)S(1)} %add_add_fusion.2), channel_id=1, source_target_pairs={{0,192},{64,0},{128,64},{192,128},{1,193},{65,1},{129,65},{193,129... | collective-permute-start | bytes 12296 | tf_op jit(solution)/shard_map/ppermute | solution.py:432
  63.8 1.9 %collective-permute-start.18 = (f32[8,128]{1,0:T(8,128)S(1)}, f32[8,128]{1,0:T(8,128)S(1)}, u32[]{:S(2)}, u32[]{:S(2)}) collective-permute-start(f32[8,128]{1,0:T(8,128)S(1)} %add_add_fusion.2), channel_id=1, source_target_pairs={{0,128},{64,192},{128,0},{192,64},{1,129},{65,193},{129,1},{193,65... | collective-permute-start | bytes 12296 | tf_op jit(solution)/shard_map/ppermute | solution.py:432
  65.7 2.0 %collective-permute-done.18 = f32[8,128]{1,0:T(8,128)S(1)} collective-permute-done((f32[8,128]{1,0:T(8,128)S(1)}, f32[8,128]{1,0:T(8,128)S(1)}, u32[]{:S(2)}, u32[]{:S(2)}) %collective-permute-start.18) | collective-permute-done | bytes 4128 | tf_op jit(solution)/shard_map/ppermute | solution.py:432
  67.7 1.6 %collective-permute-done.17 = f32[8,128]{1,0:T(8,128)S(1)} collective-permute-done((f32[8,128]{1,0:T(8,128)S(1)}, f32[8,128]{1,0:T(8,128)S(1)}, u32[]{:S(2)}, u32[]{:S(2)}) %collective-permute-start.17) | collective-permute-done | bytes 4128 | tf_op jit(solution)/shard_map/ppermute | solution.py:432
  69.4 6.1 %collective-permute-start.20 = (f32[8,128]{1,0:T(8,128)S(1)}, f32[8,128]{1,0:T(8,128)S(1)}, u32[]{:S(2)}, u32[]{:S(2)}) collective-permute-start(f32[8,128]{1,0:T(8,128)S(1)} %add_add_fusion.1), channel_id=1, source_target_pairs={{0,32},{4,36},{8,40},{12,44},{16,48},{20,52},{24,56},{28,60},{32,0... | collective-permute-start | bytes 12296 | tf_op jit(solution)/shard_map/ppermute | solution.py:367
  75.4 1.0 collective-permute-done.20
  76.4 1.1 collective-permute-start.23
  77.5 1.6 %collective-permute-start.22 = (f32[8,128]{1,0:T(8,128)S(1)}, f32[8,128]{1,0:T(8,128)S(1)}, u32[]{:S(2)}, u32[]{:S(2)}) collective-permute-start(f32[8,128]{1,0:T(8,128)S(1)} %add.223), channel_id=1, source_target_pairs={{0,2},{1,3},{2,0},{3,1},{4,6},{5,7},{6,4},{7,5},{8,10},{9,11},{10,... | collective-permute-start | bytes 12296 | tf_op jit(solution)/shard_map/ppermute | solution.py:434
  79.8 1.0 collective-permute-done.22
  80.9 2.5 %collective-permute-done.21 = f32[8,128]{1,0:T(8,128)S(1)} collective-permute-done((f32[8,128]{1,0:T(8,128)S(1)}, f32[8,128]{1,0:T(8,128)S(1)}, u32[]{:S(2)}, u32[]{:S(2)}) %collective-permute-start.21) | collective-permute-done | bytes 4128 | tf_op jit(solution)/shard_map/ppermute | solution.py:434
  83.4 1.4 %shard_map.213 = (bf16[848,128]{1,0:T(8,128)(2,1)S(1)}, f32[8,3968]{1,0:T(8,128)}, f32[8,3968]{1,0:T(8,128)}, f32[8,3968]{1,0:T(8,128)}, f32[64,928]{1,0:T(8,128...) custom-call(f32[8,128]{1,0:T(8,128)S(1)} %add_add_fusion.n_ref, ...), custom_call_target="tpu_custom_call" | custom-call | bytes 6000000 | tf_op jit(solution)/shard_map/pallas_call | solution.py:47
  84.8 5.0 %collective-permute-start.24 = (bf16[848,128]{1,0:T(8,128)(2,1)S(1)}, bf16[848,128]{1,0:T(8,128)(2,1)S(1)}, u32[]{:S(2)}, u32[]{:S(2)}) collective-permute-start(bf16[848,128]{1,0:T(8,128)(2,1)S(1)} %get-tuple-element.48), channel_id=1, source_target_pairs={{0,32},{4,36},{8,40},{12,44},{16,48},{20,52},{24,56},{28,60},{32,0... | collective-permute-start | bytes 651272 | tf_op jit(solution)/shard_map/ppermute | solution.py:367
  89.9 6.0 %collective-permute-done.24 = bf16[848,128]{1,0:T(8,128)(2,1)S(1)} collective-permute-done((bf16[848,128]{1,0:T(8,128)(2,1)S(1)}, bf16[848,128]{1,0:T(8,128)(2,1)S(1)}, u32[]{:S(2)}, u32[]{:S(2)}) %collective-permute-start.24) | collective-permute-done | bytes 217120 | tf_op jit(solution)/shard_map/ppermute | solution.py:367
  96.7 1.9 %collective-permute-start.25 = (bf16[2,128,128]{2,1,0:T(8,128)(2,1)S(1)}, bf16[2,128,128]{2,1,0:T(8,128)(2,1)S(1)}, u32[]{:S(2)}, u32[]{:S(2)}) collective-permute-start(bf16[2,128,128]{2,1,0:T(8,128)(2,1)S(1)} %pad_maximum_fusion.8), channel_id=1, source_target_pairs={{0,8},{4,12},{8,0},{12,4},{16,24},{20,28},{24,16},{28,20},{32,40},... | collective-permute-start | bytes 196616 | tf_op jit(solution)/shard_map/ppermute | solution.py:367
  98.6 0.9 collective-permute-start.27
  99.6 1.9 %collective-permute-start.32 = (bf16[2,352,128]{2,1,0:T(8,128)(2,1)S(1)}, bf16[2,352,128]{2,1,0:T(8,128)(2,1)S(1)}, u32[]{:S(2)}, u32[]{:S(2)}) collective-permute-start(bf16[2,352,128]{2,1,0:T(8,128)(2,1)S(1)} %pad_maximum_fusion.7), channel_id=1, source_target_pairs={{0,24},{4,28},{8,16},{12,20},{16,8},{20,12},{24,0},{28,4},{32,56},... | collective-permute-start | bytes 540680 | tf_op jit(solution)/shard_map/ppermute | solution.py:367
  101.5 1.5 %collective-permute-done.27 = bf16[2,128,128]{2,1,0:T(8,128)(2,1)S(1)} collective-permute-done((bf16[2,128,128]{2,1,0:T(8,128)(2,1)S(1)}, bf16[2,128,128]{2,1,0:T(8,128)(2,1)S(1)}, u32[]{:S(2)}, u32[]{:S(2)}) %collective-permute-start.27) | collective-permute-done | bytes 65568 | tf_op jit(solution)/shard_map/ppermute | solution.py:367
  103.5 1.1 collective-permute-start.28
  107.3 1.3 collective-permute-done.30
  108.6 1.4 %collective-permute-done.29 = bf16[4,2,128,128]{3,2,1,0:T(8,128)(2,1)S(1)} collective-permute-done((bf16[4,2,128,128]{3,2,1,0:T(8,128)(2,1)S(1)}, bf16[4,2,128,128]{3,2,1,0:T(8,128)(2,1)S(1)}, u32[]{:S(2)}, u32[]{:S(2)}) %collective-permute-start.29) | collective-permute-done | bytes 262176 | tf_op jit(solution)/shard_map/ppermute | solution.py:457
  110.0 3.0 %collective-permute-done.28 = bf16[4,2,128,128]{3,2,1,0:T(8,128)(2,1)S(1)} collective-permute-done((bf16[4,2,128,128]{3,2,1,0:T(8,128)(2,1)S(1)}, bf16[4,2,128,128]{3,2,1,0:T(8,128)(2,1)S(1)}, u32[]{:S(2)}, u32[]{:S(2)}) %collective-permute-start.28) | collective-permute-done | bytes 262176 | tf_op jit(solution)/shard_map/ppermute | solution.py:457
  113.1 10.5 %collective-permute-start.31 = (bf16[4,4,2,128,128]{4,3,2,1,0:T(8,128)(2,1)S(1)}, bf16[4,4,2,128,128]{4,3,2,1,0:T(8,128)(2,1)S(1)}, u32[]{:S(2)}, u32[]{:S(2)}) collective-permute-start(bf16[4,4,2,128,128]{4,3,2,1,0:T(8,128)(2,1)S(1)} %pad_maximum_fusion.own_ref), channel_id=1, source_target_pairs={{0,4},{4,0},{8,12},{12,8},{16,20},{20,16},{24,28},{28,24},{32,36},... | collective-permute-start | bytes 3145736 | tf_op jit(solution)/shard_map/ppermute | solution.py:367
  123.9 2.0 %collective-permute-done.31.got_ref = bf16[4,4,2,128,128]{4,3,2,1,0:T(8,128)(2,1)S(1)} collective-permute-done((bf16[4,4,2,128,128]{4,3,2,1,0:T(8,128)(2,1)S(1)}, bf16[4,4,2,128,128]{4,3,2,1,0:T(8,128)(2,1)S(1)}, u32[]{:S(2)}, u32[]{:S(2)}) %collective-permute-start.31) | collective-permute-done | bytes 1048608 | tf_op jit(solution)/shard_map/ppermute | solution.py:367
  126.3 2.1 %shard_map.214 = (bf16[64,14848]{1,0:T(8,128)(2,1)}, f32[8,128]{1,0:T(8,128)S(1)}) custom-call(bf16[4,4,2,128,128]{4,3,2,1,0:T(8,128)(2,1)S(1)} %pad_maximum_fusion.own_ref, bf16[4,4,2,128,128]{4,3,2,1,0:T(8,128)(2,1)S(1)} %collective-permute-done.31.got_ref), custom_call_target="tpu_custom_call" | custom-call | bytes 6000000 | tf_op jit(solution)/shard_map/pallas_call | solution.py:47
  128.3 0.8 collective-permute-done.36.got_ref
  129.2 2.3 %shard_map.215 = (bf16[128,3968]{1,0:T(8,128)(2,1)}, bf16[64,14848]{1,0:T(8,128)(2,1)}) custom-call(bf16[2,4,720,128]{3,2,1,0:T(8,128)(2,1)S(1)} %maximum_maximum_fusion.own_ref, bf16[2,4,720,128]{3,2,1,0:T(8,128)(2,1)S(1)} %collective-permute-done.36.got_ref, f32[8,128]{1,0:T(8,128)S(1)} %get-tuple-element.55._), custom_call_target="tpu_custom_call" | custom-call | bytes 9000000 | tf_op jit(solution)/shard_map/pallas_call | solution.py:47
  (88 shorter events, 11.9 us)
Async XLA Ops:
  0.6 7.2 %copy-start = (bf16[1,1,64,14848]{3,2,1,0:T(8,128)(2,1)S(1)}, bf16[1,1,64,14848]{3,2,1,0:T(8,128)(2,1)}, u32[]{:S(2)}) copy-start(bf16[1,1,64,14848]{3,2,1,0:T(8,128)(2,1)} %param.20) | copy-start | bytes 5701636
  4.5 6.5 %collective-permute-start = (bf16[2,4,720,128]{3,2,1,0:T(8,128)(2,1)}, bf16[2,4,720,128]{3,2,1,0:T(8,128)(2,1)S(1)}, u32[]{:S(2)}, u32[]{:S(2)}) collective-permute-start(bf16[2,4,720,128]{3,2,1,0:T(8,128)(2,1)} %get-tuple-element.41), channel_id=1, source_target_pairs={{0,4},{4,0},{8,12},{12,8},{16,20},{20,16},{24,28},{28,24},{32,36},... | collective-permute-start | bytes 4423688 | tf_op jit(solution)/shard_map/ppermute | solution.py:367
  8.6 2.4 %copy-start.11 = (bf16[2,4,720,128]{3,2,1,0:T(8,128)(2,1)S(1)}, bf16[2,4,720,128]{3,2,1,0:T(8,128)(2,1)}, u32[]{:S(2)}) copy-start(bf16[2,4,720,128]{3,2,1,0:T(8,128)(2,1)} %get-tuple-element.40) | copy-start | bytes 4423684
  12.3 2.7 %collective-permute-start.5 = (bf16[4,8,128,128]{3,2,1,0:T(8,128)(2,1)S(1)}, bf16[4,8,128,128]{3,2,1,0:T(8,128)(2,1)S(1)}, u32[]{:S(2)}, u32[]{:S(2)}) collective-permute-start(bf16[4,8,128,128]{3,2,1,0:T(8,128)(2,1)S(1)} %get-tuple-element.47), channel_id=1, source_target_pairs={{0,4},{4,0},{8,12},{12,8},{16,20},{20,16},{24,28},{28,24},{32,36},... | collective-permute-start | bytes 3145736 | tf_op jit(solution)/shard_map/ppermute | solution.py:367
  12.7 11.1 %collective-permute-start.1 = (f16[2,720,128]{2,1,0:T(8,128)(2,1)}, f16[2,720,128]{2,1,0:T(8,128)(2,1)}, u32[]{:S(2)}, u32[]{:S(2)}) collective-permute-start(f16[2,720,128]{2,1,0:T(8,128)(2,1)} %get-tuple-element.44), channel_id=1, source_target_pairs={{0,8},{4,12},{8,0},{12,4},{16,24},{20,28},{24,16},{28,20},{32,40},... | collective-permute-start | bytes 1105928 | tf_op jit(solution)/shard_map/ppermute | solution.py:367
  12.7 12.2 %collective-permute-start.3 = (f16[2,720,128]{2,1,0:T(8,128)(2,1)}, f16[2,720,128]{2,1,0:T(8,128)(2,1)}, u32[]{:S(2)}, u32[]{:S(2)}) collective-permute-start(f16[2,720,128]{2,1,0:T(8,128)(2,1)} %get-tuple-element.45), channel_id=1, source_target_pairs={{0,24},{4,28},{8,16},{12,20},{16,8},{20,12},{24,0},{28,4},{32,56},... | collective-permute-start | bytes 1105928 | tf_op jit(solution)/shard_map/ppermute | solution.py:367
  15.2 14.4 %collective-permute-start.8 = (f16[8,128,128]{2,1,0:T(8,128)(2,1)S(1)}, f16[8,128,128]{2,1,0:T(8,128)(2,1)S(1)}, u32[]{:S(2)}, u32[]{:S(2)}) collective-permute-start(f16[8,128,128]{2,1,0:T(8,128)(2,1)S(1)} %get-tuple-element.76), channel_id=1, source_target_pairs={{0,128},{192,64},{1,129},{193,65},{2,130},{194,66},{3,131},{195,67... | collective-permute-start | bytes 786440 | tf_op jit(solution)/shard_map/ppermute | solution.py:405
  19.1 10.5 %collective-permute-start.7 = (f16[8,128,128]{2,1,0:T(8,128)(2,1)S(1)}, f16[8,128,128]{2,1,0:T(8,128)(2,1)S(1)}, u32[]{:S(2)}, u32[]{:S(2)}) collective-permute-start(f16[8,128,128]{2,1,0:T(8,128)(2,1)S(1)} %get-tuple-element.77), channel_id=1, source_target_pairs={{0,192},{192,0},{1,193},{193,1},{2,194},{194,2},{3,195},{195,3},{4... | collective-permute-start | bytes 786440 | tf_op jit(solution)/shard_map/ppermute | solution.py:405
  21.8 7.8 %collective-permute-start.6 = (f16[8,128,128]{2,1,0:T(8,128)(2,1)S(1)}, f16[8,128,128]{2,1,0:T(8,128)(2,1)}, u32[]{:S(2)}, u32[]{:S(2)}) collective-permute-start(f16[8,128,128]{2,1,0:T(8,128)(2,1)S(1)} %get-tuple-element.78), channel_id=1, source_target_pairs={{0,64},{192,128},{1,65},{193,129},{2,66},{194,130},{3,67},{195,131... | collective-permute-start | bytes 786440 | tf_op jit(solution)/shard_map/ppermute | solution.py:405
  27.3 7.5 %collective-permute-start.4 = (f16[720,128]{1,0:T(8,128)(2,1)S(1)}, f16[720,128]{1,0:T(8,128)(2,1)S(1)}, u32[]{:S(2)}, u32[]{:S(2)}) collective-permute-start(f16[720,128]{1,0:T(8,128)(2,1)S(1)} %get-tuple-element.72), channel_id=1, source_target_pairs={{0,8},{4,12},{8,0},{12,4},{16,24},{20,28},{24,16},{28,20},{32,40},... | collective-permute-start | bytes 552968 | tf_op jit(solution)/shard_map/ppermute | solution.py:367
  27.8 7.0 %collective-permute-start.2 = (f16[720,128]{1,0:T(8,128)(2,1)S(1)}, f16[720,128]{1,0:T(8,128)(2,1)S(1)}, u32[]{:S(2)}, u32[]{:S(2)}) collective-permute-start(f16[720,128]{1,0:T(8,128)(2,1)S(1)} %get-tuple-element.73), channel_id=1, source_target_pairs={{0,24},{4,28},{8,16},{12,20},{16,8},{20,12},{24,0},{28,4},{32,56},... | collective-permute-start | bytes 552968 | tf_op jit(solution)/shard_map/ppermute | solution.py:367
  30.8 5.5 %collective-permute-start.9 = (f16[2,128,128]{2,1,0:T(8,128)(2,1)S(1)}, f16[2,128,128]{2,1,0:T(8,128)(2,1)S(1)}, u32[]{:S(2)}, u32[]{:S(2)}) collective-permute-start(f16[2,128,128]{2,1,0:T(8,128)(2,1)S(1)} %get-tuple-element.81), channel_id=1, source_target_pairs={{0,8},{4,12},{8,0},{12,4},{16,24},{20,28},{24,16},{28,20},{32,40},... | collective-permute-start | bytes 196616 | tf_op jit(solution)/shard_map/ppermute | solution.py:367
  31.5 5.1 %collective-permute-start.10 = (f16[2,128,128]{2,1,0:T(8,128)(2,1)S(1)}, f16[2,128,128]{2,1,0:T(8,128)(2,1)S(1)}, u32[]{:S(2)}, u32[]{:S(2)}) collective-permute-start(f16[2,128,128]{2,1,0:T(8,128)(2,1)S(1)} %get-tuple-element.82), channel_id=1, source_target_pairs={{0,16},{4,20},{8,24},{12,28},{16,0},{20,4},{24,8},{28,12},{32,48},... | collective-permute-start | bytes 196616 | tf_op jit(solution)/shard_map/ppermute | solution.py:367
  34.2 4.8 %collective-permute-start.11 = (f16[2,128,128]{2,1,0:T(8,128)(2,1)S(1)}, f16[2,128,128]{2,1,0:T(8,128)(2,1)S(1)}, u32[]{:S(2)}, u32[]{:S(2)}) collective-permute-start(f16[2,128,128]{2,1,0:T(8,128)(2,1)S(1)} %get-tuple-element.83), channel_id=1, source_target_pairs={{0,24},{4,28},{8,16},{12,20},{16,8},{20,12},{24,0},{28,4},{32,56},... | collective-permute-start | bytes 196616 | tf_op jit(solution)/shard_map/ppermute | solution.py:367
  36.2 47.2 %copy-start.1 = (f32[1,64,928]{2,1,0:T(8,128)S(1)}, f32[1,64,928]{2,1,0:T(8,128)}, u32[]{:S(2)}) copy-start(f32[1,64,928]{2,1,0:T(8,128)} %param.17) | copy-start | bytes 712708
  36.2 47.1 %copy-start.2 = (f32[1,64,928]{2,1,0:T(8,128)S(1)}, f32[1,64,928]{2,1,0:T(8,128)}, u32[]{:S(2)}) copy-start(f32[1,64,928]{2,1,0:T(8,128)} %param.18) | copy-start | bytes 712708
  36.2 47.1 %copy-start.3 = (f32[1,64,928]{2,1,0:T(8,128)S(1)}, f32[1,64,928]{2,1,0:T(8,128)}, u32[]{:S(2)}) copy-start(f32[1,64,928]{2,1,0:T(8,128)} %param.19) | copy-start | bytes 712708
  36.2 47.1 %copy-start.4 = (f32[1,8,3968]{2,1,0:T(8,128)S(1)}, f32[1,8,3968]{2,1,0:T(8,128)}, u32[]{:S(2)}) copy-start(f32[1,8,3968]{2,1,0:T(8,128)} %param.13) | copy-start | bytes 380932
  36.2 47.1 %copy-start.5 = (f32[1,8,3968]{2,1,0:T(8,128)S(1)}, f32[1,8,3968]{2,1,0:T(8,128)}, u32[]{:S(2)}) copy-start(f32[1,8,3968]{2,1,0:T(8,128)} %param.14) | copy-start | bytes 380932
  36.2 47.1 %copy-start.6 = (f32[1,8,3968]{2,1,0:T(8,128)S(1)}, f32[1,8,3968]{2,1,0:T(8,128)}, u32[]{:S(2)}) copy-start(f32[1,8,3968]{2,1,0:T(8,128)} %param.15) | copy-start | bytes 380932
  36.2 47.1 %copy-start.7 = (f32[64,232]{1,0:T(8,128)S(1)}, f32[64,232]{1,0:T(8,128)}, u32[]{:S(2)}) copy-start(f32[64,232]{1,0:T(8,128)} %tw_ref.1) | copy-start | bytes 178180
  36.3 47.1 %copy-start.8 = (f32[64,232]{1,0:T(8,128)S(1)}, f32[64,232]{1,0:T(8,128)}, u32[]{:S(2)}) copy-start(f32[64,232]{1,0:T(8,128)} %tm_ref.1) | copy-start | bytes 178180
  36.3 47.1 %copy-start.9 = (f32[64,232]{1,0:T(8,128)S(1)}, f32[64,232]{1,0:T(8,128)}, u32[]{:S(2)}) copy-start(f32[64,232]{1,0:T(8,128)} %tv_ref.1) | copy-start | bytes 178180
  39.1 10.4 %collective-permute-start.12 = (f16[848,128]{1,0:T(8,128)(2,1)S(1)}, f16[848,128]{1,0:T(8,128)(2,1)S(1)}, u32[]{:S(2)}, u32[]{:S(2)}) collective-permute-start(f16[848,128]{1,0:T(8,128)(2,1)S(1)} %pad_maximum_fusion.5), channel_id=1, source_target_pairs={{0,32},{4,36},{8,40},{12,44},{16,48},{20,52},{24,56},{28,60},{32,0... | collective-permute-start | bytes 651272 | tf_op jit(solution)/shard_map/ppermute | solution.py:367
  49.6 7.4 %collective-permute-start.13 = (f32[8,128]{1,0:T(8,128)S(1)}, f32[8,128]{1,0:T(8,128)S(1)}, u32[]{:S(2)}, u32[]{:S(2)}) collective-permute-start(f32[8,128]{1,0:T(8,128)S(1)} %get-tuple-element.68), channel_id=1, source_target_pairs={{0,4},{4,0},{8,12},{12,8},{16,20},{20,16},{24,28},{28,24},{32,36},... | collective-permute-start | bytes 12296 | tf_op jit(solution)/shard_map/ppermute | solution.py:367
  57.0 3.7 %collective-permute-start.16 = (f32[8,128]{1,0:T(8,128)S(1)}, f32[8,128]{1,0:T(8,128)S(1)}, u32[]{:S(2)}, u32[]{:S(2)}) collective-permute-start(f32[8,128]{1,0:T(8,128)S(1)} %add.216), channel_id=1, source_target_pairs={{0,24},{4,28},{8,16},{12,20},{16,8},{20,12},{24,0},{28,4},{32,56},... | collective-permute-start | bytes 12296 | tf_op jit(solution)/shard_map/ppermute | solution.py:367
  57.1 4.0 %collective-permute-start.15 = (f32[8,128]{1,0:T(8,128)S(1)}, f32[8,128]{1,0:T(8,128)S(1)}, u32[]{:S(2)}, u32[]{:S(2)}) collective-permute-start(f32[8,128]{1,0:T(8,128)S(1)} %add.216), channel_id=1, source_target_pairs={{0,16},{4,20},{8,24},{12,28},{16,0},{20,4},{24,8},{28,12},{32,48},... | collective-permute-start | bytes 12296 | tf_op jit(solution)/shard_map/ppermute | solution.py:367
  57.4 4.2 %collective-permute-start.14 = (f32[8,128]{1,0:T(8,128)S(1)}, f32[8,128]{1,0:T(8,128)S(1)}, u32[]{:S(2)}, u32[]{:S(2)}) collective-permute-start(f32[8,128]{1,0:T(8,128)S(1)} %add.216), channel_id=1, source_target_pairs={{0,8},{4,12},{8,0},{12,4},{16,24},{20,28},{24,16},{28,20},{32,40},... | collective-permute-start | bytes 12296 | tf_op jit(solution)/shard_map/ppermute | solution.py:367
  61.6 4.1 %collective-permute-start.19 = (f32[8,128]{1,0:T(8,128)S(1)}, f32[8,128]{1,0:T(8,128)S(1)}, u32[]{:S(2)}, u32[]{:S(2)}) collective-permute-start(f32[8,128]{1,0:T(8,128)S(1)} %add_add_fusion.2), channel_id=1, source_target_pairs={{0,192},{64,0},{128,64},{192,128},{1,193},{65,1},{129,65},{193,129... | collective-permute-start | bytes 12296 | tf_op jit(solution)/shard_map/ppermute | solution.py:432
  63.8 4.0 %collective-permute-start.18 = (f32[8,128]{1,0:T(8,128)S(1)}, f32[8,128]{1,0:T(8,128)S(1)}, u32[]{:S(2)}, u32[]{:S(2)}) collective-permute-start(f32[8,128]{1,0:T(8,128)S(1)} %add_add_fusion.2), channel_id=1, source_target_pairs={{0,128},{64,192},{128,0},{192,64},{1,129},{65,193},{129,1},{193,65... | collective-permute-start | bytes 12296 | tf_op jit(solution)/shard_map/ppermute | solution.py:432
  65.7 3.7 %collective-permute-start.17 = (f32[8,128]{1,0:T(8,128)S(1)}, f32[8,128]{1,0:T(8,128)S(1)}, u32[]{:S(2)}, u32[]{:S(2)}) collective-permute-start(f32[8,128]{1,0:T(8,128)S(1)} %add_add_fusion.2), channel_id=1, source_target_pairs={{0,64},{64,128},{128,192},{192,0},{1,65},{65,129},{129,193},{193,1... | collective-permute-start | bytes 12296 | tf_op jit(solution)/shard_map/ppermute | solution.py:432
  69.4 7.1 %collective-permute-start.20 = (f32[8,128]{1,0:T(8,128)S(1)}, f32[8,128]{1,0:T(8,128)S(1)}, u32[]{:S(2)}, u32[]{:S(2)}) collective-permute-start(f32[8,128]{1,0:T(8,128)S(1)} %add_add_fusion.1), channel_id=1, source_target_pairs={{0,32},{4,36},{8,40},{12,44},{16,48},{20,52},{24,56},{28,60},{32,0... | collective-permute-start | bytes 12296 | tf_op jit(solution)/shard_map/ppermute | solution.py:367
  76.4 3.4 %collective-permute-start.23 = (f32[8,128]{1,0:T(8,128)S(1)}, f32[8,128]{1,0:T(8,128)S(1)}, u32[]{:S(2)}, u32[]{:S(2)}) collective-permute-start(f32[8,128]{1,0:T(8,128)S(1)} %add.223), channel_id=1, source_target_pairs={{0,3},{1,0},{2,1},{3,2},{4,7},{5,4},{6,5},{7,6},{8,11},{9,8},{10,9... | collective-permute-start | bytes 12296 | tf_op jit(solution)/shard_map/ppermute | solution.py:434
  77.5 3.4 %collective-permute-start.22 = (f32[8,128]{1,0:T(8,128)S(1)}, f32[8,128]{1,0:T(8,128)S(1)}, u32[]{:S(2)}, u32[]{:S(2)}) collective-permute-start(f32[8,128]{1,0:T(8,128)S(1)} %add.223), channel_id=1, source_target_pairs={{0,2},{1,3},{2,0},{3,1},{4,6},{5,7},{6,4},{7,5},{8,10},{9,11},{10,... | collective-permute-start | bytes 12296 | tf_op jit(solution)/shard_map/ppermute | solution.py:434
  79.1 4.3 %collective-permute-start.21 = (f32[8,128]{1,0:T(8,128)S(1)}, f32[8,128]{1,0:T(8,128)S(1)}, u32[]{:S(2)}, u32[]{:S(2)}) collective-permute-start(f32[8,128]{1,0:T(8,128)S(1)} %add.223), channel_id=1, source_target_pairs={{0,1},{1,2},{2,3},{3,0},{4,5},{5,6},{6,7},{7,4},{8,9},{9,10},{10,1... | collective-permute-start | bytes 12296 | tf_op jit(solution)/shard_map/ppermute | solution.py:434
  84.8 11.1 %collective-permute-start.24 = (bf16[848,128]{1,0:T(8,128)(2,1)S(1)}, bf16[848,128]{1,0:T(8,128)(2,1)S(1)}, u32[]{:S(2)}, u32[]{:S(2)}) collective-permute-start(bf16[848,128]{1,0:T(8,128)(2,1)S(1)} %get-tuple-element.48), channel_id=1, source_target_pairs={{0,32},{4,36},{8,40},{12,44},{16,48},{20,52},{24,56},{28,60},{32,0... | collective-permute-start | bytes 651272 | tf_op jit(solution)/shard_map/ppermute | solution.py:367
  95.9 5.5 %collective-permute-start.26 = (bf16[2,128,128]{2,1,0:T(8,128)(2,1)S(1)}, bf16[2,128,128]{2,1,0:T(8,128)(2,1)S(1)}, u32[]{:S(2)}, u32[]{:S(2)}) collective-permute-start(bf16[2,128,128]{2,1,0:T(8,128)(2,1)S(1)} %pad_maximum_fusion.8), channel_id=1, source_target_pairs={{0,16},{4,20},{8,24},{12,28},{16,0},{20,4},{24,8},{28,12},{32,48},... | collective-permute-start | bytes 196616 | tf_op jit(solution)/shard_map/ppermute | solution.py:367
  96.7 4.7 %collective-permute-start.25 = (bf16[2,128,128]{2,1,0:T(8,128)(2,1)S(1)}, bf16[2,128,128]{2,1,0:T(8,128)(2,1)S(1)}, u32[]{:S(2)}, u32[]{:S(2)}) collective-permute-start(bf16[2,128,128]{2,1,0:T(8,128)(2,1)S(1)} %pad_maximum_fusion.8), channel_id=1, source_target_pairs={{0,8},{4,12},{8,0},{12,4},{16,24},{20,28},{24,16},{28,20},{32,40},... | collective-permute-start | bytes 196616 | tf_op jit(solution)/shard_map/ppermute | solution.py:367
  98.6 4.3 %collective-permute-start.27 = (bf16[2,128,128]{2,1,0:T(8,128)(2,1)S(1)}, bf16[2,128,128]{2,1,0:T(8,128)(2,1)S(1)}, u32[]{:S(2)}, u32[]{:S(2)}) collective-permute-start(bf16[2,128,128]{2,1,0:T(8,128)(2,1)S(1)} %pad_maximum_fusion.8), channel_id=1, source_target_pairs={{0,24},{4,28},{8,16},{12,20},{16,8},{20,12},{24,0},{28,4},{32,56},... | collective-permute-start | bytes 196616 | tf_op jit(solution)/shard_map/ppermute | solution.py:367
  99.6 5.6 %collective-permute-start.32 = (bf16[2,352,128]{2,1,0:T(8,128)(2,1)S(1)}, bf16[2,352,128]{2,1,0:T(8,128)(2,1)S(1)}, u32[]{:S(2)}, u32[]{:S(2)}) collective-permute-start(bf16[2,352,128]{2,1,0:T(8,128)(2,1)S(1)} %pad_maximum_fusion.7), channel_id=1, source_target_pairs={{0,24},{4,28},{8,16},{12,20},{16,8},{20,12},{24,0},{28,4},{32,56},... | collective-permute-start | bytes 540680 | tf_op jit(solution)/shard_map/ppermute | solution.py:367
  101.4 4.4 %collective-permute-start.33 = (bf16[2,368,128]{2,1,0:T(8,128)(2,1)S(1)}, bf16[2,368,128]{2,1,0:T(8,128)(2,1)S(1)}, u32[]{:S(2)}, u32[]{:S(2)}) collective-permute-start(bf16[2,368,128]{2,1,0:T(8,128)(2,1)S(1)} %pad_maximum_fusion.6), channel_id=1, source_target_pairs={{0,8},{4,12},{8,0},{12,4},{16,24},{20,28},{24,16},{28,20},{32,40},... | collective-permute-start | bytes 565256 | tf_op jit(solution)/shard_map/ppermute | solution.py:367
  103.0 5.6 %collective-permute-start.30 = (bf16[4,2,128,128]{3,2,1,0:T(8,128)(2,1)S(1)}, bf16[4,2,128,128]{3,2,1,0:T(8,128)(2,1)S(1)}, u32[]{:S(2)}, u32[]{:S(2)}) collective-permute-start(bf16[4,2,128,128]{3,2,1,0:T(8,128)(2,1)S(1)} %get-tuple-element.89), channel_id=1, source_target_pairs={{0,192},{64,0},{128,64},{192,128},{1,193},{65,1},{129,65},{193,129... | collective-permute-start | bytes 786440 | tf_op jit(solution)/shard_map/ppermute | solution.py:457
  103.1 6.9 %collective-permute-start.29 = (bf16[4,2,128,128]{3,2,1,0:T(8,128)(2,1)S(1)}, bf16[4,2,128,128]{3,2,1,0:T(8,128)(2,1)S(1)}, u32[]{:S(2)}, u32[]{:S(2)}) collective-permute-start(bf16[4,2,128,128]{3,2,1,0:T(8,128)(2,1)S(1)} %get-tuple-element.89), channel_id=1, source_target_pairs={{0,128},{64,192},{128,0},{192,64},{1,129},{65,193},{129,1},{193,65... | collective-permute-start | bytes 786440 | tf_op jit(solution)/shard_map/ppermute | solution.py:457
  103.5 9.5 %collective-permute-start.28 = (bf16[4,2,128,128]{3,2,1,0:T(8,128)(2,1)S(1)}, bf16[4,2,128,128]{3,2,1,0:T(8,128)(2,1)S(1)}, u32[]{:S(2)}, u32[]{:S(2)}) collective-permute-start(bf16[4,2,128,128]{3,2,1,0:T(8,128)(2,1)S(1)} %get-tuple-element.89), channel_id=1, source_target_pairs={{0,64},{64,128},{128,192},{192,0},{1,65},{65,129},{129,193},{193,1... | collective-permute-start | bytes 786440 | tf_op jit(solution)/shard_map/ppermute | solution.py:457
  105.9 17.7 %collective-permute-start.34 = (bf16[2,2,352,128]{3,2,1,0:T(8,128)(2,1)S(1)}, bf16[2,2,352,128]{3,2,1,0:T(8,128)(2,1)S(1)}, u32[]{:S(2)}, u32[]{:S(2)}) collective-permute-start(bf16[2,2,352,128]{3,2,1,0:T(8,128)(2,1)S(1)} %pad_maximum_fusion.3), channel_id=1, source_target_pairs={{0,8},{4,12},{8,0},{12,4},{16,24},{20,28},{24,16},{28,20},{32,40},... | collective-permute-start | bytes 1081352 | tf_op jit(solution)/shard_map/ppermute | solution.py:367
  106.5 17.2 %collective-permute-start.35 = (bf16[2,2,368,128]{3,2,1,0:T(8,128)(2,1)S(1)}, bf16[2,2,368,128]{3,2,1,0:T(8,128)(2,1)S(1)}, u32[]{:S(2)}, u32[]{:S(2)}) collective-permute-start(bf16[2,2,368,128]{3,2,1,0:T(8,128)(2,1)S(1)} %pad_maximum_fusion.2), channel_id=1, source_target_pairs={{0,24},{4,28},{8,16},{12,20},{16,8},{20,12},{24,0},{28,4},{32,56},... | collective-permute-start | bytes 1130504 | tf_op jit(solution)/shard_map/ppermute | solution.py:367
  113.1 12.8 %collective-permute-start.31 = (bf16[4,4,2,128,128]{4,3,2,1,0:T(8,128)(2,1)S(1)}, bf16[4,4,2,128,128]{4,3,2,1,0:T(8,128)(2,1)S(1)}, u32[]{:S(2)}, u32[]{:S(2)}) collective-permute-start(bf16[4,4,2,128,128]{4,3,2,1,0:T(8,128)(2,1)S(1)} %pad_maximum_fusion.own_ref), channel_id=1, source_target_pairs={{0,4},{4,0},{8,12},{12,8},{16,20},{20,16},{24,28},{28,24},{32,36},... | collective-permute-start | bytes 3145736 | tf_op jit(solution)/shard_map/ppermute | solution.py:367
  125.9 3.3 %collective-permute-start.36 = (bf16[2,4,720,128]{3,2,1,0:T(8,128)(2,1)S(1)}, bf16[2,4,720,128]{3,2,1,0:T(8,128)(2,1)S(1)}, u32[]{:S(2)}, u32[]{:S(2)}) collective-permute-start(bf16[2,4,720,128]{3,2,1,0:T(8,128)(2,1)S(1)} %maximum_maximum_fusion.own_ref), channel_id=1, source_target_pairs={{0,4},{4,0},{8,12},{12,8},{16,20},{20,16},{24,28},{28,24},{32,36},... | collective-permute-start | bytes 4423688 | tf_op jit(solution)/shard_map/ppermute | solution.py:367
  (2 other events, 2.4 us)

commit v3 on v2

--- a/solution.py
+++ b/solution.py
@@ -253,7 +253,8 @@
     return found
 
 
-def join_kernel(own_ref, got_ref, _, q_hbm, o_hbm, q_ref, o_ref, q_sems, o_sems):
+def join_kernel(own_ref, got_ref, q_hbm, o_hbm, tick_ref, q_ref, o_ref, q_sems, o_sems):
+    tick_ref[...] = jnp.zeros_like(tick_ref)
     zh, x, core = position()
     lane = lanes(64)
 
@@ -314,8 +315,7 @@
         chunk_copy(o_ref, o_hbm, o_sems, g, columns(g)).wait()
 
 
-def table_join_kernel(own_ref, got_ref, t_hbm, tick_ref, t_ref, sems):
-    tick_ref[...] = jnp.zeros_like(tick_ref)
+def table_join_kernel(own_ref, got_ref, _, t_hbm, t_ref, sems):
     zh, x, core = position()
     section = lax.axis_index("section")
     lane = lanes(64)
@@ -389,11 +389,14 @@
     near, wrap = slots(0, slice(1, 3)).astype(F16), slots(1, slice(2, 4)).astype(F16)
     near, wrap, t_send = lax.optimization_barrier((near, wrap, t_send))
     t_got = dp_send(t_send, CORE)
-    near = dp_send(near, x_perm(1)).astype(F32)
-    wrap = dp_send(wrap, x_perm(3)).astype(F32)
-    near_last = dp_send((slots(0, 3) + near[1]).astype(F16), x_perm(3)).astype(F32)
-    wrap_last = dp_send((slots(1, 1) + wrap[0]).astype(F16), x_perm(1)).astype(F32)
-    halves = (slots(0, 0) + near[0] + near_last, slots(1, 0) + wrap[1] + wrap_last)
+    near = dp_send(near, x_perm(1))
+    wrap = dp_send(wrap, x_perm(3))
+    near_last = dp_send((slots(0, 3) + near[1].astype(F32)).astype(F16), x_perm(3)).astype(F32)
+    wrap_last = dp_send((slots(1, 1) + wrap[0].astype(F32)).astype(F16), x_perm(1)).astype(F32)
+    halves = (
+        slots(0, 0) + near[0].astype(F32) + near_last,
+        slots(1, 0) + wrap[1].astype(F32) + wrap_last,
+    )
 
     first_section = section == 0
     at_ends = jnp.logical_or(first_section, section == 3)
@@ -445,40 +448,45 @@
         table_master, table_first, table_second,
     )
 
-    def along_x(value):
-        return jnp.stack([value] + [dp_send(value, x_perm(k)) for k in (1, 2, 3)])
-
-    packed = jnp.stack([packed, dp_send(packed, ZHALF)])
-    t_all = along_x(packed[:, PACK:])
-    upper, lower = packed[:, :UPPER], packed[:, UPPER:PACK]
+    mine = [packed] + [dp_send(packed, x_perm(e)) for e in (1, 2, 3)]
+    z_got = dp_send(packed, ZHALF)
+    *mine, z_got = lax.optimization_barrier((*mine, z_got))
+
+    t_got = z_got[PACK:]
+    t_others = [t_got] + [dp_send(t_got, x_perm(e)) for e in (1, 2, 3)]
+    upper, lower = z_got[:UPPER], z_got[UPPER:PACK]
     upper_wrap = dp_send(upper, x_perm(3))
     lower_near = dp_send(lower, x_perm(1))
-    _, upper_wrap, lower_near = lax.optimization_barrier((t_all, upper_wrap, lower_near))
+    w_mine = jnp.stack([m[:PACK] for m in mine])
+    mine_other = dp_send(w_mine, CORE)
+    *_, mine_other, upper_wrap, lower_near = lax.optimization_barrier(
+        (*t_others, mine_other, upper_wrap, lower_near)
+    )
+    t_all = jnp.stack([jnp.stack([m[PACK:], t]) for m, t in zip(mine, t_others)])
     t_all = jnp.stack([t_all] + [lax.ppermute(t_all, "section", ring_perm(k)) for k in (1, 2, 3)])
     upper_rest = dp_send(jnp.stack([upper, upper_wrap]), x_perm(1))
     lower_rest = dp_send(jnp.stack([lower, lower_near]), x_perm(3))
     _, upper_rest, lower_rest = lax.optimization_barrier((t_all, upper_rest, lower_rest))
-    w_all = jnp.concatenate(
+    w_rest = jnp.concatenate(
         [
-            jnp.stack([upper, upper_rest[0], upper_rest[1], upper_wrap], axis=1),
-            jnp.stack([lower, lower_near, lower_rest[1], lower_rest[0]], axis=1),
+            jnp.stack([upper, upper_rest[0], upper_rest[1], upper_wrap]),
+            jnp.stack([lower, lower_near, lower_rest[1], lower_rest[0]]),
         ],
-        axis=2,
-    )
+        axis=1,
+    )
+    rest_other = dp_send(w_rest, CORE)
     t_other = dp_send(t_all, CORE)
-    t_other, w_all = lax.optimization_barrier((t_other, w_all))
-    w_other = dp_send(w_all, CORE)
-    table_full, tick = call(
-        table_join_kernel, (out((64, 14848), BF16), out((8, 128), F32)), t_all, t_other,
-        out_hbm=(0,), scratch=[pltpu.VMEM((64, 14848), BF16), pltpu.SemaphoreType.DMA((4,))],
-    )
-    query_full, output_full = call(
-        join_kernel, (out((128, 3968), BF16), out((64, 14848), BF16)),
-        w_all, w_other, tick, micros=3, out_hbm=(0, 1),
+    query_full, output_full, tick = call(
+        join_kernel, (out((128, 3968), BF16), out((64, 14848), BF16), out((8, 128), F32)),
+        jnp.stack([w_mine, w_rest]), jnp.stack([mine_other, rest_other]), micros=3, out_hbm=(0, 1),
         scratch=[
             pltpu.VMEM((128, 3968), BF16), pltpu.VMEM((64, 14848), BF16),
             pltpu.SemaphoreType.DMA((8,)), pltpu.SemaphoreType.DMA((4,)),
         ],
+    )
+    table_full = call(
+        table_join_kernel, out((64, 14848), BF16), t_all, t_other, tick, out_hbm=(0,),
+        scratch=[pltpu.VMEM((64, 14848), BF16), pltpu.SemaphoreType.DMA((4,))],
     )
     return (
         query_full[None],

time: 132 us -> 139 us (1.053)
  waiting for transfers between devices: 36 us -> 40.5 us
  starting transfers between devices: 74.4 us -> 78.6 us
  other arithmetic: 8.29 us -> 6.84 us
    ppermute x3, waiting for transfers between devices: 5.73 us -> 9.67 us  [per_device(): lax.ppermute(t_all, 'section', ring_perm(k))]
    ppermute x25 -> x29, starting transfers between devices: 56.9 us -> 59.7 us  [dp_send(): return lax.ppermute(value, 'dp', perm)]
    ppermute x3, waiting for transfers between devices: 0.01 us -> 1.97 us  [section_send(): return lax.ppermute(quarter(i).astype(F16), 'section', perm)]
    convert_element_type x3 -> x1, other arithmetic: 3.42 us -> 1.48 us  [per_device(): (slots(1, 1) + wrap[0].astype(F32)).astype(F16)]
    ppermute x25 -> x29, waiting for transfers between devices: 23.1 us -> 21.9 us  [dp_send(): return lax.ppermute(value, 'dp', perm)]
  transfers between devices with their start and end apart: 37 -> 41, of which waited for: 23 -> 25; matrix products, arithmetic and copies ran while one was open for 5% -> 4% of each run, Pallas kernels for 3% -> 3%
where the time goes in v3:
time: 139 us
  starting transfers between devices  78.6 us (57%)
  waiting for transfers between devices  40.5 us (29%)
  Pallas kernels  11 us (8%)
  other arithmetic  6.84 us (5%)
    ppermute x29, starting transfers between devices, dp_send(): return lax.ppermute(value, 'dp', perm)  59.7 us
    ppermute x29, waiting for transfers between devices, dp_send(): return lax.ppermute(value, 'dp', perm)  21.9 us
    pallas_call x5, Pallas kernels, call(): pl.pallas_call(kernel, out_shape=list(outs) if isinstance(outs, (list, tu...  11 us
    ppermute x3, waiting for transfers between devices, per_device(): lax.ppermute(t_all, 'section', ring_perm(k))  9.67 us
    ppermute x3, starting transfers between devices, section_send(): return lax.ppermute(quarter(i).astype(F16), 'section', perm)  8.52 us
    ppermute x3, starting transfers between devices, per_device(): lax.ppermute(squares, 'section', ring_perm(k))  4.1 us
    ppermute x3, waiting for transfers between devices, per_device(): lax.ppermute(squares, 'section', ring_perm(k))  3.66 us
    ppermute x3, starting transfers between devices, per_device(): lax.ppermute(squares, 'tensor', ring_perm(k))  3.38 us
  transfers between devices with their start and end apart: 41, of which 25 were waited for; matrix products, arithmetic and copies ran while one was open for 4% of the time, Pallas kernels for 3%

profile of v3, /device:TPU:1, one launch (start us, length us, event | category | flops | bytes accessed | tf_op | source)
XLA Modules:
  0.0 139.0 jit_solution(3048344377761214311)
XLA Ops:
  0.7 3.9 %shard_map.211 = (bf16[2,4,720,128]{3,2,1,0:T(8,128)(2,1)}, bf16[2,4,720,128]{3,2,1,0:T(8,128)(2,1)}, f32[8,128]{1,0:T(8,128)}) custom-call(bf16[128,3968]{1,0:T(8,128)(2,1)} %bitcast.174, bf16[64,14848]{1,0:T(8,128)(2,1)} %bitcast.173), custom_call_target="tpu_custom_call" | custom-call | bytes 9000000 | tf_op jit(solution)/shard_map/pallas_call | solution.py:47
  4.5 3.3 %collective-permute-start = (bf16[2,4,720,128]{3,2,1,0:T(8,128)(2,1)}, bf16[2,4,720,128]{3,2,1,0:T(8,128)(2,1)S(1)}, u32[]{:S(2)}, u32[]{:S(2)}) collective-permute-start(bf16[2,4,720,128]{3,2,1,0:T(8,128)(2,1)} %get-tuple-element.44), channel_id=1, source_target_pairs={{0,4},{4,0},{8,12},{12,8},{16,20},{20,16},{24,28},{28,24},{32,36},... | collective-permute-start | bytes 4423688 | tf_op jit(solution)/shard_map/ppermute | solution.py:367
  8.6 1.3 shard_map.212
  9.8 1.1 collective-permute-done
  11.0 1.4 fusion.2
  12.7 1.3 collective-permute-start.3
  14.0 1.0 collective-permute-done.5
  15.3 3.8 %collective-permute-start.8 = (f16[8,128,128]{2,1,0:T(8,128)(2,1)S(1)}, f16[8,128,128]{2,1,0:T(8,128)(2,1)S(1)}, u32[]{:S(2)}, u32[]{:S(2)}) collective-permute-start(f16[8,128,128]{2,1,0:T(8,128)(2,1)S(1)} %get-tuple-element.82), channel_id=1, source_target_pairs={{0,128},{192,64},{1,129},{193,65},{2,130},{194,66},{3,131},{195,67... | collective-permute-start | bytes 786440 | tf_op jit(solution)/shard_map/ppermute | solution.py:408
  19.1 2.7 %collective-permute-start.7 = (f16[8,128,128]{2,1,0:T(8,128)(2,1)S(1)}, f16[8,128,128]{2,1,0:T(8,128)(2,1)S(1)}, u32[]{:S(2)}, u32[]{:S(2)}) collective-permute-start(f16[8,128,128]{2,1,0:T(8,128)(2,1)S(1)} %get-tuple-element.83), channel_id=1, source_target_pairs={{0,192},{192,0},{1,193},{193,1},{2,194},{194,2},{3,195},{195,3},{4... | collective-permute-start | bytes 786440 | tf_op jit(solution)/shard_map/ppermute | solution.py:408
  21.8 2.0 %collective-permute-start.6 = (f16[8,128,128]{2,1,0:T(8,128)(2,1)S(1)}, f16[8,128,128]{2,1,0:T(8,128)(2,1)}, u32[]{:S(2)}, u32[]{:S(2)}) collective-permute-start(f16[8,128,128]{2,1,0:T(8,128)(2,1)S(1)} %get-tuple-element.84), channel_id=1, source_target_pairs={{0,64},{192,128},{1,65},{193,129},{2,66},{194,130},{3,67},{195,131... | collective-permute-start | bytes 786440 | tf_op jit(solution)/shard_map/ppermute | solution.py:408
  24.3 1.5 %fusion.3 = (f16[720,128]{1,0:T(8,128)(2,1)S(1)}, f16[720,128]{1,0:T(8,128)(2,1)S(1)}) fusion(f16[2,720,128]{2,1,0:T(8,128)(2,1)} %collective-permute-done.3, bf16[2,4,720,128]{3,2,1,0:T(8,128)(2,1)} %copy-done.12, bf16[2,4,720,128]{3,2,1,0:T(8,128)(2,1)} %get-tuple-element.43, f16[2,720,128]{2,1,0:T(8,128)(2,1)} %collective-permute-done.1), kind=kLoop, calls=%fused_computation.17 | loop fusion | flops 1105920 | bytes 1474560 | tf_op jit(solution)/shard_map/convert_element_type | solution.py:395
  25.9 1.8 %collective-permute-start.2 = (f16[720,128]{1,0:T(8,128)(2,1)S(1)}, f16[720,128]{1,0:T(8,128)(2,1)S(1)}, u32[]{:S(2)}, u32[]{:S(2)}) collective-permute-start(f16[720,128]{1,0:T(8,128)(2,1)S(1)} %get-tuple-element.79), channel_id=1, source_target_pairs={{0,24},{4,28},{8,16},{12,20},{16,8},{20,12},{24,0},{28,4},{32,56},... | collective-permute-start | bytes 552968 | tf_op jit(solution)/shard_map/ppermute | solution.py:367
  27.7 1.4 collective-permute-done.7
  29.7 1.1 fusion
  31.6 2.7 %collective-permute-start.10 = (f16[2,128,128]{2,1,0:T(8,128)(2,1)S(1)}, f16[2,128,128]{2,1,0:T(8,128)(2,1)S(1)}, u32[]{:S(2)}, u32[]{:S(2)}) collective-permute-start(f16[2,128,128]{2,1,0:T(8,128)(2,1)S(1)} %get-tuple-element.90), channel_id=1, source_target_pairs={{0,16},{4,20},{8,24},{12,28},{16,0},{20,4},{24,8},{28,12},{32,48},... | collective-permute-start | bytes 196616 | tf_op jit(solution)/shard_map/ppermute | solution.py:367
  34.8 1.5 %broadcast_select_fusion = (f32[720,128]{1,0:T(8,128)S(1)}, f16[720,128]{1,0:T(8,128)(2,1)S(1)}) fusion(pred[]{:T(512)S(6)} %eq.11, f16[720,128]{1,0:T(8,128)(2,1)S(1)} %collective-permute-done.2, f16[2,720,128]{2,1,0:T(8,128)(2,1)} %collective-permute-done.1, bf16[2,4,720,128]{3,2,1,0:T(8,128)(2,1)} %copy-done.12, ...), kind=kLoop, calls=%fused_computation.39 | loop fusion | flops 1566720 | bytes 2027521 | tf_op jit(solution)/shard_map/jit(_where)/select_n | solution.py:429
  36.6 2.5 %collective-permute-done.11 = f16[2,128,128]{2,1,0:T(8,128)(2,1)S(1)} collective-permute-done((f16[2,128,128]{2,1,0:T(8,128)(2,1)S(1)}, f16[2,128,128]{2,1,0:T(8,128)(2,1)S(1)}, u32[]{:S(2)}, u32[]{:S(2)}) %collective-permute-start.11) | collective-permute-done | bytes 65568 | tf_op jit(solution)/shard_map/ppermute | solution.py:367
  39.1 7.0 %collective-permute-start.12 = (f16[848,128]{1,0:T(8,128)(2,1)S(1)}, f16[848,128]{1,0:T(8,128)(2,1)S(1)}, u32[]{:S(2)}, u32[]{:S(2)}) collective-permute-start(f16[848,128]{1,0:T(8,128)(2,1)S(1)} %pad_maximum_fusion.5), channel_id=1, source_target_pairs={{0,32},{4,36},{8,40},{12,44},{16,48},{20,52},{24,56},{28,60},{32,0... | collective-permute-start | bytes 651272 | tf_op jit(solution)/shard_map/ppermute | solution.py:367
  46.1 3.4 %collective-permute-done.12 = f16[848,128]{1,0:T(8,128)(2,1)S(1)} collective-permute-done((f16[848,128]{1,0:T(8,128)(2,1)S(1)}, f16[848,128]{1,0:T(8,128)(2,1)S(1)}, u32[]{:S(2)}, u32[]{:S(2)}) %collective-permute-start.12) | collective-permute-done | bytes 217120 | tf_op jit(solution)/shard_map/ppermute | solution.py:367
  49.7 6.6 %collective-permute-start.13 = (f32[8,128]{1,0:T(8,128)S(1)}, f32[8,128]{1,0:T(8,128)S(1)}, u32[]{:S(2)}, u32[]{:S(2)}) collective-permute-start(f32[8,128]{1,0:T(8,128)S(1)} %get-tuple-element.74), channel_id=1, source_target_pairs={{0,4},{4,0},{8,12},{12,8},{16,20},{20,16},{24,28},{28,24},{32,36},... | collective-permute-start | bytes 12296 | tf_op jit(solution)/shard_map/ppermute | solution.py:367
  57.4 2.9 %collective-permute-start.14 = (f32[8,128]{1,0:T(8,128)S(1)}, f32[8,128]{1,0:T(8,128)S(1)}, u32[]{:S(2)}, u32[]{:S(2)}) collective-permute-start(f32[8,128]{1,0:T(8,128)S(1)} %add.216), channel_id=1, source_target_pairs={{0,8},{4,12},{8,0},{12,4},{16,24},{20,28},{24,16},{28,20},{32,40},... | collective-permute-start | bytes 12296 | tf_op jit(solution)/shard_map/ppermute | solution.py:367
  61.7 1.0 collective-permute-start.19
  62.6 3.1 %collective-permute-start.18 = (f32[8,128]{1,0:T(8,128)S(1)}, f32[8,128]{1,0:T(8,128)S(1)}, u32[]{:S(2)}, u32[]{:S(2)}) collective-permute-start(f32[8,128]{1,0:T(8,128)S(1)} %add_add_fusion.2), channel_id=1, source_target_pairs={{0,128},{64,192},{128,0},{192,64},{1,129},{65,193},{129,1},{193,65... | collective-permute-start | bytes 12296 | tf_op jit(solution)/shard_map/ppermute | solution.py:435
  65.8 1.0 collective-permute-done.18
  66.7 2.7 %collective-permute-done.17 = f32[8,128]{1,0:T(8,128)S(1)} collective-permute-done((f32[8,128]{1,0:T(8,128)S(1)}, f32[8,128]{1,0:T(8,128)S(1)}, u32[]{:S(2)}, u32[]{:S(2)}) %collective-permute-start.17) | collective-permute-done | bytes 4128 | tf_op jit(solution)/shard_map/ppermute | solution.py:435
  69.4 6.1 %collective-permute-start.20 = (f32[8,128]{1,0:T(8,128)S(1)}, f32[8,128]{1,0:T(8,128)S(1)}, u32[]{:S(2)}, u32[]{:S(2)}) collective-permute-start(f32[8,128]{1,0:T(8,128)S(1)} %add_add_fusion.1), channel_id=1, source_target_pairs={{0,32},{4,36},{8,40},{12,44},{16,48},{20,52},{24,56},{28,60},{32,0... | collective-permute-start | bytes 12296 | tf_op jit(solution)/shard_map/ppermute | solution.py:367
  75.5 1.0 collective-permute-done.20
  76.5 1.2 collective-permute-start.23
  77.7 1.1 collective-permute-start.22
  78.8 1.0 collective-permute-start.21
  79.9 1.3 collective-permute-done.22
  81.2 1.9 %collective-permute-done.21 = f32[8,128]{1,0:T(8,128)S(1)} collective-permute-done((f32[8,128]{1,0:T(8,128)S(1)}, f32[8,128]{1,0:T(8,128)S(1)}, u32[]{:S(2)}, u32[]{:S(2)}) %collective-permute-start.21) | collective-permute-done | bytes 4128 | tf_op jit(solution)/shard_map/ppermute | solution.py:437
  83.2 1.4 %shard_map.213 = (bf16[848,128]{1,0:T(8,128)(2,1)S(1)}, f32[8,3968]{1,0:T(8,128)}, f32[8,3968]{1,0:T(8,128)}, f32[8,3968]{1,0:T(8,128)}, f32[64,928]{1,0:T(8,128...) custom-call(f32[8,128]{1,0:T(8,128)S(1)} %add_add_fusion.n_ref, ...), custom_call_target="tpu_custom_call" | custom-call | bytes 6000000 | tf_op jit(solution)/shard_map/pallas_call | solution.py:47
  84.6 5.3 %collective-permute-start.27 = (bf16[848,128]{1,0:T(8,128)(2,1)S(1)}, bf16[848,128]{1,0:T(8,128)(2,1)S(1)}, u32[]{:S(2)}, u32[]{:S(2)}) collective-permute-start(bf16[848,128]{1,0:T(8,128)(2,1)S(1)} %get-tuple-element.52), channel_id=1, source_target_pairs={{0,32},{4,36},{8,40},{12,44},{16,48},{20,52},{24,56},{28,60},{32,0... | collective-permute-start | bytes 651272 | tf_op jit(solution)/shard_map/ppermute | solution.py:367
  89.9 2.1 %collective-permute-start.26 = (bf16[848,128]{1,0:T(8,128)(2,1)S(1)}, bf16[848,128]{1,0:T(8,128)(2,1)S(1)}, u32[]{:S(2)}, u32[]{:S(2)}) collective-permute-start(bf16[848,128]{1,0:T(8,128)(2,1)S(1)} %get-tuple-element.52), channel_id=1, source_target_pairs={{0,24},{4,28},{8,16},{12,20},{16,8},{20,12},{24,0},{28,4},{32,56},... | collective-permute-start | bytes 651272 | tf_op jit(solution)/shard_map/ppermute | solution.py:367
  93.2 2.5 %collective-permute-done.27 = bf16[848,128]{1,0:T(8,128)(2,1)S(1)} collective-permute-done((bf16[848,128]{1,0:T(8,128)(2,1)S(1)}, bf16[848,128]{1,0:T(8,128)(2,1)S(1)}, u32[]{:S(2)}, u32[]{:S(2)}) %collective-permute-start.27) | collective-permute-done | bytes 217120 | tf_op jit(solution)/shard_map/ppermute | solution.py:367
  95.7 1.5 %collective-permute-done.26 = bf16[848,128]{1,0:T(8,128)(2,1)S(1)} collective-permute-done((bf16[848,128]{1,0:T(8,128)(2,1)S(1)}, bf16[848,128]{1,0:T(8,128)(2,1)S(1)}, u32[]{:S(2)}, u32[]{:S(2)}) %collective-permute-start.26) | collective-permute-done | bytes 217120 | tf_op jit(solution)/shard_map/ppermute | solution.py:367
  97.2 1.4 collective-permute-done.25
  99.2 2.2 %collective-permute-start.30 = (bf16[128,128]{1,0:T(8,128)(2,1)S(1)}, bf16[128,128]{1,0:T(8,128)(2,1)S(1)}, u32[]{:S(2)}, u32[]{:S(2)}) collective-permute-start(bf16[128,128]{1,0:T(8,128)(2,1)S(1)} %get-tuple-element.99), channel_id=1, source_target_pairs={{0,24},{4,28},{8,16},{12,20},{16,8},{20,12},{24,0},{28,4},{32,56},... | collective-permute-start | bytes 98312 | tf_op jit(solution)/shard_map/ppermute | solution.py:367
  102.6 2.2 %collective-permute-start.35 = (bf16[352,128]{1,0:T(8,128)(2,1)S(1)}, bf16[352,128]{1,0:T(8,128)(2,1)S(1)}, u32[]{:S(2)}, u32[]{:S(2)}) collective-permute-start(bf16[352,128]{1,0:T(8,128)(2,1)S(1)} %get-tuple-element.97), channel_id=1, source_target_pairs={{0,24},{4,28},{8,16},{12,20},{16,8},{20,12},{24,0},{28,4},{32,56},... | collective-permute-start | bytes 270344 | tf_op jit(solution)/shard_map/ppermute | solution.py:367
  104.9 9.8 %collective-permute-start.34 = (bf16[4,720,128]{2,1,0:T(8,128)(2,1)S(1)}, bf16[4,720,128]{2,1,0:T(8,128)(2,1)S(1)}, u32[]{:S(2)}, u32[]{:S(2)}) collective-permute-start(bf16[4,720,128]{2,1,0:T(8,128)(2,1)S(1)} %get-tuple-element.86), channel_id=1, source_target_pairs={{0,4},{4,0},{8,12},{12,8},{16,20},{20,16},{24,28},{28,24},{32,36},... | collective-permute-start | bytes 2211848 | tf_op jit(solution)/shard_map/ppermute | solution.py:367
  115.1 2.7 %collective-permute-start.33 = (bf16[4,2,128,128]{3,2,1,0:T(8,128)(2,1)S(1)}, bf16[4,2,128,128]{3,2,1,0:T(8,128)(2,1)S(1)}, u32[]{:S(2)}, u32[]{:S(2)}) collective-permute-start(bf16[4,2,128,128]{3,2,1,0:T(8,128)(2,1)S(1)} %get-tuple-element.93), channel_id=1, source_target_pairs={{0,192},{64,0},{128,64},{192,128},{1,193},{65,1},{129,65},{193,129... | collective-permute-start | bytes 786440 | tf_op jit(solution)/shard_map/ppermute | solution.py:466
  117.8 1.3 collective-permute-done.36
  120.3 3.4 %collective-permute-done.32 = bf16[4,2,128,128]{3,2,1,0:T(8,128)(2,1)S(1)} collective-permute-done((bf16[4,2,128,128]{3,2,1,0:T(8,128)(2,1)S(1)}, bf16[4,2,128,128]{3,2,1,0:T(8,128)(2,1)S(1)}, u32[]{:S(2)}, u32[]{:S(2)}) %collective-permute-start.32) | collective-permute-done | bytes 262176 | tf_op jit(solution)/shard_map/ppermute | solution.py:466
  123.7 6.3 %collective-permute-done.31 = bf16[4,2,128,128]{3,2,1,0:T(8,128)(2,1)S(1)} collective-permute-done((bf16[4,2,128,128]{3,2,1,0:T(8,128)(2,1)S(1)}, bf16[4,2,128,128]{3,2,1,0:T(8,128)(2,1)S(1)}, u32[]{:S(2)}, u32[]{:S(2)}) %collective-permute-start.31) | collective-permute-done | bytes 262176 | tf_op jit(solution)/shard_map/ppermute | solution.py:466
  131.3 2.9 %collective-permute-done.39 = bf16[4,720,128]{2,1,0:T(8,128)(2,1)S(1)} collective-permute-done((bf16[4,720,128]{2,1,0:T(8,128)(2,1)S(1)}, bf16[4,720,128]{2,1,0:T(8,128)(2,1)S(1)}, u32[]{:S(2)}, u32[]{:S(2)}) %collective-permute-start.39) | collective-permute-done | bytes 737312 | tf_op jit(solution)/shard_map/ppermute | solution.py:367
  134.4 2.3 %shard_map.214 = (bf16[128,3968]{1,0:T(8,128)(2,1)}, bf16[64,14848]{1,0:T(8,128)(2,1)}, f32[8,128]{1,0:T(8,128)S(1)}) custom-call(bf16[2,4,720,128]{3,2,1,0:T(8,128)(2,1)S(1)} %pad_maximum_fusion.own_ref, bf16[2,4,720,128]{3,2,1,0:T(8,128)(2,1)S(1)} %pad_maximum_fusion.1.got_ref), custom_call_target="tpu_custom_call" | custom-call | bytes 9000000 | tf_op jit(solution)/shard_map/pallas_call | solution.py:47
  136.7 2.1 %shard_map.215 = bf16[64,14848]{1,0:T(8,128)(2,1)} custom-call(bf16[4,4,2,128,128]{4,3,2,1,0:T(8,128)(2,1)S(1)} %pad_maximum_fusion.2.own_ref, bf16[4,4,2,128,128]{4,3,2,1,0:T(8,128)(2,1)S(1)} %collective-permute-done.40.got_ref, f32[8,128]{1,0:T(8,128)S(1)} %get-tuple-element.70._), custom_call_target="tpu_custom_call" | custom-call | bytes 6000000 | tf_op jit(solution)/shard_map/pallas_call | solution.py:47
  (100 shorter events, 12.9 us)
Async XLA Ops:
  4.5 6.5 %collective-permute-start = (bf16[2,4,720,128]{3,2,1,0:T(8,128)(2,1)}, bf16[2,4,720,128]{3,2,1,0:T(8,128)(2,1)S(1)}, u32[]{:S(2)}, u32[]{:S(2)}) collective-permute-start(bf16[2,4,720,128]{3,2,1,0:T(8,128)(2,1)} %get-tuple-element.44), channel_id=1, source_target_pairs={{0,4},{4,0},{8,12},{12,8},{16,20},{20,16},{24,28},{28,24},{32,36},... | collective-permute-start | bytes 4423688 | tf_op jit(solution)/shard_map/ppermute | solution.py:367
  12.4 2.7 %collective-permute-start.5 = (bf16[4,8,128,128]{3,2,1,0:T(8,128)(2,1)S(1)}, bf16[4,8,128,128]{3,2,1,0:T(8,128)(2,1)S(1)}, u32[]{:S(2)}, u32[]{:S(2)}) collective-permute-start(bf16[4,8,128,128]{3,2,1,0:T(8,128)(2,1)S(1)} %get-tuple-element.50), channel_id=1, source_target_pairs={{0,4},{4,0},{8,12},{12,8},{16,20},{20,16},{24,28},{28,24},{32,36},... | collective-permute-start | bytes 3145736 | tf_op jit(solution)/shard_map/ppermute | solution.py:367
  12.7 11.1 %collective-permute-start.1 = (f16[2,720,128]{2,1,0:T(8,128)(2,1)}, f16[2,720,128]{2,1,0:T(8,128)(2,1)}, u32[]{:S(2)}, u32[]{:S(2)}) collective-permute-start(f16[2,720,128]{2,1,0:T(8,128)(2,1)} %get-tuple-element.47), channel_id=1, source_target_pairs={{0,8},{4,12},{8,0},{12,4},{16,24},{20,28},{24,16},{28,20},{32,40},... | collective-permute-start | bytes 1105928 | tf_op jit(solution)/shard_map/ppermute | solution.py:367
  12.7 11.6 %collective-permute-start.3 = (f16[2,720,128]{2,1,0:T(8,128)(2,1)}, f16[2,720,128]{2,1,0:T(8,128)(2,1)}, u32[]{:S(2)}, u32[]{:S(2)}) collective-permute-start(f16[2,720,128]{2,1,0:T(8,128)(2,1)} %get-tuple-element.48), channel_id=1, source_target_pairs={{0,24},{4,28},{8,16},{12,20},{16,8},{20,12},{24,0},{28,4},{32,56},... | collective-permute-start | bytes 1105928 | tf_op jit(solution)/shard_map/ppermute | solution.py:367
  15.3 12.4 %collective-permute-start.8 = (f16[8,128,128]{2,1,0:T(8,128)(2,1)S(1)}, f16[8,128,128]{2,1,0:T(8,128)(2,1)S(1)}, u32[]{:S(2)}, u32[]{:S(2)}) collective-permute-start(f16[8,128,128]{2,1,0:T(8,128)(2,1)S(1)} %get-tuple-element.82), channel_id=1, source_target_pairs={{0,128},{192,64},{1,129},{193,65},{2,130},{194,66},{3,131},{195,67... | collective-permute-start | bytes 786440 | tf_op jit(solution)/shard_map/ppermute | solution.py:408
  19.1 9.9 %collective-permute-start.7 = (f16[8,128,128]{2,1,0:T(8,128)(2,1)S(1)}, f16[8,128,128]{2,1,0:T(8,128)(2,1)S(1)}, u32[]{:S(2)}, u32[]{:S(2)}) collective-permute-start(f16[8,128,128]{2,1,0:T(8,128)(2,1)S(1)} %get-tuple-element.83), channel_id=1, source_target_pairs={{0,192},{192,0},{1,193},{193,1},{2,194},{194,2},{3,195},{195,3},{4... | collective-permute-start | bytes 786440 | tf_op jit(solution)/shard_map/ppermute | solution.py:408
  21.8 7.8 %collective-permute-start.6 = (f16[8,128,128]{2,1,0:T(8,128)(2,1)S(1)}, f16[8,128,128]{2,1,0:T(8,128)(2,1)}, u32[]{:S(2)}, u32[]{:S(2)}) collective-permute-start(f16[8,128,128]{2,1,0:T(8,128)(2,1)S(1)} %get-tuple-element.84), channel_id=1, source_target_pairs={{0,64},{192,128},{1,65},{193,129},{2,66},{194,130},{3,67},{195,131... | collective-permute-start | bytes 786440 | tf_op jit(solution)/shard_map/ppermute | solution.py:408
  25.8 9.0 %collective-permute-start.4 = (f16[720,128]{1,0:T(8,128)(2,1)S(1)}, f16[720,128]{1,0:T(8,128)(2,1)S(1)}, u32[]{:S(2)}, u32[]{:S(2)}) collective-permute-start(f16[720,128]{1,0:T(8,128)(2,1)S(1)} %get-tuple-element.78), channel_id=1, source_target_pairs={{0,8},{4,12},{8,0},{12,4},{16,24},{20,28},{24,16},{28,20},{32,40},... | collective-permute-start | bytes 552968 | tf_op jit(solution)/shard_map/ppermute | solution.py:367
  25.9 8.9 %collective-permute-start.2 = (f16[720,128]{1,0:T(8,128)(2,1)S(1)}, f16[720,128]{1,0:T(8,128)(2,1)S(1)}, u32[]{:S(2)}, u32[]{:S(2)}) collective-permute-start(f16[720,128]{1,0:T(8,128)(2,1)S(1)} %get-tuple-element.79), channel_id=1, source_target_pairs={{0,24},{4,28},{8,16},{12,20},{16,8},{20,12},{24,0},{28,4},{32,56},... | collective-permute-start | bytes 552968 | tf_op jit(solution)/shard_map/ppermute | solution.py:367
  30.8 5.6 %collective-permute-start.9 = (f16[2,128,128]{2,1,0:T(8,128)(2,1)S(1)}, f16[2,128,128]{2,1,0:T(8,128)(2,1)S(1)}, u32[]{:S(2)}, u32[]{:S(2)}) collective-permute-start(f16[2,128,128]{2,1,0:T(8,128)(2,1)S(1)} %get-tuple-element.89), channel_id=1, source_target_pairs={{0,8},{4,12},{8,0},{12,4},{16,24},{20,28},{24,16},{28,20},{32,40},... | collective-permute-start | bytes 196616 | tf_op jit(solution)/shard_map/ppermute | solution.py:367
  31.6 5.0 %collective-permute-start.10 = (f16[2,128,128]{2,1,0:T(8,128)(2,1)S(1)}, f16[2,128,128]{2,1,0:T(8,128)(2,1)S(1)}, u32[]{:S(2)}, u32[]{:S(2)}) collective-permute-start(f16[2,128,128]{2,1,0:T(8,128)(2,1)S(1)} %get-tuple-element.90), channel_id=1, source_target_pairs={{0,16},{4,20},{8,24},{12,28},{16,0},{20,4},{24,8},{28,12},{32,48},... | collective-permute-start | bytes 196616 | tf_op jit(solution)/shard_map/ppermute | solution.py:367
  34.2 4.8 %collective-permute-start.11 = (f16[2,128,128]{2,1,0:T(8,128)(2,1)S(1)}, f16[2,128,128]{2,1,0:T(8,128)(2,1)S(1)}, u32[]{:S(2)}, u32[]{:S(2)}) collective-permute-start(f16[2,128,128]{2,1,0:T(8,128)(2,1)S(1)} %get-tuple-element.91), channel_id=1, source_target_pairs={{0,24},{4,28},{8,16},{12,20},{16,8},{20,12},{24,0},{28,4},{32,56},... | collective-permute-start | bytes 196616 | tf_op jit(solution)/shard_map/ppermute | solution.py:367
  36.3 46.8 %copy-start.1 = (f32[1,64,928]{2,1,0:T(8,128)S(1)}, f32[1,64,928]{2,1,0:T(8,128)}, u32[]{:S(2)}) copy-start(f32[1,64,928]{2,1,0:T(8,128)} %param.17) | copy-start | bytes 712708
  36.3 46.8 %copy-start.2 = (f32[1,64,928]{2,1,0:T(8,128)S(1)}, f32[1,64,928]{2,1,0:T(8,128)}, u32[]{:S(2)}) copy-start(f32[1,64,928]{2,1,0:T(8,128)} %param.18) | copy-start | bytes 712708
  36.3 46.8 %copy-start.3 = (f32[1,64,928]{2,1,0:T(8,128)S(1)}, f32[1,64,928]{2,1,0:T(8,128)}, u32[]{:S(2)}) copy-start(f32[1,64,928]{2,1,0:T(8,128)} %param.19) | copy-start | bytes 712708
  36.3 46.8 %copy-start.4 = (f32[1,8,3968]{2,1,0:T(8,128)S(1)}, f32[1,8,3968]{2,1,0:T(8,128)}, u32[]{:S(2)}) copy-start(f32[1,8,3968]{2,1,0:T(8,128)} %param.13) | copy-start | bytes 380932
  36.4 46.8 %copy-start.5 = (f32[1,8,3968]{2,1,0:T(8,128)S(1)}, f32[1,8,3968]{2,1,0:T(8,128)}, u32[]{:S(2)}) copy-start(f32[1,8,3968]{2,1,0:T(8,128)} %param.14) | copy-start | bytes 380932
  36.4 46.8 %copy-start.6 = (f32[1,8,3968]{2,1,0:T(8,128)S(1)}, f32[1,8,3968]{2,1,0:T(8,128)}, u32[]{:S(2)}) copy-start(f32[1,8,3968]{2,1,0:T(8,128)} %param.15) | copy-start | bytes 380932
  36.4 46.8 %copy-start.7 = (f32[64,232]{1,0:T(8,128)S(1)}, f32[64,232]{1,0:T(8,128)}, u32[]{:S(2)}) copy-start(f32[64,232]{1,0:T(8,128)} %tw_ref.1) | copy-start | bytes 178180
  39.1 10.4 %collective-permute-start.12 = (f16[848,128]{1,0:T(8,128)(2,1)S(1)}, f16[848,128]{1,0:T(8,128)(2,1)S(1)}, u32[]{:S(2)}, u32[]{:S(2)}) collective-permute-start(f16[848,128]{1,0:T(8,128)(2,1)S(1)} %pad_maximum_fusion.5), channel_id=1, source_target_pairs={{0,32},{4,36},{8,40},{12,44},{16,48},{20,52},{24,56},{28,60},{32,0... | collective-permute-start | bytes 651272 | tf_op jit(solution)/shard_map/ppermute | solution.py:367
  49.7 7.4 %collective-permute-start.13 = (f32[8,128]{1,0:T(8,128)S(1)}, f32[8,128]{1,0:T(8,128)S(1)}, u32[]{:S(2)}, u32[]{:S(2)}) collective-permute-start(f32[8,128]{1,0:T(8,128)S(1)} %get-tuple-element.74), channel_id=1, source_target_pairs={{0,4},{4,0},{8,12},{12,8},{16,20},{20,16},{24,28},{28,24},{32,36},... | collective-permute-start | bytes 12296 | tf_op jit(solution)/shard_map/ppermute | solution.py:367
  57.1 3.7 %collective-permute-start.16 = (f32[8,128]{1,0:T(8,128)S(1)}, f32[8,128]{1,0:T(8,128)S(1)}, u32[]{:S(2)}, u32[]{:S(2)}) collective-permute-start(f32[8,128]{1,0:T(8,128)S(1)} %add.216), channel_id=1, source_target_pairs={{0,24},{4,28},{8,16},{12,20},{16,8},{20,12},{24,0},{28,4},{32,56},... | collective-permute-start | bytes 12296 | tf_op jit(solution)/shard_map/ppermute | solution.py:367
  57.1 4.0 %collective-permute-start.15 = (f32[8,128]{1,0:T(8,128)S(1)}, f32[8,128]{1,0:T(8,128)S(1)}, u32[]{:S(2)}, u32[]{:S(2)}) collective-permute-start(f32[8,128]{1,0:T(8,128)S(1)} %add.216), channel_id=1, source_target_pairs={{0,16},{4,20},{8,24},{12,28},{16,0},{20,4},{24,8},{28,12},{32,48},... | collective-permute-start | bytes 12296 | tf_op jit(solution)/shard_map/ppermute | solution.py:367
  57.4 4.2 %collective-permute-start.14 = (f32[8,128]{1,0:T(8,128)S(1)}, f32[8,128]{1,0:T(8,128)S(1)}, u32[]{:S(2)}, u32[]{:S(2)}) collective-permute-start(f32[8,128]{1,0:T(8,128)S(1)} %add.216), channel_id=1, source_target_pairs={{0,8},{4,12},{8,0},{12,4},{16,24},{20,28},{24,16},{28,20},{32,40},... | collective-permute-start | bytes 12296 | tf_op jit(solution)/shard_map/ppermute | solution.py:367
  61.7 4.1 %collective-permute-start.19 = (f32[8,128]{1,0:T(8,128)S(1)}, f32[8,128]{1,0:T(8,128)S(1)}, u32[]{:S(2)}, u32[]{:S(2)}) collective-permute-start(f32[8,128]{1,0:T(8,128)S(1)} %add_add_fusion.2), channel_id=1, source_target_pairs={{0,192},{64,0},{128,64},{192,128},{1,193},{65,1},{129,65},{193,129... | collective-permute-start | bytes 12296 | tf_op jit(solution)/shard_map/ppermute | solution.py:435
  62.6 4.1 %collective-permute-start.18 = (f32[8,128]{1,0:T(8,128)S(1)}, f32[8,128]{1,0:T(8,128)S(1)}, u32[]{:S(2)}, u32[]{:S(2)}) collective-permute-start(f32[8,128]{1,0:T(8,128)S(1)} %add_add_fusion.2), channel_id=1, source_target_pairs={{0,128},{64,192},{128,0},{192,64},{1,129},{65,193},{129,1},{193,65... | collective-permute-start | bytes 12296 | tf_op jit(solution)/shard_map/ppermute | solution.py:435
  65.7 3.7 %collective-permute-start.17 = (f32[8,128]{1,0:T(8,128)S(1)}, f32[8,128]{1,0:T(8,128)S(1)}, u32[]{:S(2)}, u32[]{:S(2)}) collective-permute-start(f32[8,128]{1,0:T(8,128)S(1)} %add_add_fusion.2), channel_id=1, source_target_pairs={{0,64},{64,128},{128,192},{192,0},{1,65},{65,129},{129,193},{193,1... | collective-permute-start | bytes 12296 | tf_op jit(solution)/shard_map/ppermute | solution.py:435
  69.4 7.1 %collective-permute-start.20 = (f32[8,128]{1,0:T(8,128)S(1)}, f32[8,128]{1,0:T(8,128)S(1)}, u32[]{:S(2)}, u32[]{:S(2)}) collective-permute-start(f32[8,128]{1,0:T(8,128)S(1)} %add_add_fusion.1), channel_id=1, source_target_pairs={{0,32},{4,36},{8,40},{12,44},{16,48},{20,52},{24,56},{28,60},{32,0... | collective-permute-start | bytes 12296 | tf_op jit(solution)/shard_map/ppermute | solution.py:367
  76.5 3.4 %collective-permute-start.23 = (f32[8,128]{1,0:T(8,128)S(1)}, f32[8,128]{1,0:T(8,128)S(1)}, u32[]{:S(2)}, u32[]{:S(2)}) collective-permute-start(f32[8,128]{1,0:T(8,128)S(1)} %add.223), channel_id=1, source_target_pairs={{0,3},{1,0},{2,1},{3,2},{4,7},{5,4},{6,5},{7,6},{8,11},{9,8},{10,9... | collective-permute-start | bytes 12296 | tf_op jit(solution)/shard_map/ppermute | solution.py:437
  77.7 3.5 %collective-permute-start.22 = (f32[8,128]{1,0:T(8,128)S(1)}, f32[8,128]{1,0:T(8,128)S(1)}, u32[]{:S(2)}, u32[]{:S(2)}) collective-permute-start(f32[8,128]{1,0:T(8,128)S(1)} %add.223), channel_id=1, source_target_pairs={{0,2},{1,3},{2,0},{3,1},{4,6},{5,7},{6,4},{7,5},{8,10},{9,11},{10,... | collective-permute-start | bytes 12296 | tf_op jit(solution)/shard_map/ppermute | solution.py:437
  78.8 4.3 %collective-permute-start.21 = (f32[8,128]{1,0:T(8,128)S(1)}, f32[8,128]{1,0:T(8,128)S(1)}, u32[]{:S(2)}, u32[]{:S(2)}) collective-permute-start(f32[8,128]{1,0:T(8,128)S(1)} %add.223), channel_id=1, source_target_pairs={{0,1},{1,2},{2,3},{3,0},{4,5},{5,6},{6,7},{7,4},{8,9},{9,10},{10,1... | collective-permute-start | bytes 12296 | tf_op jit(solution)/shard_map/ppermute | solution.py:437
  84.6 11.1 %collective-permute-start.27 = (bf16[848,128]{1,0:T(8,128)(2,1)S(1)}, bf16[848,128]{1,0:T(8,128)(2,1)S(1)}, u32[]{:S(2)}, u32[]{:S(2)}) collective-permute-start(bf16[848,128]{1,0:T(8,128)(2,1)S(1)} %get-tuple-element.52), channel_id=1, source_target_pairs={{0,32},{4,36},{8,40},{12,44},{16,48},{20,52},{24,56},{28,60},{32,0... | collective-permute-start | bytes 651272 | tf_op jit(solution)/shard_map/ppermute | solution.py:367
  89.9 7.3 %collective-permute-start.26 = (bf16[848,128]{1,0:T(8,128)(2,1)S(1)}, bf16[848,128]{1,0:T(8,128)(2,1)S(1)}, u32[]{:S(2)}, u32[]{:S(2)}) collective-permute-start(bf16[848,128]{1,0:T(8,128)(2,1)S(1)} %get-tuple-element.52), channel_id=1, source_target_pairs={{0,24},{4,28},{8,16},{12,20},{16,8},{20,12},{24,0},{28,4},{32,56},... | collective-permute-start | bytes 651272 | tf_op jit(solution)/shard_map/ppermute | solution.py:367
  92.1 6.5 %collective-permute-start.25 = (bf16[848,128]{1,0:T(8,128)(2,1)S(1)}, bf16[848,128]{1,0:T(8,128)(2,1)S(1)}, u32[]{:S(2)}, u32[]{:S(2)}) collective-permute-start(bf16[848,128]{1,0:T(8,128)(2,1)S(1)} %get-tuple-element.52), channel_id=1, source_target_pairs={{0,16},{4,20},{8,24},{12,28},{16,0},{20,4},{24,8},{28,12},{32,48},... | collective-permute-start | bytes 651272 | tf_op jit(solution)/shard_map/ppermute | solution.py:367
  93.0 6.1 %collective-permute-start.24 = (bf16[848,128]{1,0:T(8,128)(2,1)S(1)}, bf16[848,128]{1,0:T(8,128)(2,1)S(1)}, u32[]{:S(2)}, u32[]{:S(2)}) collective-permute-start(bf16[848,128]{1,0:T(8,128)(2,1)S(1)} %get-tuple-element.52), channel_id=1, source_target_pairs={{0,8},{4,12},{8,0},{12,4},{16,24},{20,28},{24,16},{28,20},{32,40},... | collective-permute-start | bytes 651272 | tf_op jit(solution)/shard_map/ppermute | solution.py:367
  99.2 15.5 %collective-permute-start.30 = (bf16[128,128]{1,0:T(8,128)(2,1)S(1)}, bf16[128,128]{1,0:T(8,128)(2,1)S(1)}, u32[]{:S(2)}, u32[]{:S(2)}) collective-permute-start(bf16[128,128]{1,0:T(8,128)(2,1)S(1)} %get-tuple-element.99), channel_id=1, source_target_pairs={{0,24},{4,28},{8,16},{12,20},{16,8},{20,12},{24,0},{28,4},{32,56},... | collective-permute-start | bytes 98312 | tf_op jit(solution)/shard_map/ppermute | solution.py:367
  101.4 13.5 %collective-permute-start.29 = (bf16[128,128]{1,0:T(8,128)(2,1)S(1)}, bf16[128,128]{1,0:T(8,128)(2,1)S(1)}, u32[]{:S(2)}, u32[]{:S(2)}) collective-permute-start(bf16[128,128]{1,0:T(8,128)(2,1)S(1)} %get-tuple-element.99), channel_id=1, source_target_pairs={{0,16},{4,20},{8,24},{12,28},{16,0},{20,4},{24,8},{28,12},{32,48},... | collective-permute-start | bytes 98312 | tf_op jit(solution)/shard_map/ppermute | solution.py:367
  102.3 12.6 %collective-permute-start.28 = (bf16[128,128]{1,0:T(8,128)(2,1)S(1)}, bf16[128,128]{1,0:T(8,128)(2,1)S(1)}, u32[]{:S(2)}, u32[]{:S(2)}) collective-permute-start(bf16[128,128]{1,0:T(8,128)(2,1)S(1)} %get-tuple-element.99), channel_id=1, source_target_pairs={{0,8},{4,12},{8,0},{12,4},{16,24},{20,28},{24,16},{28,20},{32,40},... | collective-permute-start | bytes 98312 | tf_op jit(solution)/shard_map/ppermute | solution.py:367
  102.6 12.6 %collective-permute-start.35 = (bf16[352,128]{1,0:T(8,128)(2,1)S(1)}, bf16[352,128]{1,0:T(8,128)(2,1)S(1)}, u32[]{:S(2)}, u32[]{:S(2)}) collective-permute-start(bf16[352,128]{1,0:T(8,128)(2,1)S(1)} %get-tuple-element.97), channel_id=1, source_target_pairs={{0,24},{4,28},{8,16},{12,20},{16,8},{20,12},{24,0},{28,4},{32,56},... | collective-permute-start | bytes 270344 | tf_op jit(solution)/shard_map/ppermute | solution.py:367
  104.9 14.2 %collective-permute-start.34 = (bf16[4,720,128]{2,1,0:T(8,128)(2,1)S(1)}, bf16[4,720,128]{2,1,0:T(8,128)(2,1)S(1)}, u32[]{:S(2)}, u32[]{:S(2)}) collective-permute-start(bf16[4,720,128]{2,1,0:T(8,128)(2,1)S(1)} %get-tuple-element.86), channel_id=1, source_target_pairs={{0,4},{4,0},{8,12},{12,8},{16,20},{20,16},{24,28},{28,24},{32,36},... | collective-permute-start | bytes 2211848 | tf_op jit(solution)/shard_map/ppermute | solution.py:367
  114.7 4.4 %collective-permute-start.36 = (bf16[368,128]{1,0:T(8,128)(2,1)S(1)}, bf16[368,128]{1,0:T(8,128)(2,1)S(1)}, u32[]{:S(2)}, u32[]{:S(2)}) collective-permute-start(bf16[368,128]{1,0:T(8,128)(2,1)S(1)} %get-tuple-element.95), channel_id=1, source_target_pairs={{0,8},{4,12},{8,0},{12,4},{16,24},{20,28},{24,16},{28,20},{32,40},... | collective-permute-start | bytes 282632 | tf_op jit(solution)/shard_map/ppermute | solution.py:367
  114.9 8.7 %collective-permute-start.32 = (bf16[4,2,128,128]{3,2,1,0:T(8,128)(2,1)S(1)}, bf16[4,2,128,128]{3,2,1,0:T(8,128)(2,1)S(1)}, u32[]{:S(2)}, u32[]{:S(2)}) collective-permute-start(bf16[4,2,128,128]{3,2,1,0:T(8,128)(2,1)S(1)} %get-tuple-element.93), channel_id=1, source_target_pairs={{0,128},{64,192},{128,0},{192,64},{1,129},{65,193},{129,1},{193,65... | collective-permute-start | bytes 786440 | tf_op jit(solution)/shard_map/ppermute | solution.py:466
  115.1 14.9 %collective-permute-start.31 = (bf16[4,2,128,128]{3,2,1,0:T(8,128)(2,1)S(1)}, bf16[4,2,128,128]{3,2,1,0:T(8,128)(2,1)S(1)}, u32[]{:S(2)}, u32[]{:S(2)}) collective-permute-start(bf16[4,2,128,128]{3,2,1,0:T(8,128)(2,1)S(1)} %get-tuple-element.93), channel_id=1, source_target_pairs={{0,64},{64,128},{128,192},{192,0},{1,65},{65,129},{129,193},{193,1... | collective-permute-start | bytes 786440 | tf_op jit(solution)/shard_map/ppermute | solution.py:466
  115.1 14.8 %collective-permute-start.33 = (bf16[4,2,128,128]{3,2,1,0:T(8,128)(2,1)S(1)}, bf16[4,2,128,128]{3,2,1,0:T(8,128)(2,1)S(1)}, u32[]{:S(2)}, u32[]{:S(2)}) collective-permute-start(bf16[4,2,128,128]{3,2,1,0:T(8,128)(2,1)S(1)} %get-tuple-element.93), channel_id=1, source_target_pairs={{0,192},{64,0},{128,64},{192,128},{1,193},{65,1},{129,65},{193,129... | collective-permute-start | bytes 786440 | tf_op jit(solution)/shard_map/ppermute | solution.py:466
  119.1 11.8 %collective-permute-start.38 = (bf16[2,368,128]{2,1,0:T(8,128)(2,1)S(1)}, bf16[2,368,128]{2,1,0:T(8,128)(2,1)S(1)}, u32[]{:S(2)}, u32[]{:S(2)}) collective-permute-start(bf16[2,368,128]{2,1,0:T(8,128)(2,1)S(1)} %pad_maximum_fusion.6), channel_id=1, source_target_pairs={{0,24},{4,28},{8,16},{12,20},{16,8},{20,12},{24,0},{28,4},{32,56},... | collective-permute-start | bytes 565256 | tf_op jit(solution)/shard_map/ppermute | solution.py:367
  119.4 11.5 %collective-permute-start.37 = (bf16[2,352,128]{2,1,0:T(8,128)(2,1)S(1)}, bf16[2,352,128]{2,1,0:T(8,128)(2,1)S(1)}, u32[]{:S(2)}, u32[]{:S(2)}) collective-permute-start(bf16[2,352,128]{2,1,0:T(8,128)(2,1)S(1)} %pad_maximum_fusion.7), channel_id=1, source_target_pairs={{0,8},{4,12},{8,0},{12,4},{16,24},{20,28},{24,16},{28,20},{32,40},... | collective-permute-start | bytes 540680 | tf_op jit(solution)/shard_map/ppermute | solution.py:367
  130.1 6.6 %collective-permute-start.40 = (bf16[4,4,2,128,128]{4,3,2,1,0:T(8,128)(2,1)S(1)}, bf16[4,4,2,128,128]{4,3,2,1,0:T(8,128)(2,1)S(1)}, u32[]{:S(2)}, u32[]{:S(2)}) collective-permute-start(bf16[4,4,2,128,128]{4,3,2,1,0:T(8,128)(2,1)S(1)} %pad_maximum_fusion.2.own_ref), channel_id=1, source_target_pairs={{0,4},{4,0},{8,12},{12,8},{16,20},{20,16},{24,28},{28,24},{32,36},... | collective-permute-start | bytes 3145736 | tf_op jit(solution)/shard_map/ppermute | solution.py:367
  131.0 3.2 %collective-permute-start.39 = (bf16[4,720,128]{2,1,0:T(8,128)(2,1)S(1)}, bf16[4,720,128]{2,1,0:T(8,128)(2,1)S(1)}, u32[]{:S(2)}, u32[]{:S(2)}) collective-permute-start(bf16[4,720,128]{2,1,0:T(8,128)(2,1)S(1)} %maximum_maximum_fusion), channel_id=1, source_target_pairs={{0,4},{4,0},{8,12},{12,8},{16,20},{20,16},{24,28},{28,24},{32,36},... | collective-permute-start | bytes 2211848 | tf_op jit(solution)/shard_map/ppermute | solution.py:367
  (6 other events, 105.6 us)

commit v4 on v2

--- a/solution.py
+++ b/solution.py
@@ -33,6 +33,10 @@
 
 def x_perm(e):
     return pair_perm(lambda d: d ^ (2 * e))
+
+
+def line_perm(e):
+    return [(i, i ^ e) for i in range(4)]
 
 
 def ring_perm(k):
@@ -389,11 +393,14 @@
     near, wrap = slots(0, slice(1, 3)).astype(F16), slots(1, slice(2, 4)).astype(F16)
     near, wrap, t_send = lax.optimization_barrier((near, wrap, t_send))
     t_got = dp_send(t_send, CORE)
-    near = dp_send(near, x_perm(1)).astype(F32)
-    wrap = dp_send(wrap, x_perm(3)).astype(F32)
-    near_last = dp_send((slots(0, 3) + near[1]).astype(F16), x_perm(3)).astype(F32)
-    wrap_last = dp_send((slots(1, 1) + wrap[0]).astype(F16), x_perm(1)).astype(F32)
-    halves = (slots(0, 0) + near[0] + near_last, slots(1, 0) + wrap[1] + wrap_last)
+    near = dp_send(near, x_perm(1))
+    wrap = dp_send(wrap, x_perm(3))
+    near_last = dp_send((slots(0, 3) + near[1].astype(F32)).astype(F16), x_perm(3)).astype(F32)
+    wrap_last = dp_send((slots(1, 1) + wrap[0].astype(F32)).astype(F16), x_perm(1)).astype(F32)
+    halves = (
+        slots(0, 0) + near[0].astype(F32) + near_last,
+        slots(1, 0) + wrap[1].astype(F32) + wrap_last,
+    )
 
     first_section = section == 0
     at_ends = jnp.logical_or(first_section, section == 3)
@@ -404,9 +411,9 @@
     def section_send(i, perm):
         return lax.ppermute(quarter(i).astype(F16), "section", perm)
 
-    t_far = section_send(jnp.where(first_section, 2, 1), [(0, 2), (3, 1)])
     t_near = section_send(jnp.where(first_section, 1, 2), [(0, 1), (3, 2)])
     t_end = section_send(jnp.where(first_section, 3, 0), [(0, 3), (3, 0)])
+    t_far = section_send(jnp.where(first_section, 2, 1), [(0, 2), (3, 1)])
     t_sum = jnp.where(at_ends, quarter(section), t_near.astype(F32)) + jnp.where(
         at_ends, t_end, t_far
     ).astype(F32)
@@ -430,8 +437,8 @@
     squares = squares + dp_send(squares, CORE)
     squares = squares + sum(dp_send(squares, x_perm(k)) for k in (1, 2, 3))
     squares = squares + sum(lax.ppermute(squares, "section", ring_perm(k)) for k in (1, 2, 3))
+    squares = squares + sum(lax.ppermute(squares, "tensor", line_perm(e)) for e in (1, 2, 3))
     squares = squares + dp_send(squares, ZHALF)
-    squares = squares + sum(lax.ppermute(squares, "tensor", ring_perm(k)) for k in (1, 2, 3))
 
     params_count = 4 * (128 * 15872 + 256 * 14848) + 256 * 14848
     limit = 0.5 * math.sqrt(params_count)

time: 132 us -> 129 us (0.977)
  other arithmetic: 8.29 us -> 6.48 us
  waiting for transfers between devices: 36 us -> 34.4 us
    ppermute x25, waiting for transfers between devices: 23.1 us -> 20.9 us  [dp_send(): return lax.ppermute(value, 'dp', perm)]
    convert_element_type x3 -> x1, other arithmetic: 3.42 us -> 1.48 us  [per_device(): (slots(1, 1) + wrap[0].astype(F32)).astype(F16)]
    ppermute x3, waiting for transfers between devices: 0.01 us -> 1.95 us  [section_send(): return lax.ppermute(quarter(i).astype(F16), 'section', perm)]
    ppermute x3, waiting for transfers between devices: 3.5 us -> 1.94 us  [per_device(): lax.ppermute(squares, 'tensor', line_perm(e))]
  transfers between devices with their start and end apart: 37 -> 37, of which waited for: 23 -> 27; matrix products, arithmetic and copies ran while one was open for 5% -> 4% of each run, Pallas kernels for 3% -> 3%
where the time goes in v4:
time: 129 us
  starting transfers between devices  75 us (58%)
  waiting for transfers between devices  34.4 us (27%)
  Pallas kernels  10.9 us (8%)
  other arithmetic  6.48 us (5%)
    ppermute x25, starting transfers between devices, dp_send(): return lax.ppermute(value, 'dp', perm)  57.3 us
    ppermute x25, waiting for transfers between devices, dp_send(): return lax.ppermute(value, 'dp', perm)  20.9 us
    pallas_call x5, Pallas kernels, call(): pl.pallas_call(kernel, out_shape=list(outs) if isinstance(outs, (list, tu...  10.9 us
    ppermute x3, starting transfers between devices, section_send(): return lax.ppermute(quarter(i).astype(F16), 'section', perm)  8.55 us
    ppermute x3, waiting for transfers between devices, per_device(): lax.ppermute(t_all, 'section', ring_perm(k))  5.99 us
    ppermute x3, starting transfers between devices, per_device(): lax.ppermute(squares, 'section', ring_perm(k))  4.1 us
    ppermute x3, waiting for transfers between devices, per_device(): lax.ppermute(squares, 'section', ring_perm(k))  3.66 us
    ppermute x3, starting transfers between devices, per_device(): lax.ppermute(squares, 'tensor', line_perm(e))  3.55 us
  transfers between devices with their start and end apart: 37, of which 27 were waited for; matrix products, arithmetic and copies ran while one was open for 4% of the time, Pallas kernels for 3%

profile of v4, /device:TPU:1, one launch (start us, length us, event | category | flops | bytes accessed | tf_op | source)
XLA Modules:
  0.0 128.8 jit_solution(14326721979885294019)
XLA Ops:
  0.7 3.9 %shard_map.211 = (bf16[2,4,720,128]{3,2,1,0:T(8,128)(2,1)}, bf16[2,4,720,128]{3,2,1,0:T(8,128)(2,1)}, f32[8,128]{1,0:T(8,128)}) custom-call(bf16[128,3968]{1,0:T(8,128)(2,1)} %bitcast.182, bf16[64,14848]{1,0:T(8,128)(2,1)} %bitcast.181), custom_call_target="tpu_custom_call" | custom-call | bytes 9000000 | tf_op jit(solution)/shard_map/pallas_call | solution.py:51
  4.5 3.3 %collective-permute-start = (bf16[2,4,720,128]{3,2,1,0:T(8,128)(2,1)}, bf16[2,4,720,128]{3,2,1,0:T(8,128)(2,1)S(1)}, u32[]{:S(2)}, u32[]{:S(2)}) collective-permute-start(bf16[2,4,720,128]{3,2,1,0:T(8,128)(2,1)} %get-tuple-element.41), channel_id=1, source_target_pairs={{0,4},{4,0},{8,12},{12,8},{16,20},{20,16},{24,28},{28,24},{32,36},... | collective-permute-start | bytes 4423688 | tf_op jit(solution)/shard_map/ppermute | solution.py:371
  8.6 1.3 shard_map.212
  9.8 1.1 collective-permute-done
  11.0 1.3 %fusion.2 = (f16[2,720,128]{2,1,0:T(8,128)(2,1)}, f16[2,720,128]{2,1,0:T(8,128)(2,1)}) fusion(bf16[2,4,720,128]{3,2,1,0:T(8,128)(2,1)S(1)} %collective-permute-done, bf16[2,4,720,128]{3,2,1,0:T(8,128)(2,1)S(1)} %copy-done.11), kind=kLoop, calls=%fused_computation.14 | loop fusion | flops 1474560 | bytes 2211840 | tf_op jit(solution)/shard_map/convert_element_type | solution.py:393
  12.7 1.3 %collective-permute-start.3 = (f16[2,720,128]{2,1,0:T(8,128)(2,1)}, f16[2,720,128]{2,1,0:T(8,128)(2,1)}, u32[]{:S(2)}, u32[]{:S(2)}) collective-permute-start(f16[2,720,128]{2,1,0:T(8,128)(2,1)} %get-tuple-element.45), channel_id=1, source_target_pairs={{0,24},{4,28},{8,16},{12,20},{16,8},{20,12},{24,0},{28,4},{32,56},... | collective-permute-start | bytes 1105928 | tf_op jit(solution)/shard_map/ppermute | solution.py:371
  14.0 1.0 collective-permute-done.5
  15.3 3.8 %collective-permute-start.8 = (f16[8,128,128]{2,1,0:T(8,128)(2,1)S(1)}, f16[8,128,128]{2,1,0:T(8,128)(2,1)S(1)}, u32[]{:S(2)}, u32[]{:S(2)}) collective-permute-start(f16[8,128,128]{2,1,0:T(8,128)(2,1)S(1)} %get-tuple-element.76), channel_id=1, source_target_pairs={{0,128},{192,64},{1,129},{193,65},{2,130},{194,66},{3,131},{195,67... | collective-permute-start | bytes 786440 | tf_op jit(solution)/shard_map/ppermute | solution.py:412
  19.1 2.7 %collective-permute-start.7 = (f16[8,128,128]{2,1,0:T(8,128)(2,1)S(1)}, f16[8,128,128]{2,1,0:T(8,128)(2,1)S(1)}, u32[]{:S(2)}, u32[]{:S(2)}) collective-permute-start(f16[8,128,128]{2,1,0:T(8,128)(2,1)S(1)} %get-tuple-element.77), channel_id=1, source_target_pairs={{0,192},{192,0},{1,193},{193,1},{2,194},{194,2},{3,195},{195,3},{4... | collective-permute-start | bytes 786440 | tf_op jit(solution)/shard_map/ppermute | solution.py:412
  21.8 2.0 %collective-permute-start.6 = (f16[8,128,128]{2,1,0:T(8,128)(2,1)S(1)}, f16[8,128,128]{2,1,0:T(8,128)(2,1)}, u32[]{:S(2)}, u32[]{:S(2)}) collective-permute-start(f16[8,128,128]{2,1,0:T(8,128)(2,1)S(1)} %get-tuple-element.78), channel_id=1, source_target_pairs={{0,64},{192,128},{1,65},{193,129},{2,66},{194,130},{3,67},{195,131... | collective-permute-start | bytes 786440 | tf_op jit(solution)/shard_map/ppermute | solution.py:412
  24.3 1.5 %fusion.3 = (f16[720,128]{1,0:T(8,128)(2,1)S(1)}, f16[720,128]{1,0:T(8,128)(2,1)S(1)}) fusion(f16[2,720,128]{2,1,0:T(8,128)(2,1)} %collective-permute-done.3, bf16[2,4,720,128]{3,2,1,0:T(8,128)(2,1)} %copy-done.12, bf16[2,4,720,128]{3,2,1,0:T(8,128)(2,1)} %get-tuple-element.40, f16[2,720,128]{2,1,0:T(8,128)(2,1)} %collective-permute-done.1), kind=kLoop, calls=%fused_computation.16 | loop fusion | flops 1105920 | bytes 1474560 | tf_op jit(solution)/shard_map/convert_element_type | solution.py:399
  25.9 1.8 %collective-permute-start.2 = (f16[720,128]{1,0:T(8,128)(2,1)S(1)}, f16[720,128]{1,0:T(8,128)(2,1)S(1)}, u32[]{:S(2)}, u32[]{:S(2)}) collective-permute-start(f16[720,128]{1,0:T(8,128)(2,1)S(1)} %get-tuple-element.73), channel_id=1, source_target_pairs={{0,24},{4,28},{8,16},{12,20},{16,8},{20,12},{24,0},{28,4},{32,56},... | collective-permute-start | bytes 552968 | tf_op jit(solution)/shard_map/ppermute | solution.py:371
  27.7 1.3 %collective-permute-done.7 = f16[8,128,128]{2,1,0:T(8,128)(2,1)S(1)} collective-permute-done((f16[8,128,128]{2,1,0:T(8,128)(2,1)S(1)}, f16[8,128,128]{2,1,0:T(8,128)(2,1)S(1)}, u32[]{:S(2)}, u32[]{:S(2)}) %collective-permute-start.7) | collective-permute-done | bytes 262176 | tf_op jit(solution)/shard_map/ppermute | solution.py:412
  29.6 1.1 fusion
  31.5 2.7 %collective-permute-start.10 = (f16[2,128,128]{2,1,0:T(8,128)(2,1)S(1)}, f16[2,128,128]{2,1,0:T(8,128)(2,1)S(1)}, u32[]{:S(2)}, u32[]{:S(2)}) collective-permute-start(f16[2,128,128]{2,1,0:T(8,128)(2,1)S(1)} %get-tuple-element.82), channel_id=1, source_target_pairs={{0,16},{4,20},{8,24},{12,28},{16,0},{20,4},{24,8},{28,12},{32,48},... | collective-permute-start | bytes 196616 | tf_op jit(solution)/shard_map/ppermute | solution.py:371
  34.7 1.5 %broadcast_select_fusion = (f32[720,128]{1,0:T(8,128)S(1)}, f16[720,128]{1,0:T(8,128)(2,1)S(1)}) fusion(pred[]{:T(512)S(6)} %eq.11, f16[720,128]{1,0:T(8,128)(2,1)S(1)} %collective-permute-done.2, f16[2,720,128]{2,1,0:T(8,128)(2,1)} %collective-permute-done.1, bf16[2,4,720,128]{3,2,1,0:T(8,128)(2,1)} %copy-done.12, ...), kind=kLoop, calls=%fused_computation.37 | loop fusion | flops 1566720 | bytes 2027521 | tf_op jit(solution)/shard_map/jit(_where)/select_n | solution.py:433
  36.5 2.5 %collective-permute-done.11 = f16[2,128,128]{2,1,0:T(8,128)(2,1)S(1)} collective-permute-done((f16[2,128,128]{2,1,0:T(8,128)(2,1)S(1)}, f16[2,128,128]{2,1,0:T(8,128)(2,1)S(1)}, u32[]{:S(2)}, u32[]{:S(2)}) %collective-permute-start.11) | collective-permute-done | bytes 65568 | tf_op jit(solution)/shard_map/ppermute | solution.py:371
  39.1 7.0 %collective-permute-start.12 = (f16[848,128]{1,0:T(8,128)(2,1)S(1)}, f16[848,128]{1,0:T(8,128)(2,1)S(1)}, u32[]{:S(2)}, u32[]{:S(2)}) collective-permute-start(f16[848,128]{1,0:T(8,128)(2,1)S(1)} %pad_maximum_fusion.5), channel_id=1, source_target_pairs={{0,32},{4,36},{8,40},{12,44},{16,48},{20,52},{24,56},{28,60},{32,0... | collective-permute-start | bytes 651272 | tf_op jit(solution)/shard_map/ppermute | solution.py:371
  46.1 3.4 %collective-permute-done.12 = f16[848,128]{1,0:T(8,128)(2,1)S(1)} collective-permute-done((f16[848,128]{1,0:T(8,128)(2,1)S(1)}, f16[848,128]{1,0:T(8,128)(2,1)S(1)}, u32[]{:S(2)}, u32[]{:S(2)}) %collective-permute-start.12) | collective-permute-done | bytes 217120 | tf_op jit(solution)/shard_map/ppermute | solution.py:371
  49.6 6.6 %collective-permute-start.13 = (f32[8,128]{1,0:T(8,128)S(1)}, f32[8,128]{1,0:T(8,128)S(1)}, u32[]{:S(2)}, u32[]{:S(2)}) collective-permute-start(f32[8,128]{1,0:T(8,128)S(1)} %get-tuple-element.68), channel_id=1, source_target_pairs={{0,4},{4,0},{8,12},{12,8},{16,20},{20,16},{24,28},{28,24},{32,36},... | collective-permute-start | bytes 12296 | tf_op jit(solution)/shard_map/ppermute | solution.py:371
  57.4 2.9 %collective-permute-start.14 = (f32[8,128]{1,0:T(8,128)S(1)}, f32[8,128]{1,0:T(8,128)S(1)}, u32[]{:S(2)}, u32[]{:S(2)}) collective-permute-start(f32[8,128]{1,0:T(8,128)S(1)} %add.216), channel_id=1, source_target_pairs={{0,8},{4,12},{8,0},{12,4},{16,24},{20,28},{24,16},{28,20},{32,40},... | collective-permute-start | bytes 12296 | tf_op jit(solution)/shard_map/ppermute | solution.py:371
  61.6 1.0 collective-permute-start.19
  62.6 3.1 %collective-permute-start.18 = (f32[8,128]{1,0:T(8,128)S(1)}, f32[8,128]{1,0:T(8,128)S(1)}, u32[]{:S(2)}, u32[]{:S(2)}) collective-permute-start(f32[8,128]{1,0:T(8,128)S(1)} %add_add_fusion.2), channel_id=1, source_target_pairs={{0,128},{64,192},{128,0},{192,64},{1,129},{65,193},{129,1},{193,65... | collective-permute-start | bytes 12296 | tf_op jit(solution)/shard_map/ppermute | solution.py:439
  65.7 1.0 collective-permute-done.18
  66.7 2.7 %collective-permute-done.17 = f32[8,128]{1,0:T(8,128)S(1)} collective-permute-done((f32[8,128]{1,0:T(8,128)S(1)}, f32[8,128]{1,0:T(8,128)S(1)}, u32[]{:S(2)}, u32[]{:S(2)}) %collective-permute-start.17) | collective-permute-done | bytes 4128 | tf_op jit(solution)/shard_map/ppermute | solution.py:439
  69.4 1.9 %collective-permute-start.22 = (f32[8,128]{1,0:T(8,128)S(1)}, f32[8,128]{1,0:T(8,128)S(1)}, u32[]{:S(2)}, u32[]{:S(2)}) collective-permute-start(f32[8,128]{1,0:T(8,128)S(1)} %add_add_fusion.1), channel_id=1, source_target_pairs={{0,3},{1,2},{2,1},{3,0},{4,7},{5,6},{6,5},{7,4},{8,11},{9,10},{10,... | collective-permute-start | bytes 12296 | tf_op jit(solution)/shard_map/ppermute | solution.py:440
  71.3 1.1 collective-permute-start.21
  73.6 1.0 collective-permute-done.21
  74.9 5.3 %collective-permute-start.23 = (f32[8,128]{1,0:T(8,128)S(1)}, f32[8,128]{1,0:T(8,128)S(1)}, u32[]{:S(2)}, u32[]{:S(2)}) collective-permute-start(f32[8,128]{1,0:T(8,128)S(1)} %add_add_fusion), channel_id=1, source_target_pairs={{0,32},{4,36},{8,40},{12,44},{16,48},{20,52},{24,56},{28,60},{32,0... | collective-permute-start | bytes 12296 | tf_op jit(solution)/shard_map/ppermute | solution.py:371
  80.2 1.0 collective-permute-done.23
  81.3 1.4 %shard_map.213 = (bf16[848,128]{1,0:T(8,128)(2,1)S(1)}, f32[8,3968]{1,0:T(8,128)}, f32[8,3968]{1,0:T(8,128)}, f32[8,3968]{1,0:T(8,128)}, f32[64,928]{1,0:T(8,128...) custom-call(f32[8,128]{1,0:T(8,128)S(1)} %add.226.n_ref, ...), custom_call_target="tpu_custom_call" | custom-call | bytes 6000000 | tf_op jit(solution)/shard_map/pallas_call | solution.py:51
  82.8 5.3 %collective-permute-start.24 = (bf16[848,128]{1,0:T(8,128)(2,1)S(1)}, bf16[848,128]{1,0:T(8,128)(2,1)S(1)}, u32[]{:S(2)}, u32[]{:S(2)}) collective-permute-start(bf16[848,128]{1,0:T(8,128)(2,1)S(1)} %get-tuple-element.48), channel_id=1, source_target_pairs={{0,32},{4,36},{8,40},{12,44},{16,48},{20,52},{24,56},{28,60},{32,0... | collective-permute-start | bytes 651272 | tf_op jit(solution)/shard_map/ppermute | solution.py:371
  88.1 3.4 %collective-permute-done.24 = bf16[848,128]{1,0:T(8,128)(2,1)S(1)} collective-permute-done((bf16[848,128]{1,0:T(8,128)(2,1)S(1)}, bf16[848,128]{1,0:T(8,128)(2,1)S(1)}, u32[]{:S(2)}, u32[]{:S(2)}) %collective-permute-start.24) | collective-permute-done | bytes 217120 | tf_op jit(solution)/shard_map/ppermute | solution.py:371
  91.5 1.5 %collective-permute-start.26 = (bf16[2,128,128]{2,1,0:T(8,128)(2,1)S(1)}, bf16[2,128,128]{2,1,0:T(8,128)(2,1)S(1)}, u32[]{:S(2)}, u32[]{:S(2)}) collective-permute-start(bf16[2,128,128]{2,1,0:T(8,128)(2,1)S(1)} %pad_maximum_fusion.8), channel_id=1, source_target_pairs={{0,16},{4,20},{8,24},{12,28},{16,0},{20,4},{24,8},{28,12},{32,48},... | collective-permute-start | bytes 196616 | tf_op jit(solution)/shard_map/ppermute | solution.py:371
  93.0 1.3 collective-permute-start.25
  94.3 0.9 collective-permute-start.27
  95.2 1.8 %collective-permute-start.32 = (bf16[2,352,128]{2,1,0:T(8,128)(2,1)S(1)}, bf16[2,352,128]{2,1,0:T(8,128)(2,1)S(1)}, u32[]{:S(2)}, u32[]{:S(2)}) collective-permute-start(bf16[2,352,128]{2,1,0:T(8,128)(2,1)S(1)} %pad_maximum_fusion.7), channel_id=1, source_target_pairs={{0,24},{4,28},{8,16},{12,20},{16,8},{20,12},{24,0},{28,4},{32,56},... | collective-permute-start | bytes 540680 | tf_op jit(solution)/shard_map/ppermute | solution.py:371
  97.1 1.8 %collective-permute-done.27 = bf16[2,128,128]{2,1,0:T(8,128)(2,1)S(1)} collective-permute-done((bf16[2,128,128]{2,1,0:T(8,128)(2,1)S(1)}, bf16[2,128,128]{2,1,0:T(8,128)(2,1)S(1)}, u32[]{:S(2)}, u32[]{:S(2)}) %collective-permute-start.27) | collective-permute-done | bytes 65568 | tf_op jit(solution)/shard_map/ppermute | solution.py:371
  99.6 0.9 collective-permute-start.28
  101.7 1.2 collective-permute-start.35
  102.9 1.6 %collective-permute-done.30 = bf16[4,2,128,128]{3,2,1,0:T(8,128)(2,1)S(1)} collective-permute-done((bf16[4,2,128,128]{3,2,1,0:T(8,128)(2,1)S(1)}, bf16[4,2,128,128]{3,2,1,0:T(8,128)(2,1)S(1)}, u32[]{:S(2)}, u32[]{:S(2)}) %collective-permute-start.30) | collective-permute-done | bytes 262176 | tf_op jit(solution)/shard_map/ppermute | solution.py:464
  104.5 1.4 %collective-permute-done.29 = bf16[4,2,128,128]{3,2,1,0:T(8,128)(2,1)S(1)} collective-permute-done((bf16[4,2,128,128]{3,2,1,0:T(8,128)(2,1)S(1)}, bf16[4,2,128,128]{3,2,1,0:T(8,128)(2,1)S(1)}, u32[]{:S(2)}, u32[]{:S(2)}) %collective-permute-start.29) | collective-permute-done | bytes 262176 | tf_op jit(solution)/shard_map/ppermute | solution.py:464
  105.9 3.0 %collective-permute-done.28 = bf16[4,2,128,128]{3,2,1,0:T(8,128)(2,1)S(1)} collective-permute-done((bf16[4,2,128,128]{3,2,1,0:T(8,128)(2,1)S(1)}, bf16[4,2,128,128]{3,2,1,0:T(8,128)(2,1)S(1)}, u32[]{:S(2)}, u32[]{:S(2)}) %collective-permute-start.28) | collective-permute-done | bytes 262176 | tf_op jit(solution)/shard_map/ppermute | solution.py:464
  109.1 11.7 %collective-permute-start.31 = (bf16[4,4,2,128,128]{4,3,2,1,0:T(8,128)(2,1)S(1)}, bf16[4,4,2,128,128]{4,3,2,1,0:T(8,128)(2,1)S(1)}, u32[]{:S(2)}, u32[]{:S(2)}) collective-permute-start(bf16[4,4,2,128,128]{4,3,2,1,0:T(8,128)(2,1)S(1)} %pad_maximum_fusion.own_ref), channel_id=1, source_target_pairs={{0,4},{4,0},{8,12},{12,8},{16,20},{20,16},{24,28},{28,24},{32,36},... | collective-permute-start | bytes 3145736 | tf_op jit(solution)/shard_map/ppermute | solution.py:371
  121.1 2.0 %collective-permute-done.31.got_ref = bf16[4,4,2,128,128]{4,3,2,1,0:T(8,128)(2,1)S(1)} collective-permute-done((bf16[4,4,2,128,128]{4,3,2,1,0:T(8,128)(2,1)S(1)}, bf16[4,4,2,128,128]{4,3,2,1,0:T(8,128)(2,1)S(1)}, u32[]{:S(2)}, u32[]{:S(2)}) %collective-permute-start.31) | collective-permute-done | bytes 1048608 | tf_op jit(solution)/shard_map/ppermute | solution.py:371
  123.5 2.1 %shard_map.214 = (bf16[64,14848]{1,0:T(8,128)(2,1)}, f32[8,128]{1,0:T(8,128)S(1)}) custom-call(bf16[4,4,2,128,128]{4,3,2,1,0:T(8,128)(2,1)S(1)} %pad_maximum_fusion.own_ref, bf16[4,4,2,128,128]{4,3,2,1,0:T(8,128)(2,1)S(1)} %collective-permute-done.31.got_ref), custom_call_target="tpu_custom_call" | custom-call | bytes 6000000 | tf_op jit(solution)/shard_map/pallas_call | solution.py:51
  125.5 0.8 collective-permute-done.36.got_ref
  126.4 2.3 %shard_map.215 = (bf16[128,3968]{1,0:T(8,128)(2,1)}, bf16[64,14848]{1,0:T(8,128)(2,1)}) custom-call(bf16[2,4,720,128]{3,2,1,0:T(8,128)(2,1)S(1)} %maximum_maximum_fusion.own_ref, bf16[2,4,720,128]{3,2,1,0:T(8,128)(2,1)S(1)} %collective-permute-done.36.got_ref, f32[8,128]{1,0:T(8,128)S(1)} %get-tuple-element.55._), custom_call_target="tpu_custom_call" | custom-call | bytes 9000000 | tf_op jit(solution)/shard_map/pallas_call | solution.py:51
  (86 shorter events, 11.0 us)
Async XLA Ops:
  0.6 7.2 %copy-start = (bf16[1,1,64,14848]{3,2,1,0:T(8,128)(2,1)S(1)}, bf16[1,1,64,14848]{3,2,1,0:T(8,128)(2,1)}, u32[]{:S(2)}) copy-start(bf16[1,1,64,14848]{3,2,1,0:T(8,128)(2,1)} %param.20) | copy-start | bytes 5701636
  4.5 6.5 %collective-permute-start = (bf16[2,4,720,128]{3,2,1,0:T(8,128)(2,1)}, bf16[2,4,720,128]{3,2,1,0:T(8,128)(2,1)S(1)}, u32[]{:S(2)}, u32[]{:S(2)}) collective-permute-start(bf16[2,4,720,128]{3,2,1,0:T(8,128)(2,1)} %get-tuple-element.41), channel_id=1, source_target_pairs={{0,4},{4,0},{8,12},{12,8},{16,20},{20,16},{24,28},{28,24},{32,36},... | collective-permute-start | bytes 4423688 | tf_op jit(solution)/shard_map/ppermute | solution.py:371
  8.6 2.4 %copy-start.11 = (bf16[2,4,720,128]{3,2,1,0:T(8,128)(2,1)S(1)}, bf16[2,4,720,128]{3,2,1,0:T(8,128)(2,1)}, u32[]{:S(2)}) copy-start(bf16[2,4,720,128]{3,2,1,0:T(8,128)(2,1)} %get-tuple-element.40) | copy-start | bytes 4423684
  12.3 2.7 %collective-permute-start.5 = (bf16[4,8,128,128]{3,2,1,0:T(8,128)(2,1)S(1)}, bf16[4,8,128,128]{3,2,1,0:T(8,128)(2,1)S(1)}, u32[]{:S(2)}, u32[]{:S(2)}) collective-permute-start(bf16[4,8,128,128]{3,2,1,0:T(8,128)(2,1)S(1)} %get-tuple-element.47), channel_id=1, source_target_pairs={{0,4},{4,0},{8,12},{12,8},{16,20},{20,16},{24,28},{28,24},{32,36},... | collective-permute-start | bytes 3145736 | tf_op jit(solution)/shard_map/ppermute | solution.py:371
  12.7 11.1 %collective-permute-start.1 = (f16[2,720,128]{2,1,0:T(8,128)(2,1)}, f16[2,720,128]{2,1,0:T(8,128)(2,1)}, u32[]{:S(2)}, u32[]{:S(2)}) collective-permute-start(f16[2,720,128]{2,1,0:T(8,128)(2,1)} %get-tuple-element.44), channel_id=1, source_target_pairs={{0,8},{4,12},{8,0},{12,4},{16,24},{20,28},{24,16},{28,20},{32,40},... | collective-permute-start | bytes 1105928 | tf_op jit(solution)/shard_map/ppermute | solution.py:371
  12.7 11.6 %collective-permute-start.3 = (f16[2,720,128]{2,1,0:T(8,128)(2,1)}, f16[2,720,128]{2,1,0:T(8,128)(2,1)}, u32[]{:S(2)}, u32[]{:S(2)}) collective-permute-start(f16[2,720,128]{2,1,0:T(8,128)(2,1)} %get-tuple-element.45), channel_id=1, source_target_pairs={{0,24},{4,28},{8,16},{12,20},{16,8},{20,12},{24,0},{28,4},{32,56},... | collective-permute-start | bytes 1105928 | tf_op jit(solution)/shard_map/ppermute | solution.py:371
  15.3 12.4 %collective-permute-start.8 = (f16[8,128,128]{2,1,0:T(8,128)(2,1)S(1)}, f16[8,128,128]{2,1,0:T(8,128)(2,1)S(1)}, u32[]{:S(2)}, u32[]{:S(2)}) collective-permute-start(f16[8,128,128]{2,1,0:T(8,128)(2,1)S(1)} %get-tuple-element.76), channel_id=1, source_target_pairs={{0,128},{192,64},{1,129},{193,65},{2,130},{194,66},{3,131},{195,67... | collective-permute-start | bytes 786440 | tf_op jit(solution)/shard_map/ppermute | solution.py:412
  19.1 9.9 %collective-permute-start.7 = (f16[8,128,128]{2,1,0:T(8,128)(2,1)S(1)}, f16[8,128,128]{2,1,0:T(8,128)(2,1)S(1)}, u32[]{:S(2)}, u32[]{:S(2)}) collective-permute-start(f16[8,128,128]{2,1,0:T(8,128)(2,1)S(1)} %get-tuple-element.77), channel_id=1, source_target_pairs={{0,192},{192,0},{1,193},{193,1},{2,194},{194,2},{3,195},{195,3},{4... | collective-permute-start | bytes 786440 | tf_op jit(solution)/shard_map/ppermute | solution.py:412
  21.8 7.8 %collective-permute-start.6 = (f16[8,128,128]{2,1,0:T(8,128)(2,1)S(1)}, f16[8,128,128]{2,1,0:T(8,128)(2,1)}, u32[]{:S(2)}, u32[]{:S(2)}) collective-permute-start(f16[8,128,128]{2,1,0:T(8,128)(2,1)S(1)} %get-tuple-element.78), channel_id=1, source_target_pairs={{0,64},{192,128},{1,65},{193,129},{2,66},{194,130},{3,67},{195,131... | collective-permute-start | bytes 786440 | tf_op jit(solution)/shard_map/ppermute | solution.py:412
  25.8 9.0 %collective-permute-start.4 = (f16[720,128]{1,0:T(8,128)(2,1)S(1)}, f16[720,128]{1,0:T(8,128)(2,1)S(1)}, u32[]{:S(2)}, u32[]{:S(2)}) collective-permute-start(f16[720,128]{1,0:T(8,128)(2,1)S(1)} %get-tuple-element.72), channel_id=1, source_target_pairs={{0,8},{4,12},{8,0},{12,4},{16,24},{20,28},{24,16},{28,20},{32,40},... | collective-permute-start | bytes 552968 | tf_op jit(solution)/shard_map/ppermute | solution.py:371
  25.9 8.9 %collective-permute-start.2 = (f16[720,128]{1,0:T(8,128)(2,1)S(1)}, f16[720,128]{1,0:T(8,128)(2,1)S(1)}, u32[]{:S(2)}, u32[]{:S(2)}) collective-permute-start(f16[720,128]{1,0:T(8,128)(2,1)S(1)} %get-tuple-element.73), channel_id=1, source_target_pairs={{0,24},{4,28},{8,16},{12,20},{16,8},{20,12},{24,0},{28,4},{32,56},... | collective-permute-start | bytes 552968 | tf_op jit(solution)/shard_map/ppermute | solution.py:371
  30.8 5.6 %collective-permute-start.9 = (f16[2,128,128]{2,1,0:T(8,128)(2,1)S(1)}, f16[2,128,128]{2,1,0:T(8,128)(2,1)S(1)}, u32[]{:S(2)}, u32[]{:S(2)}) collective-permute-start(f16[2,128,128]{2,1,0:T(8,128)(2,1)S(1)} %get-tuple-element.81), channel_id=1, source_target_pairs={{0,8},{4,12},{8,0},{12,4},{16,24},{20,28},{24,16},{28,20},{32,40},... | collective-permute-start | bytes 196616 | tf_op jit(solution)/shard_map/ppermute | solution.py:371
  31.5 5.0 %collective-permute-start.10 = (f16[2,128,128]{2,1,0:T(8,128)(2,1)S(1)}, f16[2,128,128]{2,1,0:T(8,128)(2,1)S(1)}, u32[]{:S(2)}, u32[]{:S(2)}) collective-permute-start(f16[2,128,128]{2,1,0:T(8,128)(2,1)S(1)} %get-tuple-element.82), channel_id=1, source_target_pairs={{0,16},{4,20},{8,24},{12,28},{16,0},{20,4},{24,8},{28,12},{32,48},... | collective-permute-start | bytes 196616 | tf_op jit(solution)/shard_map/ppermute | solution.py:371
  34.2 4.8 %collective-permute-start.11 = (f16[2,128,128]{2,1,0:T(8,128)(2,1)S(1)}, f16[2,128,128]{2,1,0:T(8,128)(2,1)S(1)}, u32[]{:S(2)}, u32[]{:S(2)}) collective-permute-start(f16[2,128,128]{2,1,0:T(8,128)(2,1)S(1)} %get-tuple-element.83), channel_id=1, source_target_pairs={{0,24},{4,28},{8,16},{12,20},{16,8},{20,12},{24,0},{28,4},{32,56},... | collective-permute-start | bytes 196616 | tf_op jit(solution)/shard_map/ppermute | solution.py:371
  36.3 45.0 %copy-start.1 = (f32[1,64,928]{2,1,0:T(8,128)S(1)}, f32[1,64,928]{2,1,0:T(8,128)}, u32[]{:S(2)}) copy-start(f32[1,64,928]{2,1,0:T(8,128)} %param.17) | copy-start | bytes 712708
  36.3 45.0 %copy-start.2 = (f32[1,64,928]{2,1,0:T(8,128)S(1)}, f32[1,64,928]{2,1,0:T(8,128)}, u32[]{:S(2)}) copy-start(f32[1,64,928]{2,1,0:T(8,128)} %param.18) | copy-start | bytes 712708
  36.3 45.0 %copy-start.3 = (f32[1,64,928]{2,1,0:T(8,128)S(1)}, f32[1,64,928]{2,1,0:T(8,128)}, u32[]{:S(2)}) copy-start(f32[1,64,928]{2,1,0:T(8,128)} %param.19) | copy-start | bytes 712708
  36.3 45.0 %copy-start.4 = (f32[1,8,3968]{2,1,0:T(8,128)S(1)}, f32[1,8,3968]{2,1,0:T(8,128)}, u32[]{:S(2)}) copy-start(f32[1,8,3968]{2,1,0:T(8,128)} %param.13) | copy-start | bytes 380932
  36.3 45.0 %copy-start.5 = (f32[1,8,3968]{2,1,0:T(8,128)S(1)}, f32[1,8,3968]{2,1,0:T(8,128)}, u32[]{:S(2)}) copy-start(f32[1,8,3968]{2,1,0:T(8,128)} %param.14) | copy-start | bytes 380932
  36.3 45.0 %copy-start.6 = (f32[1,8,3968]{2,1,0:T(8,128)S(1)}, f32[1,8,3968]{2,1,0:T(8,128)}, u32[]{:S(2)}) copy-start(f32[1,8,3968]{2,1,0:T(8,128)} %param.15) | copy-start | bytes 380932
  36.3 45.0 %copy-start.7 = (f32[64,232]{1,0:T(8,128)S(1)}, f32[64,232]{1,0:T(8,128)}, u32[]{:S(2)}) copy-start(f32[64,232]{1,0:T(8,128)} %tw_ref.1) | copy-start | bytes 178180
  36.4 45.0 %copy-start.8 = (f32[64,232]{1,0:T(8,128)S(1)}, f32[64,232]{1,0:T(8,128)}, u32[]{:S(2)}) copy-start(f32[64,232]{1,0:T(8,128)} %tm_ref.1) | copy-start | bytes 178180
  36.4 45.0 %copy-start.9 = (f32[64,232]{1,0:T(8,128)S(1)}, f32[64,232]{1,0:T(8,128)}, u32[]{:S(2)}) copy-start(f32[64,232]{1,0:T(8,128)} %tv_ref.1) | copy-start | bytes 178180
  39.1 10.4 %collective-permute-start.12 = (f16[848,128]{1,0:T(8,128)(2,1)S(1)}, f16[848,128]{1,0:T(8,128)(2,1)S(1)}, u32[]{:S(2)}, u32[]{:S(2)}) collective-permute-start(f16[848,128]{1,0:T(8,128)(2,1)S(1)} %pad_maximum_fusion.5), channel_id=1, source_target_pairs={{0,32},{4,36},{8,40},{12,44},{16,48},{20,52},{24,56},{28,60},{32,0... | collective-permute-start | bytes 651272 | tf_op jit(solution)/shard_map/ppermute | solution.py:371
  49.6 7.4 %collective-permute-start.13 = (f32[8,128]{1,0:T(8,128)S(1)}, f32[8,128]{1,0:T(8,128)S(1)}, u32[]{:S(2)}, u32[]{:S(2)}) collective-permute-start(f32[8,128]{1,0:T(8,128)S(1)} %get-tuple-element.68), channel_id=1, source_target_pairs={{0,4},{4,0},{8,12},{12,8},{16,20},{20,16},{24,28},{28,24},{32,36},... | collective-permute-start | bytes 12296 | tf_op jit(solution)/shard_map/ppermute | solution.py:371
  57.0 3.7 %collective-permute-start.16 = (f32[8,128]{1,0:T(8,128)S(1)}, f32[8,128]{1,0:T(8,128)S(1)}, u32[]{:S(2)}, u32[]{:S(2)}) collective-permute-start(f32[8,128]{1,0:T(8,128)S(1)} %add.216), channel_id=1, source_target_pairs={{0,24},{4,28},{8,16},{12,20},{16,8},{20,12},{24,0},{28,4},{32,56},... | collective-permute-start | bytes 12296 | tf_op jit(solution)/shard_map/ppermute | solution.py:371
  57.1 4.0 %collective-permute-start.15 = (f32[8,128]{1,0:T(8,128)S(1)}, f32[8,128]{1,0:T(8,128)S(1)}, u32[]{:S(2)}, u32[]{:S(2)}) collective-permute-start(f32[8,128]{1,0:T(8,128)S(1)} %add.216), channel_id=1, source_target_pairs={{0,16},{4,20},{8,24},{12,28},{16,0},{20,4},{24,8},{28,12},{32,48},... | collective-permute-start | bytes 12296 | tf_op jit(solution)/shard_map/ppermute | solution.py:371
  57.4 4.2 %collective-permute-start.14 = (f32[8,128]{1,0:T(8,128)S(1)}, f32[8,128]{1,0:T(8,128)S(1)}, u32[]{:S(2)}, u32[]{:S(2)}) collective-permute-start(f32[8,128]{1,0:T(8,128)S(1)} %add.216), channel_id=1, source_target_pairs={{0,8},{4,12},{8,0},{12,4},{16,24},{20,28},{24,16},{28,20},{32,40},... | collective-permute-start | bytes 12296 | tf_op jit(solution)/shard_map/ppermute | solution.py:371
  61.6 4.1 %collective-permute-start.19 = (f32[8,128]{1,0:T(8,128)S(1)}, f32[8,128]{1,0:T(8,128)S(1)}, u32[]{:S(2)}, u32[]{:S(2)}) collective-permute-start(f32[8,128]{1,0:T(8,128)S(1)} %add_add_fusion.2), channel_id=1, source_target_pairs={{0,192},{64,0},{128,64},{192,128},{1,193},{65,1},{129,65},{193,129... | collective-permute-start | bytes 12296 | tf_op jit(solution)/shard_map/ppermute | solution.py:439
  62.6 4.1 %collective-permute-start.18 = (f32[8,128]{1,0:T(8,128)S(1)}, f32[8,128]{1,0:T(8,128)S(1)}, u32[]{:S(2)}, u32[]{:S(2)}) collective-permute-start(f32[8,128]{1,0:T(8,128)S(1)} %add_add_fusion.2), channel_id=1, source_target_pairs={{0,128},{64,192},{128,0},{192,64},{1,129},{65,193},{129,1},{193,65... | collective-permute-start | bytes 12296 | tf_op jit(solution)/shard_map/ppermute | solution.py:439
  65.7 3.7 %collective-permute-start.17 = (f32[8,128]{1,0:T(8,128)S(1)}, f32[8,128]{1,0:T(8,128)S(1)}, u32[]{:S(2)}, u32[]{:S(2)}) collective-permute-start(f32[8,128]{1,0:T(8,128)S(1)} %add_add_fusion.2), channel_id=1, source_target_pairs={{0,64},{64,128},{128,192},{192,0},{1,65},{65,129},{129,193},{193,1... | collective-permute-start | bytes 12296 | tf_op jit(solution)/shard_map/ppermute | solution.py:439
  69.4 4.3 %collective-permute-start.22 = (f32[8,128]{1,0:T(8,128)S(1)}, f32[8,128]{1,0:T(8,128)S(1)}, u32[]{:S(2)}, u32[]{:S(2)}) collective-permute-start(f32[8,128]{1,0:T(8,128)S(1)} %add_add_fusion.1), channel_id=1, source_target_pairs={{0,3},{1,2},{2,1},{3,0},{4,7},{5,6},{6,5},{7,4},{8,11},{9,10},{10,... | collective-permute-start | bytes 12296 | tf_op jit(solution)/shard_map/ppermute | solution.py:440
  71.3 3.4 %collective-permute-start.21 = (f32[8,128]{1,0:T(8,128)S(1)}, f32[8,128]{1,0:T(8,128)S(1)}, u32[]{:S(2)}, u32[]{:S(2)}) collective-permute-start(f32[8,128]{1,0:T(8,128)S(1)} %add_add_fusion.1), channel_id=1, source_target_pairs={{0,2},{1,3},{2,0},{3,1},{4,6},{5,7},{6,4},{7,5},{8,10},{9,11},{10,... | collective-permute-start | bytes 12296 | tf_op jit(solution)/shard_map/ppermute | solution.py:440
  72.4 2.5 %collective-permute-start.20 = (f32[8,128]{1,0:T(8,128)S(1)}, f32[8,128]{1,0:T(8,128)S(1)}, u32[]{:S(2)}, u32[]{:S(2)}) collective-permute-start(f32[8,128]{1,0:T(8,128)S(1)} %add_add_fusion.1), channel_id=1, source_target_pairs={{0,1},{1,0},{2,3},{3,2},{4,5},{5,4},{6,7},{7,6},{8,9},{9,8},{10,11... | collective-permute-start | bytes 12296 | tf_op jit(solution)/shard_map/ppermute | solution.py:440
  74.9 6.4 %collective-permute-start.23 = (f32[8,128]{1,0:T(8,128)S(1)}, f32[8,128]{1,0:T(8,128)S(1)}, u32[]{:S(2)}, u32[]{:S(2)}) collective-permute-start(f32[8,128]{1,0:T(8,128)S(1)} %add_add_fusion), channel_id=1, source_target_pairs={{0,32},{4,36},{8,40},{12,44},{16,48},{20,52},{24,56},{28,60},{32,0... | collective-permute-start | bytes 12296 | tf_op jit(solution)/shard_map/ppermute | solution.py:371
  82.8 8.8 %collective-permute-start.24 = (bf16[848,128]{1,0:T(8,128)(2,1)S(1)}, bf16[848,128]{1,0:T(8,128)(2,1)S(1)}, u32[]{:S(2)}, u32[]{:S(2)}) collective-permute-start(bf16[848,128]{1,0:T(8,128)(2,1)S(1)} %get-tuple-element.48), channel_id=1, source_target_pairs={{0,32},{4,36},{8,40},{12,44},{16,48},{20,52},{24,56},{28,60},{32,0... | collective-permute-start | bytes 651272 | tf_op jit(solution)/shard_map/ppermute | solution.py:371
  91.5 5.6 %collective-permute-start.26 = (bf16[2,128,128]{2,1,0:T(8,128)(2,1)S(1)}, bf16[2,128,128]{2,1,0:T(8,128)(2,1)S(1)}, u32[]{:S(2)}, u32[]{:S(2)}) collective-permute-start(bf16[2,128,128]{2,1,0:T(8,128)(2,1)S(1)} %pad_maximum_fusion.8), channel_id=1, source_target_pairs={{0,16},{4,20},{8,24},{12,28},{16,0},{20,4},{24,8},{28,12},{32,48},... | collective-permute-start | bytes 196616 | tf_op jit(solution)/shard_map/ppermute | solution.py:371
  93.0 4.1 %collective-permute-start.25 = (bf16[2,128,128]{2,1,0:T(8,128)(2,1)S(1)}, bf16[2,128,128]{2,1,0:T(8,128)(2,1)S(1)}, u32[]{:S(2)}, u32[]{:S(2)}) collective-permute-start(bf16[2,128,128]{2,1,0:T(8,128)(2,1)S(1)} %pad_maximum_fusion.8), channel_id=1, source_target_pairs={{0,8},{4,12},{8,0},{12,4},{16,24},{20,28},{24,16},{28,20},{32,40},... | collective-permute-start | bytes 196616 | tf_op jit(solution)/shard_map/ppermute | solution.py:371
  94.3 4.6 %collective-permute-start.27 = (bf16[2,128,128]{2,1,0:T(8,128)(2,1)S(1)}, bf16[2,128,128]{2,1,0:T(8,128)(2,1)S(1)}, u32[]{:S(2)}, u32[]{:S(2)}) collective-permute-start(bf16[2,128,128]{2,1,0:T(8,128)(2,1)S(1)} %pad_maximum_fusion.8), channel_id=1, source_target_pairs={{0,24},{4,28},{8,16},{12,20},{16,8},{20,12},{24,0},{28,4},{32,56},... | collective-permute-start | bytes 196616 | tf_op jit(solution)/shard_map/ppermute | solution.py:371
  95.2 5.6 %collective-permute-start.32 = (bf16[2,352,128]{2,1,0:T(8,128)(2,1)S(1)}, bf16[2,352,128]{2,1,0:T(8,128)(2,1)S(1)}, u32[]{:S(2)}, u32[]{:S(2)}) collective-permute-start(bf16[2,352,128]{2,1,0:T(8,128)(2,1)S(1)} %pad_maximum_fusion.7), channel_id=1, source_target_pairs={{0,24},{4,28},{8,16},{12,20},{16,8},{20,12},{24,0},{28,4},{32,56},... | collective-permute-start | bytes 540680 | tf_op jit(solution)/shard_map/ppermute | solution.py:371
  97.1 4.4 %collective-permute-start.33 = (bf16[2,368,128]{2,1,0:T(8,128)(2,1)S(1)}, bf16[2,368,128]{2,1,0:T(8,128)(2,1)S(1)}, u32[]{:S(2)}, u32[]{:S(2)}) collective-permute-start(bf16[2,368,128]{2,1,0:T(8,128)(2,1)S(1)} %pad_maximum_fusion.6), channel_id=1, source_target_pairs={{0,8},{4,12},{8,0},{12,4},{16,24},{20,28},{24,16},{28,20},{32,40},... | collective-permute-start | bytes 565256 | tf_op jit(solution)/shard_map/ppermute | solution.py:371
  98.9 5.6 %collective-permute-start.30 = (bf16[4,2,128,128]{3,2,1,0:T(8,128)(2,1)S(1)}, bf16[4,2,128,128]{3,2,1,0:T(8,128)(2,1)S(1)}, u32[]{:S(2)}, u32[]{:S(2)}) collective-permute-start(bf16[4,2,128,128]{3,2,1,0:T(8,128)(2,1)S(1)} %get-tuple-element.89), channel_id=1, source_target_pairs={{0,192},{64,0},{128,64},{192,128},{1,193},{65,1},{129,65},{193,129... | collective-permute-start | bytes 786440 | tf_op jit(solution)/shard_map/ppermute | solution.py:464
  99.0 6.9 %collective-permute-start.29 = (bf16[4,2,128,128]{3,2,1,0:T(8,128)(2,1)S(1)}, bf16[4,2,128,128]{3,2,1,0:T(8,128)(2,1)S(1)}, u32[]{:S(2)}, u32[]{:S(2)}) collective-permute-start(bf16[4,2,128,128]{3,2,1,0:T(8,128)(2,1)S(1)} %get-tuple-element.89), channel_id=1, source_target_pairs={{0,128},{64,192},{128,0},{192,64},{1,129},{65,193},{129,1},{193,65... | collective-permute-start | bytes 786440 | tf_op jit(solution)/shard_map/ppermute | solution.py:464
  99.6 9.3 %collective-permute-start.28 = (bf16[4,2,128,128]{3,2,1,0:T(8,128)(2,1)S(1)}, bf16[4,2,128,128]{3,2,1,0:T(8,128)(2,1)S(1)}, u32[]{:S(2)}, u32[]{:S(2)}) collective-permute-start(bf16[4,2,128,128]{3,2,1,0:T(8,128)(2,1)S(1)} %get-tuple-element.89), channel_id=1, source_target_pairs={{0,64},{64,128},{128,192},{192,0},{1,65},{65,129},{129,193},{193,1... | collective-permute-start | bytes 786440 | tf_op jit(solution)/shard_map/ppermute | solution.py:464
  101.6 19.3 %collective-permute-start.34 = (bf16[2,2,352,128]{3,2,1,0:T(8,128)(2,1)S(1)}, bf16[2,2,352,128]{3,2,1,0:T(8,128)(2,1)S(1)}, u32[]{:S(2)}, u32[]{:S(2)}) collective-permute-start(bf16[2,2,352,128]{3,2,1,0:T(8,128)(2,1)S(1)} %pad_maximum_fusion.3), channel_id=1, source_target_pairs={{0,8},{4,12},{8,0},{12,4},{16,24},{20,28},{24,16},{28,20},{32,40},... | collective-permute-start | bytes 1081352 | tf_op jit(solution)/shard_map/ppermute | solution.py:371
  101.7 19.2 %collective-permute-start.35 = (bf16[2,2,368,128]{3,2,1,0:T(8,128)(2,1)S(1)}, bf16[2,2,368,128]{3,2,1,0:T(8,128)(2,1)S(1)}, u32[]{:S(2)}, u32[]{:S(2)}) collective-permute-start(bf16[2,2,368,128]{3,2,1,0:T(8,128)(2,1)S(1)} %pad_maximum_fusion.2), channel_id=1, source_target_pairs={{0,24},{4,28},{8,16},{12,20},{16,8},{20,12},{24,0},{28,4},{32,56},... | collective-permute-start | bytes 1130504 | tf_op jit(solution)/shard_map/ppermute | solution.py:371
  109.1 14.0 %collective-permute-start.31 = (bf16[4,4,2,128,128]{4,3,2,1,0:T(8,128)(2,1)S(1)}, bf16[4,4,2,128,128]{4,3,2,1,0:T(8,128)(2,1)S(1)}, u32[]{:S(2)}, u32[]{:S(2)}) collective-permute-start(bf16[4,4,2,128,128]{4,3,2,1,0:T(8,128)(2,1)S(1)} %pad_maximum_fusion.own_ref), channel_id=1, source_target_pairs={{0,4},{4,0},{8,12},{12,8},{16,20},{20,16},{24,28},{28,24},{32,36},... | collective-permute-start | bytes 3145736 | tf_op jit(solution)/shard_map/ppermute | solution.py:371
  123.1 3.3 %collective-permute-start.36 = (bf16[2,4,720,128]{3,2,1,0:T(8,128)(2,1)S(1)}, bf16[2,4,720,128]{3,2,1,0:T(8,128)(2,1)S(1)}, u32[]{:S(2)}, u32[]{:S(2)}) collective-permute-start(bf16[2,4,720,128]{3,2,1,0:T(8,128)(2,1)S(1)} %maximum_maximum_fusion.own_ref), channel_id=1, source_target_pairs={{0,4},{4,0},{8,12},{12,8},{16,20},{20,16},{24,28},{28,24},{32,36},... | collective-permute-start | bytes 4423688 | tf_op jit(solution)/shard_map/ppermute | solution.py:371
  (2 other events, 2.4 us)
